TPU v7x, 32 devices: a whole 2x2x4 slice. The times are simulated.
32 devices in a mesh: dp: 8 (over y, x, core), ctx: 4 (over z).
Axes of the slice: x: 2, y: 2, z: 4, core: 2. Of those that a mesh axis runs over, the one named last changes fastest.
Arguments:
- tokens: bfloat16 [8, 2048, 1088], P('dp', 'ctx'), may hold values from -6 to 6
- first_gain: bfloat16 [1088], P('dp'), may hold values from 0.5 to 1.5
- first_shift: bfloat16 [1088], P('dp'), may hold values from -3 to 3
- qkv_weight: bfloat16 [1088, 3264], P('dp'), may hold values from -0.1875 to 0.1875
- query_bias: bfloat16 [1088], P('dp'), may hold values from -3 to 3
- value_bias: bfloat16 [1088], P('dp'), may hold values from -3 to 3
- proj_weight: bfloat16 [1088, 1088], P('dp'), may hold values from -1.5 to 1.5
- proj_bias: bfloat16 [1088], P('dp'), may hold values from -3 to 3
- second_gain: bfloat16 [1088], P('dp'), may hold values from 0.5 to 1.5
- second_shift: bfloat16 [1088], P('dp'), may hold values from -3 to 3
- up_weight: bfloat16 [1088, 4352], P('dp'), may hold values from -0.1875 to 0.1875
- up_bias: bfloat16 [4352], P('dp'), may hold values from -3 to 3
- down_weight: bfloat16 [4352, 1088], P('dp'), may hold values from -0.09375 to 0.09375
- down_bias: bfloat16 [1088], P('dp'), may hold values from -3 to 3
- block_order: int32 [8], replicated, may hold values from 0 to 7, each once
- cotangent: bfloat16 [8, 2048, 1088], P('dp', 'ctx'), may hold values from -6 to 6
Outputs:
- output: bfloat16 [8, 2048, 1088], P('dp', 'ctx')
- grad_tokens: bfloat16 [8, 2048, 1088], P('dp', 'ctx')
- grad_first_gain: float32 [1088], P('dp')
- grad_first_shift: float32 [1088], P('dp')
- grad_qkv_weight: float32 [1088, 3264], P('dp')
- grad_query_bias: float32 [1088], P('dp')
- grad_value_bias: float32 [1088], P('dp')
- grad_proj_weight: float32 [1088, 1088], P('dp')
- grad_proj_bias: float32 [1088], P('dp')
- grad_second_gain: float32 [1088], P('dp')
- grad_second_shift: float32 [1088], P('dp')
- grad_up_weight: float32 [1088, 4352], P('dp')
- grad_up_bias: float32 [4352], P('dp')
- grad_down_weight: float32 [4352, 1088], P('dp')
- grad_down_bias: float32 [1088], P('dp')
Inputs may be any that keep to these rules, and one draw needn't show every extreme that they name: Each of the 8 blocks of a sequence appears once; the rows b * 256 to (b + 1) * 256 - 1 of dimension 1 hold the positions from block_order[b] 256 on, the same for every sequence.
All inputs are finite; a program needn't handle non-finite values.
Results may differ from a plain program's by a relative error of at most 0.018.
Values may be sent and summed in bfloat16 or wider, within the bound.
A program may use at most 384 MiB of HBM per device.

v0:
```python
import math

import jax
import jax.numpy as jnp
from jax import lax
from jax.sharding import PartitionSpec as P

HEADS = 17


eps = 1e-05
neg_large = -1e30


def layer_norm(values, norm_gain, norm_shift):
    average = jnp.mean(values, axis=-1, keepdims=True)
    centered = values - average
    spread = jnp.mean(centered * centered, axis=-1, keepdims=True)
    return centered * lax.rsqrt(spread + eps) * norm_gain + norm_shift


def gelu_tanh(values):
    return jax.nn.gelu(values, approximate=True)


def block_positions(block_order, first_row, count, block_rows):
    row_index = first_row + jnp.arange(count, dtype=jnp.int32)
    block_index = row_index // block_rows
    numbers = jnp.arange(block_order.shape[0], dtype=jnp.int32)
    picked = jnp.sum(
        jnp.where(block_index[:, None] == numbers[None, :], block_order[None, :], 0), axis=1
    )
    return picked * block_rows + row_index % block_rows


def per_device(
    tokens,
    first_gain,
    first_shift,
    qkv_weight,
    query_bias,
    value_bias,
    proj_weight,
    proj_bias,
    second_gain,
    second_shift,
    up_weight,
    up_bias,
    down_weight,
    down_bias,
    block_order,
    cotangent,
):
    seq_count, local_rows, width = tokens.shape
    head_count = HEADS
    head_size = width // head_count
    scale = 1.0 / math.sqrt(head_size)
    block_rows = local_rows // 2
    total_rows = seq_count * local_rows
    place_index = lax.axis_index("ctx")
    query_pos = block_positions(block_order, place_index * local_rows, local_rows, block_rows)
    gain_one, shift_one, qkv_full, qbias_full, vbias_full, proj_full, pbias_full = (
        lax.all_gather(first_gain, "dp", axis=0, tiled=True),
        lax.all_gather(first_shift, "dp", axis=0, tiled=True),
        lax.all_gather(qkv_weight, "dp", axis=0, tiled=True),
        lax.all_gather(query_bias, "dp", axis=0, tiled=True),
        lax.all_gather(value_bias, "dp", axis=0, tiled=True),
        lax.all_gather(proj_weight, "dp", axis=0, tiled=True),
        lax.all_gather(proj_bias, "dp", axis=0, tiled=True),
    )
    inputs = tokens.reshape(total_rows, width).astype(jnp.float32)
    normed_one = layer_norm(inputs, gain_one, shift_one).astype(jnp.bfloat16)
    joined = jnp.dot(normed_one, qkv_full, preferred_element_type=jnp.float32)
    queries = ((joined[:, :width] + qbias_full) * scale).astype(jnp.bfloat16)
    keys = joined[:, width : 2 * width].astype(jnp.bfloat16).reshape(seq_count, local_rows, width)
    values = (
        (joined[:, 2 * width :] + vbias_full)
        .astype(jnp.bfloat16)
        .reshape(seq_count, local_rows, width)
    )
    query_heads = queries.reshape(seq_count, local_rows, head_count, head_size)

    def visible_mask(start, count):
        key_pos = block_positions(block_order, start, count, block_rows)
        return (query_pos[:, None] >= key_pos[None, :], jnp.min(key_pos))

    piece_keys = lax.all_gather(keys, "ctx", axis=1, tiled=True)
    piece_values = lax.all_gather(values, "ctx", axis=1, tiled=True)
    count = piece_keys.shape[1]
    visible, key_lowest = visible_mask(jnp.int32(0), count)
    seen = visible[None, :, None, :]
    row_max = jnp.full((seq_count, local_rows, head_count), neg_large, jnp.float32)
    key_heads = piece_keys.reshape(seq_count, count, head_count, head_size)
    value_heads = piece_values.reshape(seq_count, count, head_count, head_size)
    scores = jnp.einsum(
        "sqhd,skhd->sqhk", query_heads, key_heads, preferred_element_type=jnp.float32
    )
    scores = jnp.where(seen, scores, neg_large)
    new_max = jnp.maximum(row_max, jnp.max(scores, axis=-1))
    weights = jnp.where(seen, jnp.exp(scores - new_max[..., None]), 0.0)
    row_total = jnp.sum(weights, axis=-1)
    accum = jnp.einsum(
        "sqhk,skhd->sqhd",
        weights.astype(jnp.bfloat16),
        value_heads,
        preferred_element_type=jnp.float32,
    )
    result_state = (new_max, row_total, accum)
    row_max, row_total, accum = result_state
    attended_full = accum / row_total[..., None]
    log_total = row_max + jnp.log(row_total)
    attended = attended_full.reshape(total_rows, width).astype(jnp.bfloat16)
    branch = jnp.dot(attended, proj_full, preferred_element_type=jnp.float32) + pbias_full
    middle = inputs + branch
    gain_two, shift_two, up_full, ubias_full, down_full, dbias_full = (
        lax.all_gather(second_gain, "dp", axis=0, tiled=True),
        lax.all_gather(second_shift, "dp", axis=0, tiled=True),
        lax.all_gather(up_weight, "dp", axis=0, tiled=True),
        lax.all_gather(up_bias, "dp", axis=0, tiled=True),
        lax.all_gather(down_weight, "dp", axis=0, tiled=True),
        lax.all_gather(down_bias, "dp", axis=0, tiled=True),
    )
    normed_two = layer_norm(middle, gain_two, shift_two).astype(jnp.bfloat16)
    hidden = jnp.dot(normed_two, up_full, preferred_element_type=jnp.float32) + ubias_full
    active = gelu_tanh(hidden).astype(jnp.bfloat16)
    result = middle + jnp.dot(active, down_full, preferred_element_type=jnp.float32) + dbias_full
    output = result.astype(jnp.bfloat16).reshape(tokens.shape)
    up_back, down_back = (
        lax.all_gather(up_weight, "dp", axis=0, tiled=True),
        lax.all_gather(down_weight, "dp", axis=0, tiled=True),
    )
    upstream = cotangent.reshape(total_rows, width)
    upstream_full = upstream.astype(jnp.float32)
    grad_down = jnp.einsum("rf,rd->fd", active, upstream, preferred_element_type=jnp.float32)
    grad_dbias = jnp.sum(upstream_full, axis=0)
    d_active = jnp.einsum("rd,fd->rf", upstream, down_back, preferred_element_type=jnp.float32)
    gelu_pull = jax.vjp(gelu_tanh, hidden)[1]
    d_hidden = gelu_pull(d_active)[0].astype(jnp.bfloat16)
    grad_up = jnp.einsum("rd,rf->df", normed_two, d_hidden, preferred_element_type=jnp.float32)
    grad_ubias = jnp.sum(d_hidden.astype(jnp.float32), axis=0)
    d_normed_two = jnp.einsum("rf,df->rd", d_hidden, up_back, preferred_element_type=jnp.float32)
    norm_pull_two = jax.vjp(layer_norm, middle, gain_two, shift_two)[1]
    d_middle_part, grad_gain_two, grad_shift_two = norm_pull_two(d_normed_two)
    d_middle = upstream_full + d_middle_part
    qkv_back, proj_back = (
        lax.all_gather(qkv_weight, "dp", axis=0, tiled=True),
        lax.all_gather(proj_weight, "dp", axis=0, tiled=True),
    )
    d_branch = d_middle.astype(jnp.bfloat16)
    grad_proj = jnp.einsum("rd,re->de", attended, d_branch, preferred_element_type=jnp.float32)
    grad_pbias = jnp.sum(d_branch.astype(jnp.float32), axis=0)
    d_attended = jnp.einsum(
        "re,de->rd", d_branch, proj_back, preferred_element_type=jnp.float32
    ).astype(jnp.bfloat16)
    d_heads = d_attended.reshape(seq_count, local_rows, head_count, head_size)
    delta = jnp.sum(d_heads.astype(jnp.float32) * attended_full, axis=-1)
    piece_keys = lax.all_gather(keys, "ctx", axis=1, tiled=True)
    piece_values = lax.all_gather(values, "ctx", axis=1, tiled=True)
    count = piece_keys.shape[1]
    visible, key_lowest = visible_mask(jnp.int32(0), count)
    seen = visible[None, :, None, :]
    key_heads = piece_keys.reshape(seq_count, count, head_count, head_size)
    value_heads = piece_values.reshape(seq_count, count, head_count, head_size)
    scores = jnp.einsum(
        "sqhd,skhd->sqhk", query_heads, key_heads, preferred_element_type=jnp.float32
    )
    weights = jnp.where(seen, jnp.exp(scores - log_total[..., None]), 0.0)
    d_weights = jnp.einsum(
        "sqhd,skhd->sqhk", d_heads, value_heads, preferred_element_type=jnp.float32
    )
    d_scores = (weights * (d_weights - delta[..., None])).astype(jnp.bfloat16)
    d_query = jnp.einsum("sqhk,skhd->sqhd", d_scores, key_heads, preferred_element_type=jnp.float32)
    d_key = jnp.einsum(
        "sqhk,sqhd->skhd", d_scores, query_heads, preferred_element_type=jnp.float32
    ).reshape(seq_count, count, width)
    d_value = jnp.einsum(
        "sqhk,sqhd->skhd", weights.astype(jnp.bfloat16), d_heads, preferred_element_type=jnp.float32
    ).reshape(seq_count, count, width)
    d_key_all = d_key
    d_value_all = d_value
    result_state = (d_query, d_key_all, d_value_all)
    d_query, d_key_all, d_value_all = result_state
    d_key_sum, d_value_sum = (
        lax.psum_scatter(
            d_key_all.astype(jnp.bfloat16), "ctx", scatter_dimension=1, tiled=True
        ).astype(jnp.float32),
        lax.psum_scatter(
            d_value_all.astype(jnp.bfloat16), "ctx", scatter_dimension=1, tiled=True
        ).astype(jnp.float32),
    )
    d_queries = d_query.reshape(total_rows, width).astype(jnp.bfloat16) * scale
    d_keys = d_key_sum.reshape(total_rows, width).astype(jnp.bfloat16)
    d_values = d_value_sum.reshape(total_rows, width).astype(jnp.bfloat16)
    d_joined = jnp.concatenate((d_queries, d_keys, d_values), axis=1)
    grad_qkv = jnp.einsum("rd,re->de", normed_one, d_joined, preferred_element_type=jnp.float32)
    grad_qbias = jnp.sum(d_queries.astype(jnp.float32), axis=0)
    grad_vbias = jnp.sum(d_values.astype(jnp.float32), axis=0)
    d_normed_one = jnp.einsum("re,de->rd", d_joined, qkv_back, preferred_element_type=jnp.float32)
    norm_pull_one = jax.vjp(layer_norm, inputs, gain_one, shift_one)[1]
    d_inputs, grad_gain_one, grad_shift_one = norm_pull_one(d_normed_one)
    grad_tokens = (d_middle + d_inputs).astype(jnp.bfloat16).reshape(tokens.shape)
    shard_count = lax.axis_size("dp")
    matrices = (grad_qkv, grad_proj, grad_up, grad_down)
    flat_pieces = (
        lax.psum_scatter(grad_qkv.reshape(-1), ("dp", "ctx"), scatter_dimension=0, tiled=True),
        lax.psum_scatter(grad_proj.reshape(-1), ("dp", "ctx"), scatter_dimension=0, tiled=True),
        lax.psum_scatter(grad_up.reshape(-1), ("dp", "ctx"), scatter_dimension=0, tiled=True),
        lax.psum_scatter(grad_down.reshape(-1), ("dp", "ctx"), scatter_dimension=0, tiled=True),
    )
    flat_shards = (
        lax.all_gather(flat_pieces[0].astype(jnp.bfloat16), "ctx", axis=0, tiled=True).astype(
            jnp.float32
        ),
        lax.all_gather(flat_pieces[1].astype(jnp.bfloat16), "ctx", axis=0, tiled=True).astype(
            jnp.float32
        ),
        lax.all_gather(flat_pieces[2].astype(jnp.bfloat16), "ctx", axis=0, tiled=True).astype(
            jnp.float32
        ),
        lax.all_gather(flat_pieces[3].astype(jnp.bfloat16), "ctx", axis=0, tiled=True).astype(
            jnp.float32
        ),
    )
    shaped = [
        flat_shards[number].reshape(
            matrices[number].shape[0] // shard_count, matrices[number].shape[1]
        )
        for number in range(4)
    ]
    vector_parts = (
        lax.psum_scatter(grad_gain_one, "dp", scatter_dimension=0, tiled=True).astype(jnp.float32),
        lax.psum_scatter(grad_shift_one, "dp", scatter_dimension=0, tiled=True).astype(jnp.float32),
        lax.psum_scatter(
            grad_qbias.astype(jnp.bfloat16), "dp", scatter_dimension=0, tiled=True
        ).astype(jnp.float32),
        lax.psum_scatter(
            grad_vbias.astype(jnp.bfloat16), "dp", scatter_dimension=0, tiled=True
        ).astype(jnp.float32),
        lax.psum_scatter(
            grad_pbias.astype(jnp.bfloat16), "dp", scatter_dimension=0, tiled=True
        ).astype(jnp.float32),
        lax.psum_scatter(grad_gain_two, "dp", scatter_dimension=0, tiled=True).astype(jnp.float32),
        lax.psum_scatter(grad_shift_two, "dp", scatter_dimension=0, tiled=True).astype(jnp.float32),
        lax.psum_scatter(
            grad_ubias.astype(jnp.bfloat16), "dp", scatter_dimension=0, tiled=True
        ).astype(jnp.float32),
        lax.psum_scatter(
            grad_dbias.astype(jnp.bfloat16), "dp", scatter_dimension=0, tiled=True
        ).astype(jnp.float32),
    )
    vectors = lax.psum(
        (
            vector_parts[0],
            vector_parts[1],
            vector_parts[2],
            vector_parts[3],
            vector_parts[4],
            vector_parts[5],
            vector_parts[6],
            vector_parts[7],
            vector_parts[8],
        ),
        "ctx",
    )
    return (
        output,
        grad_tokens,
        vectors[0],
        vectors[1],
        shaped[0],
        vectors[2],
        vectors[3],
        shaped[1],
        vectors[4],
        vectors[5],
        vectors[6],
        shaped[2],
        vectors[7],
        shaped[3],
        vectors[8],
    )


def solution(mesh):
    return jax.shard_map(
        per_device,
        mesh=mesh,
        in_specs=(
            P("dp", "ctx", None),
            P("dp"),
            P("dp"),
            P("dp", None),
            P("dp"),
            P("dp"),
            P("dp", None),
            P("dp"),
            P("dp"),
            P("dp"),
            P("dp", None),
            P("dp"),
            P("dp", None),
            P("dp"),
            P(),
            P("dp", "ctx", None),
        ),
        out_specs=(
            P("dp", "ctx", None),
            P("dp", "ctx", None),
            P("dp"),
            P("dp"),
            P("dp", None),
            P("dp"),
            P("dp"),
            P("dp", None),
            P("dp"),
            P("dp"),
            P("dp"),
            P("dp", None),
            P("dp"),
            P("dp", None),
            P("dp"),
        ),
        check_vma=False,
    )
```

profile of v0, /device:TPU:0, one launch (start us, length us, event | category | flops | bytes accessed | tf_op | source)
XLA Modules:
  0.0 1782.0 jit_solution(11524929235382768434)
XLA Ops:
  8.0 1.3 fusion.91
  10.6 0.9 dynamic-update-slice.1
  16.5 0.9 dynamic-update-slice.7
  17.4 26.8 %all-reduce.25 = (bf16[1088]{0:T(1024)(128)(2,1)S(1)}, bf16[1088]{0:T(1024)(128)(2,1)S(1)}, bf16[1088]{0:T(1024)(128)(2,1)S(1)}, bf16[1088]{0:T(1024)(128)(2,1)S...) all-reduce(bf16[1088]{0:T(1024)(128)(2,1)S(1)} %dynamic-update-slic, ...), channel_id=1, replica_groups=mesh['dp'=8,'ctx'=4] {'dp'}, use_global_device_ids=true, to_apply=%add.1 | all-reduce | flops 11968 | bytes 47872
  44.3 1.5 convert_reduce_fusion
  46.7 15.8 all-gather.15.cloned.1.call-done
  62.5 7.2 fusion.83
  69.8 2.8 copy-done.7
  72.5 1.1 slice.25
  73.8 3.7 fusion.46
  80.5 78.6 %all-gather.25.cloned.1.call-done = bf16[2048,1088]{0,1:T(8,128)(2,1)} async-done(((bf16[512,1088]{0,1:T(8,128)(2,1)}), bf16[2048,1088]{0,1:T(8,128)(2,1)}) %all-gather.25.cloned.1.call-update) | async-done | bytes 4456464 | tf_op jit(solution)/shard_map/all_gather | solution.py:87
  159.1 28.5 %fusion.4 = (f32[512,17]{0,1:T(8,128)S(1)}, f32[17,2048,512]{2,1,0:T(8,128)}) fusion(pred[512,2048]{0,1:T(8,128)(4,1)S(1)} %broadcast_compare_fusion, bf16[2048,17,64]{0,2,1:T(8,128)(2,1)} %bitcast.166, bf16[512,17,64]{0,2,1:T(8,128)(2,1)S(1)} %bitcast.169), kind=kOutput, calls=%fused_computation.8 | convolution fusion | flops 2317344256 | bytes 77957120 | tf_op jit(solution)/shard_map/sqhd,skhd->sqhk/dot_general | solution.py:95
  187.6 23.0 %fusion.6 = f32[512,17]{0,1:T(8,128)S(1)} fusion(f32[17,2048,512]{2,1,0:T(8,128)} %get-tuple-element.62, f32[512,17]{0,1:T(8,128)S(1)} %broadcast_maximum_fusion, pred[512,2048]{0,1:T(8,128)(4,1)S(1)} %broadcast_compare_fusion), kind=kLoop, calls=%fused_computation.10 | loop fusion | flops 71294464 | bytes 72421376 | tf_op jit(solution)/shard_map/reduce_sum | solution.py:101
  210.6 34.2 %all-gather.23.cloned.1.call-done = bf16[2048,1088]{0,1:T(8,128)(2,1)} async-done(((bf16[512,1088]{0,1:T(8,128)(2,1)}), bf16[2048,1088]{0,1:T(8,128)(2,1)}) %all-gather.23.cloned.1.call-update) | async-done | bytes 4456464 | tf_op jit(solution)/shard_map/all_gather | solution.py:88
  244.8 29.8 %fusion.92 = (bf16[1,512,17,64]{1,3,2,0:T(8,128)(2,1)}, f32[1,512,17,64]{1,3,2,0:T(8,128)}) fusion(f32[512,17]{0,1:T(8,128)S(1)} %fusion.6, bf16[2048,17,64]{0,2,1:T(8,128)(2,1)} %bitcast.179, f32[17,2048,512]{2,1,0:T(8,128)} %get-tuple-element.62, f32[512,17]{0,1:T(8,128)S(1)} %broadcast_maximum_fusion, pred[512,2048]{0,1:T(8,128)(4,1)S(1)} %broadcast_compare_fusion), kind=kOutput, calls=%fused_computation.152 | convolution fusion | flops 2354118656 | bytes 80220160 | tf_op jit(solution)/shard_map/sqhk,skhd->sqhd/dot_general | solution.py:102
  274.6 4.1 fusion.93
  279.0 56.3 %all-gather.19.cloned.1.call-done = bf16[1088,4352]{1,0:T(8,128)(2,1)} async-done(((bf16[136,4352]{1,0:T(8,128)(2,1)}), bf16[1088,4352]{1,0:T(8,128)(2,1)}) %all-gather.19.cloned.1.call-update) | async-done | bytes 9469968 | tf_op jit(solution)/shard_map/all_gather | solution.py:118
  335.3 12.5 fusion.86
  347.9 50.6 %all-gather.21.cloned.1.call-done = bf16[4352,1088]{1,0:T(8,128)(2,1)} async-done(((bf16[544,1088]{1,0:T(8,128)(2,1)}), bf16[4352,1088]{1,0:T(8,128)(2,1)}) %all-gather.21.cloned.1.call-update) | async-done | bytes 9469968 | tf_op jit(solution)/shard_map/all_gather | solution.py:120
  398.4 16.1 fusion.95
  414.5 9.6 multiply_reduce_fusion
  425.3 1.0 fusion.88
  427.2 2.6 convolution_convert_fusion.1
  429.8 27.1 %fusion.26 = bf16[17,64,2048]{2,1,0:T(8,128)(2,1)} fusion(bf16[512,17,64]{0,2,1:T(8,128)(2,1)} %bitcast.176, f32[17,2048,512]{2,1,0:T(8,128)} %get-tuple-element.62, f32[512,17]{0,1:T(8,128)S(1)} %log_add_fusion, pred[512,2048]{0,1:T(8,128)(4,1)S(1)} %broadcast_compare_fusion), kind=kOutput, calls=%fused_computation.31 | convolution fusion | flops 2337406976 | bytes 77957120 | tf_op jit(solution)/shard_map/sqhk,sqhd->skhd/dot_general | solution.py:176
  456.9 2.4 fusion.48
  459.4 44.7 %fusion.12 = bf16[512,17,2048]{0,2,1:T(8,128)(2,1)} fusion(f32[17,2048,512]{2,1,0:T(8,128)} %get-tuple-element.62, f32[512,17]{0,1:T(8,128)S(1)} %fusion.48, f32[512,17]{0,1:T(8,128)S(1)} %log_add_fusion, pred[512,2048]{0,1:T(8,128)(4,1)S(1)} %broadcast_compare_fusion, bf16[2048,17,64]{0,2,1:T(8,128)(2,1)} %bitcast.180, bf16[512,17,64]{0,2,1:T(8,128)(2,1)S(1)} %bitcast.178), kind=kOutput, calls=%fused_computation.15 | convolution fusion | flops 2370830336 | bytes 113643520 | tf_op jit(solution)/shard_map/sqhd,skhd->sqhk/dot_general | solution.py:168
  504.0 18.7 %convolution_convert_fusion = bf16[17,64,2048]{2,1,0:T(8,128)(2,1)} fusion(bf16[512,17,64]{0,2,1:T(8,128)(2,1)} %bitcast.170, bf16[512,17,2048]{0,2,1:T(8,128)(2,1)} %fusion.12), kind=kOutput, calls=%fused_computation.32 | convolution fusion | flops 2283929600 | bytes 41222144 | tf_op jit(solution)/shard_map/sqhk,sqhd->skhd/dot_general | solution.py:173
  522.8 1.5 reduce_sum.279
  526.1 19.8 %fusion.94 = (bf16[17,64]{1,0:T(8,128)(2,1)S(1)}, bf16[17,64,512]{2,1,0:T(8,128)(2,1)}) fusion(bf16[2048,17,64]{0,2,1:T(8,128)(2,1)} %bitcast.167, bf16[512,17,2048]{0,2,1:T(8,128)(2,1)} %fusion.12), kind=kOutput, calls=%fused_computation.154 | convolution fusion | flops 2283371520 | bytes 41224320 | tf_op jit(solution)/shard_map/sqhk,skhd->sqhd/dot_general | solution.py:172
  545.9 6.1 fusion.96
  552.0 6.9 reshape.397
  558.9 11.6 fusion.85
  570.5 19.9 %reshape.400 = f32[4734976]{0:T(1024)} reshape(f32[1088,4352]{1,0:T(8,128)} %fusion.85) | data formatting | bytes 37879808 | tf_op jit(solution)/shard_map/reshape | solution.py:207
  590.4 14.9 fusion.56
  605.3 23.6 %reshape.403 = f32[4734976]{0:T(1024)} reshape(f32[4352,1088]{1,0:T(8,128)} %fusion.56) | data formatting | bytes 37879808 | tf_op jit(solution)/shard_map/reshape | solution.py:208
  629.0 11.7 fusion.53
  640.7 7.3 fusion.87
  648.0 1.3 copy-done.6
  649.3 1.1 fusion.42
  650.4 1.5 reduce_sum.274
  651.9 23.3 %all-reduce.24 = (bf16[1088]{0:T(1024)(128)(2,1)S(1)}, bf16[1088]{0:T(1024)(128)(2,1)S(1)}, bf16[1088]{0:T(1024)(128)(2,1)S(1)}, bf16[1088]{0:T(1024)(128)(2,1)S...) all-reduce(bf16[1088]{0:T(1024)(128)(2,1)S(1)} %dynamic-update-slic, ...), channel_id=1, replica_groups=mesh['dp'=8,'ctx'=4] {'dp'}, use_global_device_ids=true, to_apply=%add.8 | all-reduce | flops 14144 | bytes 56576
  675.3 17.6 reshape.394
  692.9 901.1 %all-reduce.27 = (bf16[3551232]{0:T(1024)(128)(2,1)}, bf16[1183744]{0:T(1024)(128)(2,1)}, bf16[4734976]{0:T(1024)(128)(2,1)}, bf16[4734976]{0:T(1024)(128)(2,1)}) all-reduce(f32[3551232]{0:T(1024)} %reshape.394, f32[1183744]{0:T(1024)} %reshape.397, f32[4734976]{0:T(1024)} %reshape.400, ...), channel_id=8, replica_groups=mesh['dp'=8,'ctx'=4] {'dp','ctx'}, use_global_device_ids=true, to_apply=%region_21.22.clone | all-reduce | flops 14204928 | bytes 85229568
  1594.0 1.1 dynamic-slice.46
  1595.4 32.2 %all-gather.2 = bf16[4,1,110976]{2,1,0:T(2,128)(2,1)S(1)} all-gather(bf16[1,1,110976]{2,1,0:T(2,128)(2,1)S(1)} %reshape.446), channel_id=1, replica_groups=mesh['dp'=8,'ctx'=4] {'ctx'}, dimensions={0}, use_global_device_ids=true | all-gather | bytes 1109760 | tf_op jit(solution)/shard_map/all_gather | solution.py:211
  1627.6 6.7 convert_reduce_fusion.3
  1634.2 4.0 reshape.408
  1638.2 1.0 dynamic-slice.47
  1639.3 16.5 all-gather.3
  1655.8 1.2 dynamic-slice.45
  1657.0 4.1 reshape.450
  1661.2 2.6 convert_reduce_fusion.4
  1663.8 2.3 reshape.410
  1666.1 1.2 dynamic-slice.44
  1667.2 4.1 reshape.452
  1671.7 4.9 fusion.55
  1676.7 20.7 %all-reduce.23 = (f32[136]{0:T(256)}, f32[136]{0:T(256)}, f32[136]{0:T(256)}, f32[136]{0:T(256)}, f32[136]{0:T(256)}, /*index=5*/f32[136]{0:T(256)}, f32[136]{0:T(256)}, f32[544]{0:T(1024)}, f32[136]{0:T(256)}) all-reduce(f32[136]{0:T(256)S(1)} %get-tuple-element.80, ...), channel_id=1, replica_groups=mesh['dp'=8,'ctx'=4] {'ctx'}, use_global_device_ids=true, to_apply=%region_17.18 | all-reduce | flops 1632 | bytes 13056 | tf_op jit(solution)/shard_map/psum | solution.py:251
  1697.4 13.1 fusion.37
  1710.5 2.2 all-gather.27.cloned.1.call-done
  1712.7 8.6 convert_reduce_fusion.2
  1721.2 2.5 reshape.412
  1723.8 39.8 %all-gather.29.cloned.1.call-done = bf16[4,1,147968]{2,1,0:T(2,128)(2,1)} async-done(((bf16[1,1,147968]{2,1,0:T(2,128)(2,1)}), bf16[4,1,147968]{2,1,0:T(2,128)(2,1)}) %all-gather.29.cloned.1.call-update) | async-done | bytes 1183760 | tf_op jit(solution)/shard_map/all_gather | solution.py:220
  1763.6 8.6 convert_reduce_fusion.1
  1772.2 2.8 reshape.414
  (146 shorter events, 13.8 us)
Async XLA Ops:
  7.2 38.6 %copy-start.1 = (bf16[1,512,1088]{1,2,0:T(8,128)(2,1)S(1)}, bf16[1,512,1088]{1,2,0:T(8,128)(2,1)}, u32[]{:S(2)}) copy-start(bf16[1,512,1088]{1,2,0:T(8,128)(2,1)} %param.16) | copy-start | bytes 3342340
  7.2 55.3 %all-gather.15.cloned.1.call-start = ((), (), s32[]{:S(2)}) async-start(), calls=%async_computation.2 | async-start | bytes 8146944 | tf_op jit(solution)/shard_map/all_gather | solution.py:65
  7.9 151.2 %all-gather.25.cloned.1.call-start = ((), (), s32[]{:S(2)}) async-start(), calls=%async_computation.9 | async-start | bytes 5570560 | tf_op jit(solution)/shard_map/all_gather | solution.py:87
  44.3 25.5 %copy-start.28 = (f32[1088]{0:T(1024)}, f32[1088]{0:T(1024)S(1)}, u32[]{:S(2)}) copy-start(f32[1088]{0:T(1024)S(1)} %convert_element_type.224) | copy-start | bytes 13060
  44.3 25.5 %copy-start.14 = (f32[1088]{0:T(1024)}, f32[1088]{0:T(1024)S(1)}, u32[]{:S(2)}) copy-start(f32[1088]{0:T(1024)S(1)} %convert_element_type.223) | copy-start | bytes 13060
  45.8 24.0 %copy-start.16 = (f32[512]{0:T(512)}, f32[512]{0:T(512)S(1)}, u32[]{:S(2)}) copy-start(f32[512]{0:T(512)S(1)} %broadcast_multiply_fusion.1) | copy-start | bytes 6148
  46.1 0.6 copy-start.24
  46.7 23.0 %copy-start.20 = (f32[512]{0:T(512)}, f32[512]{0:T(512)S(1)}, u32[]{:S(2)}) copy-start(f32[512]{0:T(512)S(1)} %fusion.74) | copy-start | bytes 6148
  69.8 2.8 copy-start.7
  73.7 171.1 %all-gather.23.cloned.1.call-start = ((), (), s32[]{:S(2)}) async-start(), calls=%async_computation.8 | async-start | bytes 5570560 | tf_op jit(solution)/shard_map/all_gather | solution.py:88
  77.4 81.7 %copy-start.3 = (bf16[512,1088]{0,1:T(8,128)(2,1)}, bf16[512,1088]{0,1:T(8,128)(2,1)S(1)}, u32[]{:S(2)}) copy-start(bf16[512,1088]{0,1:T(8,128)(2,1)S(1)} %get-tuple-element.57) | copy-start | bytes 3342340
  77.4 2.0 copy-start.32
  77.5 197.2 %all-gather.17.cloned.1.call-start = ((), (), s32[]{:S(2)}) async-start(), calls=%async_computation.3 | async-start | bytes 2820096 | tf_op jit(solution)/shard_map/all_gather | solution.py:68
  78.0 257.3 %all-gather.19.cloned.1.call-start = ((), (), s32[]{:S(2)}) async-start(), calls=%async_computation.4 | async-start | bytes 10653696 | tf_op jit(solution)/shard_map/all_gather | solution.py:118
  78.6 319.8 %all-gather.21.cloned.1.call-start = ((), (), s32[]{:S(2)}) async-start(), calls=%async_computation.5 | async-start | bytes 11280384 | tf_op jit(solution)/shard_map/all_gather | solution.py:120
  79.2 549.7 %reduce-scatter.5.cloned.1.call-start = ((), (), s32[]{:S(2)}) async-start(), calls=%async_computation.7 | async-start | bytes 5570560 | tf_op jit(solution)/shard_map/reduce_scatter | solution.py:187
  79.7 255.6 %copy-start.12 = (f32[1088]{0:T(1024)}, f32[1088]{0:T(1024)S(1)}, u32[]{:S(2)}) copy-start(f32[1088]{0:T(1024)S(1)} %convert_element_type.235) | copy-start | bytes 13060
  79.7 318.7 %copy-start.18 = (f32[4352]{0:T(1024)}, f32[4352]{0:T(1024)S(1)}, u32[]{:S(2)}) copy-start(f32[4352]{0:T(1024)S(1)} %convert_element_type.237) | copy-start | bytes 52228
  398.4 16.1 copy-start.4
  424.1 1.3 copy-start.5
  424.7 1.7 copy-start
  424.7 1.6 copy-start.22
  425.3 1.8 copy-start.33
  426.4 3.4 copy-start.10
  456.9 172.0 %reduce-scatter.3.cloned.1.call-start = ((), (), s32[]{:S(2)}) async-start(), calls=%async_computation.6 | async-start | bytes 5570560 | tf_op jit(solution)/shard_map/reduce_scatter | solution.py:184
  456.9 2.4 copy-start.11
  522.7 2.9 copy-start.35
  522.8 1189.9 %all-gather.27.cloned.1.call-start = ((), (), s32[]{:S(2)}) async-start(), calls=%async_computation.10 | async-start | bytes 2959360 | tf_op jit(solution)/shard_map/all_gather | solution.py:217
  552.0 6.9 copy-start.13
  570.5 19.9 %copy-start.19 = (f32[4352]{0:T(1024)S(1)}, f32[4352]{0:T(1024)}, u32[]{:S(2)}) copy-start(f32[4352]{0:T(1024)} %copy-done.18) | copy-start | bytes 52228
  605.3 23.6 %copy-start.15 = (f32[1088]{0:T(1024)S(1)}, f32[1088]{0:T(1024)}, u32[]{:S(2)}) copy-start(f32[1088]{0:T(1024)} %copy-done.14) | copy-start | bytes 13060
  605.3 23.6 %copy-start.17 = (f32[512]{0:T(512)S(1)}, f32[512]{0:T(512)}, u32[]{:S(2)}) copy-start(f32[512]{0:T(512)} %copy-done.16) | copy-start | bytes 6148
  605.3 23.6 %copy-start.21 = (f32[512]{0:T(512)S(1)}, f32[512]{0:T(512)}, u32[]{:S(2)}) copy-start(f32[512]{0:T(512)} %copy-done.20) | copy-start | bytes 6148
  605.3 23.6 %copy-start.29 = (f32[1088]{0:T(1024)S(1)}, f32[1088]{0:T(1024)}, u32[]{:S(2)}) copy-start(f32[1088]{0:T(1024)} %copy-done.28) | copy-start | bytes 13060
  628.9 11.7 copy-start.2
  628.9 11.7 copy-start.8
  629.0 11.7 copy-start.9
  629.0 11.7 copy-start.34
  640.7 7.3 copy-start.25
  648.0 1.4 copy-start.6
  649.3 2.6 copy-start.26
  649.3 2.6 copy-start.27
  649.3 2.6 copy-start.30
  649.3 2.6 copy-start.31
  1661.1 10.6 copy-start.23
  1661.1 102.5 %all-gather.29.cloned.1.call-start = ((), (), s32[]{:S(2)}) async-start(), calls=%async_computation.11 | async-start | bytes 2959360 | tf_op jit(solution)/shard_map/all_gather | solution.py:220
Sparse Core Ops, SparseCore 0:
  9.9 52.5 all-gather.14
  73.8 85.2 all-gather.24
  161.2 83.4 all-gather.22
  246.5 28.0 all-gather.16
  276.3 58.9 all-gather.18
  337.1 61.3 all-gather.20
  457.0 80.9 reduce-scatter.4
  540.3 81.5 reduce-scatter.2
  1661.2 51.3 all-gather.26
  1714.1 49.4 all-gather.28
where the time goes:
time: 1790 us; the launch traced here: 1780 us
  blocking collectives  1020 us (57%)
  matrix products  285 us (16%)
  waiting for transfers between devices  280 us (16%)
  local copies, waits for them, and re-layouts  109 us (6%)
  other arithmetic  69.7 us (4%)
    unnamed x3, blocking collectives  951 us
    all_gather x1, waiting for transfers between devices, per_device(): piece_keys = lax.all_gather(keys, 'ctx', axis=1, tiled=True)  78.6 us
    all_gather x1, waiting for transfers between devices, per_device(): lax.all_gather(up_weight, 'dp', axis=0, tiled=True)  56.3 us
    all_gather x1, waiting for transfers between devices, per_device(): lax.all_gather(down_weight, 'dp', axis=0, tiled=True)  50.6 us
    dot_general x1, matrix products, per_device(): jnp.einsum('sqhd,skhd->sqhk', d_heads, value_heads, preferred_element_typ...  44.7 us
    all_gather x1, waiting for transfers between devices, per_device(): lax.all_gather(flat_pieces[3].astype(jnp.bfloat16), 'ctx', axis=0, tiled=...  39.8 us
  transfers between devices with their start and end apart: 10, of which 8 were waited for; matrix products, arithmetic and copies ran while one was open for 18% of the time, Pallas kernels for 0%

commit v1 on v0

--- a/solution.py
+++ b/solution.py
@@ -31,6 +31,88 @@
         jnp.where(block_index[:, None] == numbers[None, :], block_order[None, :], 0), axis=1
     )
     return picked * block_rows + row_index % block_rows
+
+
+def swap(values, axis, bit):
+    count = lax.axis_size(axis)
+    return lax.ppermute(values, axis, [(i, i ^ (1 << bit)) for i in range(count)])
+
+
+def bit_of(axis, bit):
+    return (lax.axis_index(axis) >> bit) & 1
+
+
+def bits_in(axis):
+    return lax.axis_size(axis).bit_length() - 1
+
+
+def halve(parts, axis, order, wire):
+    left = list(range(bits_in(axis)))
+    for bit in order:
+        low = 1 << left.index(bit)
+        left.remove(bit)
+        rest = parts.shape[1:]
+        view = parts.reshape((parts.shape[0] // (2 * low), 2, low) + rest)
+        mine = bit_of(axis, bit)
+        sent = lax.dynamic_index_in_dim(view, 1 - mine, 1, keepdims=False).astype(wire)
+        kept = lax.dynamic_index_in_dim(view, mine, 1, keepdims=False)
+        total = kept.astype(jnp.float32) + swap(sent, axis, bit).astype(jnp.float32)
+        parts = total.astype(wire).reshape((-1,) + rest)
+    return parts[0]
+
+
+def double(piece, axis, order):
+    have = []
+    parts = piece[None]
+    for bit in order:
+        low = 1 << sum(1 for other in have if other < bit)
+        have.append(bit)
+        rest = parts.shape[1:]
+        other = swap(parts, axis, bit)
+        mine = bit_of(axis, bit) == 1
+        first = jnp.where(mine, other, parts)
+        second = jnp.where(mine, parts, other)
+        high = parts.shape[0] // low
+        pair = jnp.stack(
+            (first.reshape((high, low) + rest), second.reshape((high, low) + rest)), axis=1
+        )
+        parts = pair.reshape((-1,) + rest)
+    return parts
+
+
+def reduce_matrix(grad, flip):
+    dp_count, ctx_count = lax.axis_size("dp"), lax.axis_size("ctx")
+    rows, columns = grad.shape
+    order = list(range(bits_in("dp")))
+    if flip:
+        order = order[:1] + order[:0:-1]
+    own = rows // dp_count
+    shard = halve(grad.reshape(dp_count, own, columns), "dp", order, jnp.bfloat16)
+    order = list(range(bits_in("ctx")))
+    extra = -own % ctx_count
+    if extra:
+        shard = jnp.pad(shard, ((0, extra), (0, 0)))
+    piece = halve(shard.reshape(ctx_count, -1, columns), "ctx", order, jnp.bfloat16)
+    gathered = double(piece, "ctx", order[::-1]).reshape(-1, columns)
+    return gathered[:own].astype(jnp.float32)
+
+
+def reduce_vectors(grads):
+    dp_count = lax.axis_size("dp")
+    parts = jnp.concatenate([grad.reshape(dp_count, -1) for grad in grads], axis=1)
+    total = halve(parts, "dp", list(range(bits_in("dp"))), jnp.float32)
+    for bit in range(bits_in("ctx")):
+        total = total + swap(total, "ctx", bit)
+    sizes = [grad.shape[0] // dp_count for grad in grads]
+    return jnp.split(total, [sum(sizes[: i + 1]) for i in range(len(sizes) - 1)])
+
+
+def gather_vectors(shards):
+    joined = jnp.concatenate(shards).astype(jnp.float32)
+    parts = double(joined, "dp", list(range(bits_in("dp"))))
+    sizes = [shard.shape[0] for shard in shards]
+    pieces = jnp.split(parts, [sum(sizes[: i + 1]) for i in range(len(sizes) - 1)], axis=1)
+    return [piece.reshape(-1) for piece in pieces]
 
 
 def per_device(
@@ -59,15 +141,33 @@
     total_rows = seq_count * local_rows
     place_index = lax.axis_index("ctx")
     query_pos = block_positions(block_order, place_index * local_rows, local_rows, block_rows)
-    gain_one, shift_one, qkv_full, qbias_full, vbias_full, proj_full, pbias_full = (
-        lax.all_gather(first_gain, "dp", axis=0, tiled=True),
-        lax.all_gather(first_shift, "dp", axis=0, tiled=True),
-        lax.all_gather(qkv_weight, "dp", axis=0, tiled=True),
-        lax.all_gather(query_bias, "dp", axis=0, tiled=True),
-        lax.all_gather(value_bias, "dp", axis=0, tiled=True),
-        lax.all_gather(proj_weight, "dp", axis=0, tiled=True),
-        lax.all_gather(proj_bias, "dp", axis=0, tiled=True),
-    )
+    (
+        gain_one,
+        shift_one,
+        qbias_full,
+        vbias_full,
+        pbias_full,
+        gain_two,
+        shift_two,
+        ubias_full,
+        dbias_full,
+    ) = gather_vectors(
+        (
+            first_gain,
+            first_shift,
+            query_bias,
+            value_bias,
+            proj_bias,
+            second_gain,
+            second_shift,
+            up_bias,
+            down_bias,
+        )
+    )
+    qkv_full = lax.all_gather(qkv_weight, "dp", axis=0, tiled=True)
+    proj_full = lax.all_gather(proj_weight, "dp", axis=0, tiled=True)
+    up_full = lax.all_gather(up_weight, "dp", axis=0, tiled=True)
+    down_full = lax.all_gather(down_weight, "dp", axis=0, tiled=True)
     inputs = tokens.reshape(total_rows, width).astype(jnp.float32)
     normed_one = layer_norm(inputs, gain_one, shift_one).astype(jnp.bfloat16)
     joined = jnp.dot(normed_one, qkv_full, preferred_element_type=jnp.float32)
@@ -112,23 +212,12 @@
     attended = attended_full.reshape(total_rows, width).astype(jnp.bfloat16)
     branch = jnp.dot(attended, proj_full, preferred_element_type=jnp.float32) + pbias_full
     middle = inputs + branch
-    gain_two, shift_two, up_full, ubias_full, down_full, dbias_full = (
-        lax.all_gather(second_gain, "dp", axis=0, tiled=True),
-        lax.all_gather(second_shift, "dp", axis=0, tiled=True),
-        lax.all_gather(up_weight, "dp", axis=0, tiled=True),
-        lax.all_gather(up_bias, "dp", axis=0, tiled=True),
-        lax.all_gather(down_weight, "dp", axis=0, tiled=True),
-        lax.all_gather(down_bias, "dp", axis=0, tiled=True),
-    )
     normed_two = layer_norm(middle, gain_two, shift_two).astype(jnp.bfloat16)
     hidden = jnp.dot(normed_two, up_full, preferred_element_type=jnp.float32) + ubias_full
     active = gelu_tanh(hidden).astype(jnp.bfloat16)
     result = middle + jnp.dot(active, down_full, preferred_element_type=jnp.float32) + dbias_full
     output = result.astype(jnp.bfloat16).reshape(tokens.shape)
-    up_back, down_back = (
-        lax.all_gather(up_weight, "dp", axis=0, tiled=True),
-        lax.all_gather(down_weight, "dp", axis=0, tiled=True),
-    )
+    up_back, down_back = up_full, down_full
     upstream = cotangent.reshape(total_rows, width)
     upstream_full = upstream.astype(jnp.float32)
     grad_down = jnp.einsum("rf,rd->fd", active, upstream, preferred_element_type=jnp.float32)
@@ -142,10 +231,7 @@
     norm_pull_two = jax.vjp(layer_norm, middle, gain_two, shift_two)[1]
     d_middle_part, grad_gain_two, grad_shift_two = norm_pull_two(d_normed_two)
     d_middle = upstream_full + d_middle_part
-    qkv_back, proj_back = (
-        lax.all_gather(qkv_weight, "dp", axis=0, tiled=True),
-        lax.all_gather(proj_weight, "dp", axis=0, tiled=True),
-    )
+    qkv_back, proj_back = qkv_full, proj_full
     d_branch = d_middle.astype(jnp.bfloat16)
     grad_proj = jnp.einsum("rd,re->de", attended, d_branch, preferred_element_type=jnp.float32)
     grad_pbias = jnp.sum(d_branch.astype(jnp.float32), axis=0)
@@ -192,92 +278,42 @@
     d_keys = d_key_sum.reshape(total_rows, width).astype(jnp.bfloat16)
     d_values = d_value_sum.reshape(total_rows, width).astype(jnp.bfloat16)
     d_joined = jnp.concatenate((d_queries, d_keys, d_values), axis=1)
-    grad_qkv = jnp.einsum("rd,re->de", normed_one, d_joined, preferred_element_type=jnp.float32)
+    grad_parts = [
+        jnp.einsum("rd,re->de", normed_one, part, preferred_element_type=jnp.float32)
+        for part in (d_queries, d_keys, d_values)
+    ]
     grad_qbias = jnp.sum(d_queries.astype(jnp.float32), axis=0)
     grad_vbias = jnp.sum(d_values.astype(jnp.float32), axis=0)
     d_normed_one = jnp.einsum("re,de->rd", d_joined, qkv_back, preferred_element_type=jnp.float32)
     norm_pull_one = jax.vjp(layer_norm, inputs, gain_one, shift_one)[1]
     d_inputs, grad_gain_one, grad_shift_one = norm_pull_one(d_normed_one)
     grad_tokens = (d_middle + d_inputs).astype(jnp.bfloat16).reshape(tokens.shape)
-    shard_count = lax.axis_size("dp")
-    matrices = (grad_qkv, grad_proj, grad_up, grad_down)
-    flat_pieces = (
-        lax.psum_scatter(grad_qkv.reshape(-1), ("dp", "ctx"), scatter_dimension=0, tiled=True),
-        lax.psum_scatter(grad_proj.reshape(-1), ("dp", "ctx"), scatter_dimension=0, tiled=True),
-        lax.psum_scatter(grad_up.reshape(-1), ("dp", "ctx"), scatter_dimension=0, tiled=True),
-        lax.psum_scatter(grad_down.reshape(-1), ("dp", "ctx"), scatter_dimension=0, tiled=True),
-    )
-    flat_shards = (
-        lax.all_gather(flat_pieces[0].astype(jnp.bfloat16), "ctx", axis=0, tiled=True).astype(
-            jnp.float32
-        ),
-        lax.all_gather(flat_pieces[1].astype(jnp.bfloat16), "ctx", axis=0, tiled=True).astype(
-            jnp.float32
-        ),
-        lax.all_gather(flat_pieces[2].astype(jnp.bfloat16), "ctx", axis=0, tiled=True).astype(
-            jnp.float32
-        ),
-        lax.all_gather(flat_pieces[3].astype(jnp.bfloat16), "ctx", axis=0, tiled=True).astype(
-            jnp.float32
-        ),
-    )
-    shaped = [
-        flat_shards[number].reshape(
-            matrices[number].shape[0] // shard_count, matrices[number].shape[1]
-        )
-        for number in range(4)
-    ]
-    vector_parts = (
-        lax.psum_scatter(grad_gain_one, "dp", scatter_dimension=0, tiled=True).astype(jnp.float32),
-        lax.psum_scatter(grad_shift_one, "dp", scatter_dimension=0, tiled=True).astype(jnp.float32),
-        lax.psum_scatter(
-            grad_qbias.astype(jnp.bfloat16), "dp", scatter_dimension=0, tiled=True
-        ).astype(jnp.float32),
-        lax.psum_scatter(
-            grad_vbias.astype(jnp.bfloat16), "dp", scatter_dimension=0, tiled=True
-        ).astype(jnp.float32),
-        lax.psum_scatter(
-            grad_pbias.astype(jnp.bfloat16), "dp", scatter_dimension=0, tiled=True
-        ).astype(jnp.float32),
-        lax.psum_scatter(grad_gain_two, "dp", scatter_dimension=0, tiled=True).astype(jnp.float32),
-        lax.psum_scatter(grad_shift_two, "dp", scatter_dimension=0, tiled=True).astype(jnp.float32),
-        lax.psum_scatter(
-            grad_ubias.astype(jnp.bfloat16), "dp", scatter_dimension=0, tiled=True
-        ).astype(jnp.float32),
-        lax.psum_scatter(
-            grad_dbias.astype(jnp.bfloat16), "dp", scatter_dimension=0, tiled=True
-        ).astype(jnp.float32),
-    )
-    vectors = lax.psum(
-        (
-            vector_parts[0],
-            vector_parts[1],
-            vector_parts[2],
-            vector_parts[3],
-            vector_parts[4],
-            vector_parts[5],
-            vector_parts[6],
-            vector_parts[7],
-            vector_parts[8],
-        ),
-        "ctx",
-    )
+    shaped_qkv = jnp.concatenate(
+        [reduce_matrix(grad_parts[number], number == 2) for number in range(3)], axis=1
+    )
+    shaped_proj = reduce_matrix(grad_proj, True)
+    shaped_up = reduce_matrix(grad_up, True)
+    shaped_down = reduce_matrix(grad_down, False)
+    early = reduce_vectors(
+        (grad_pbias, grad_gain_two, grad_shift_two, grad_ubias, grad_dbias)
+    )
+    late = reduce_vectors((grad_gain_one, grad_shift_one, grad_qbias, grad_vbias))
     return (
         output,
         grad_tokens,
-        vectors[0],
-        vectors[1],
-        shaped[0],
-        vectors[2],
-        vectors[3],
-        shaped[1],
-        vectors[4],
-        vectors[5],
-        vectors[6],
-        shaped[2],
-        vectors[7],
-        shaped[3],
-        vectors[8],
+        late[0],
+        late[1],
+        shaped_qkv,
+        late[2],
+        late[3],
+        shaped_proj,
+        early[0],
+        early[1],
+        early[2],
+        shaped_up,
+        early[3],
+        shaped_down,
+        early[4],
     )
 
 

time: 1790 us -> 1020 us (0.57)
  blocking collectives: 1020 us -> 0 us
  waiting for transfers between devices: 280 us -> 519 us
  starting transfers between devices: 0.57 us -> 51 us
  local copies, waits for them, and re-layouts: 109 us -> 74.9 us
    unnamed x3 -> x0, blocking collectives: 951 us -> none
    ppermute x0 -> x55, waiting for transfers between devices: none -> 264 us  [swap(): return lax.ppermute(values, axis, [(i, i ^ 1 << bit) for i in range(count)])]
    reshape x8 -> x3, local copies, waits for them, and re-layouts: 79.6 us -> 0.5 us  [double(): parts = pair.reshape((-1,) + rest)]
    ppermute x0 -> x55, starting transfers between devices: none -> 50.5 us  [swap(): return lax.ppermute(values, axis, [(i, i ^ 1 << bit) for i in range(count)])]
    all_gather x2 -> x0, blocking collectives: 48.7 us -> none  [the longest x1 32.2 us: per_device(): lax.all_gather(flat_pieces[0].astype(jnp.bfloat16), 'ctx', axis=0, tiled=...]
    convert_element_type x13 -> x29, other arithmetic: 0.43 us -> 34.2 us  [the longest x24 31.8 us: halve(): parts = total.astype(wire).reshape((-1,) + rest)]
    convert_element_type x0 -> x14, local copies, waits for them, and re-layouts: none -> 31 us  [the longest x6 17.8 us: halve(): lax.dynamic_index_in_dim(view, 1 - mine, 1, keepdims=False).astype(wire)]
    reshape x5 -> x7, other arithmetic: 31.3 us -> 1.81 us  [double(): parts = pair.reshape((-1,) + rest)]
  transfers between devices with their start and end apart: 10 -> 63, of which waited for: 8 -> 45; matrix products, arithmetic and copies ran while one was open for 18% -> 34% of each run, Pallas kernels for 0% -> 0%
where the time goes in v1:
time: 1020 us; the launch traced here: 1010 us
  waiting for transfers between devices  519 us (51%)
  matrix products  273 us (27%)
  other arithmetic  79.6 us (8%)
  local copies, waits for them, and re-layouts  74.9 us (7%)
  starting transfers between devices  51 us (5%)
  between operations  15.9 us (2%)
    ppermute x55, waiting for transfers between devices, swap(): return lax.ppermute(values, axis, [(i, i ^ 1 << bit) for i in range(count)])  264 us
    all_gather x1, waiting for transfers between devices, per_device(): piece_keys = lax.all_gather(keys, 'ctx', axis=1, tiled=True)  77.2 us
    all_gather x1, waiting for transfers between devices, per_device(): up_full = lax.all_gather(up_weight, 'dp', axis=0, tiled=True)  55.6 us
    ppermute x55, starting transfers between devices, swap(): return lax.ppermute(values, axis, [(i, i ^ 1 << bit) for i in range(count)])  50.5 us
    all_gather x1, waiting for transfers between devices, per_device(): down_full = lax.all_gather(down_weight, 'dp', axis=0, tiled=True)  47.9 us
    dot_general x1, matrix products, per_device(): jnp.einsum('sqhd,skhd->sqhk', d_heads, value_heads, preferred_element_typ...  44.3 us
    all_gather x1, waiting for transfers between devices, per_device(): qkv_full = lax.all_gather(qkv_weight, 'dp', axis=0, tiled=True)  37.4 us
    all_gather x1, waiting for transfers between devices, per_device(): piece_values = lax.all_gather(values, 'ctx', axis=1, tiled=True)  34.2 us
  transfers between devices with their start and end apart: 63, of which 45 were waited for; matrix products, arithmetic and copies ran while one was open for 34% of the time, Pallas kernels for 0%

profile of v1, /device:TPU:0, one launch (start us, length us, event | category | flops | bytes accessed | tf_op | source)
XLA Modules:
  0.0 1013.1 jit_solution(4387502128471183326)
XLA Ops:
  16.1 2.6 collective-permute-start.1
  25.4 37.4 %all-gather.9.cloned.1.call-done = bf16[1088,3264]{1,0:T(8,128)(2,1)} async-done(((bf16[136,3264]{1,0:T(8,128)(2,1)}), bf16[1088,3264]{1,0:T(8,128)(2,1)}) %all-gather.9.cloned.1.call-update) | async-done | bytes 7102480 | tf_op jit(solution)/shard_map/all_gather | solution.py:167
  62.8 6.9 fusion.148
  69.7 2.7 copy-done.22
  73.8 3.7 fusion.66
  81.6 77.2 %all-gather.19.cloned.1.call-done = bf16[2048,1088]{0,1:T(8,128)(2,1)} async-done(((bf16[512,1088]{0,1:T(8,128)(2,1)}), bf16[2048,1088]{0,1:T(8,128)(2,1)}) %all-gather.19.cloned.1.call-update) | async-done | bytes 4456464 | tf_op jit(solution)/shard_map/all_gather | solution.py:187
  158.8 28.5 %fusion.4 = (f32[512,17]{0,1:T(8,128)S(1)}, f32[17,2048,512]{2,1,0:T(8,128)}) fusion(pred[512,2048]{0,1:T(8,128)(4,1)S(1)} %broadcast_compare_fusion, bf16[2048,17,64]{0,2,1:T(8,128)(2,1)} %bitcast.458, bf16[512,17,64]{0,2,1:T(8,128)(2,1)S(1)} %bitcast.472), kind=kOutput, calls=%fused_computation.8 | convolution fusion | flops 2317344256 | bytes 77957120 | tf_op jit(solution)/shard_map/sqhd,skhd->sqhk/dot_general | solution.py:195
  187.3 23.0 %fusion.6 = f32[512,17]{0,1:T(8,128)S(1)} fusion(f32[17,2048,512]{2,1,0:T(8,128)} %get-tuple-element.76, f32[512,17]{0,1:T(8,128)S(1)} %broadcast_maximum_fusion, pred[512,2048]{0,1:T(8,128)(4,1)S(1)} %broadcast_compare_fusion), kind=kLoop, calls=%fused_computation.10 | loop fusion | flops 71294464 | bytes 72421376 | tf_op jit(solution)/shard_map/reduce_sum | solution.py:201
  210.3 34.2 %all-gather.17.cloned.1.call-done = bf16[2048,1088]{0,1:T(8,128)(2,1)} async-done(((bf16[512,1088]{0,1:T(8,128)(2,1)}), bf16[2048,1088]{0,1:T(8,128)(2,1)}) %all-gather.17.cloned.1.call-update) | async-done | bytes 4456464 | tf_op jit(solution)/shard_map/all_gather | solution.py:188
  244.5 29.3 %fusion.146 = (bf16[1,512,17,64]{1,3,2,0:T(8,128)(2,1)S(1)}, f32[1,512,17,64]{1,3,2,0:T(8,128)}) fusion(f32[512,17]{0,1:T(8,128)S(1)} %fusion.6, bf16[2048,17,64]{0,2,1:T(8,128)(2,1)} %bitcast.502, f32[17,2048,512]{2,1,0:T(8,128)} %get-tuple-element.76, f32[512,17]{0,1:T(8,128)S(1)} %broadcast_maximum_fusion, pred[512,2048]{0,1:T(8,128)(4,1)S(1)} %broadcast_compare_fusion), kind=kOutput, calls=%fused_computation.316 | convolution fusion | flops 2354118656 | bytes 80220160 | tf_op jit(solution)/shard_map/sqhk,skhd->sqhd/dot_general | solution.py:202
  274.4 3.4 fusion.147
  279.5 55.6 %all-gather.13.cloned.1.call-done = bf16[1088,4352]{1,0:T(8,128)(2,1)} async-done(((bf16[136,4352]{1,0:T(8,128)(2,1)}), bf16[1088,4352]{1,0:T(8,128)(2,1)}) %all-gather.13.cloned.1.call-update) | async-done | bytes 9469968 | tf_op jit(solution)/shard_map/all_gather | solution.py:169
  335.1 15.2 %fusion.34 = (bf16[4352,512]{0,1:T(8,128)(2,1)}, f32[512,4352]{1,0:T(8,128)}) fusion(f32[4352]{0:T(1024)S(1)} %add.457, bf16[1088,4352]{1,0:T(8,128)(2,1)} %all-gather.13.cloned.1.call-done, f32[512,1088]{0,1:T(8,128)} %copy-done.18, f32[1088]{0:T(1024)S(1)} %add.454, f32[1088]{0:T(1024)S(1)} %mul.243, f32[512]{0:T(512)S(1)} %fusion.130, ...), kind=kOutput, calls=%fused_computation.43 | convolution fusion | flops 4873682944 | bytes 25097728 | tf_op jit(solution)/shard_map/dot_general | solution.py:216
  350.3 47.9 %all-gather.15.cloned.1.call-done = bf16[4352,1088]{1,0:T(8,128)(2,1)} async-done(((bf16[544,1088]{1,0:T(8,128)(2,1)}), bf16[4352,1088]{1,0:T(8,128)(2,1)}) %all-gather.15.cloned.1.call-update) | async-done | bytes 9469968 | tf_op jit(solution)/shard_map/all_gather | solution.py:170
  398.2 14.9 %convert_reduce_fusion = (f32[4352]{0:T(1024)S(1)}, bf16[512,4352]{1,0:T(8,128)(2,1)}) fusion(f32[512,4352]{1,0:T(8,128)} %get-tuple-element.89, bf16[4352,1088]{1,0:T(8,128)(2,1)} %all-gather.15.cloned.1.call-done, bf16[1,512,1088]{1,2,0:T(8,128)(2,1)S(1)} %copy-done.23), kind=kOutput, calls=%fused_computation.44 | convolution fusion | flops 4897632256 | bytes 23970816 | tf_op jit(solution)/shard_map/rd,fd->rf/dot_general | solution.py:225
  413.1 8.7 multiply_reduce_fusion
  427.0 27.2 %fusion.39 = bf16[17,64,2048]{2,1,0:T(8,128)(2,1)} fusion(bf16[512,17,64]{0,2,1:T(8,128)(2,1)S(1)} %bitcast.494, f32[17,2048,512]{2,1,0:T(8,128)} %get-tuple-element.76, f32[512,17]{0,1:T(8,128)S(1)} %log_add_fusion, pred[512,2048]{0,1:T(8,128)(4,1)S(1)} %broadcast_compare_fusion), kind=kOutput, calls=%fused_computation.53 | convolution fusion | flops 2337406976 | bytes 77957120 | tf_op jit(solution)/shard_map/sqhk,sqhd->skhd/dot_general | solution.py:262
  456.3 44.3 %fusion.12 = bf16[512,17,2048]{0,2,1:T(8,128)(2,1)} fusion(f32[17,2048,512]{2,1,0:T(8,128)} %get-tuple-element.76, f32[512,17]{0,1:T(8,128)S(1)} %fusion.68, f32[512,17]{0,1:T(8,128)S(1)} %log_add_fusion, pred[512,2048]{0,1:T(8,128)(4,1)S(1)} %broadcast_compare_fusion, bf16[2048,17,64]{0,2,1:T(8,128)(2,1)} %bitcast.503, bf16[512,17,64]{0,2,1:T(8,128)(2,1)S(1)} %bitcast.496), kind=kOutput, calls=%fused_computation.15 | convolution fusion | flops 2370830336 | bytes 113643520 | tf_op jit(solution)/shard_map/sqhd,skhd->sqhk/dot_general | solution.py:254
  500.6 18.9 %convert_reduce_fusion.5 = (f32[17,64]{1,0:T(8,128)S(1)}, bf16[17,64,512]{2,1,0:T(8,128)(2,1)S(1)}) fusion(bf16[2048,17,64]{0,2,1:T(8,128)(2,1)} %bitcast.459, bf16[512,17,2048]{0,2,1:T(8,128)(2,1)} %fusion.12), kind=kOutput, calls=%fused_computation.110 | convolution fusion | flops 2283928576 | bytes 41226496 | tf_op jit(solution)/shard_map/sqhk,skhd->sqhd/dot_general | solution.py:258
  530.1 12.2 %fusion.140 = f32[1088,4352]{1,0:T(8,128)} fusion(bf16[512,4352]{1,0:T(8,128)(2,1)} %get-tuple-element.87, f32[512,1088]{0,1:T(8,128)} %copy-done.18, f32[1088]{0:T(1024)S(1)} %add.454, f32[1088]{0:T(1024)S(1)} %mul.243, f32[512]{0:T(512)S(1)} %fusion.130, f32[512]{0:T(512)S(1)} %broadcast_multiply_fusion), kind=kOutput, calls=%fused_computation.311 | convolution fusion | flops 4851400704 | bytes 25637376 | tf_op jit(solution)/shard_map/rd,rf->df/dot_general | solution.py:228
  542.4 6.3 fusion.36
  549.0 6.5 copy.138
  555.5 14.9 %fusion.57 = bf16[1,512,1088]{1,2,0:T(8,128)(2,1)} fusion(f32[512,1088]{0,1:T(8,128)} %copy-done.18, bf16[4352,1088]{1,0:T(8,128)(2,1)} %all-gather.15.cloned.1.call-done, f32[512,4352]{1,0:T(8,128)} %get-tuple-element.89, f32[1088]{0:T(1024)S(1)} %copy-done.43), kind=kOutput, calls=%fused_computation.78 | convolution fusion | flops 4870340608 | bytes 21729536 | tf_op jit(solution)/shard_map/dot_general | solution.py:218
  570.4 18.3 %convolution_convert_fusion = bf16[17,64,2048]{2,1,0:T(8,128)(2,1)} fusion(bf16[512,17,64]{0,2,1:T(8,128)(2,1)S(1)} %bitcast.473, bf16[512,17,2048]{0,2,1:T(8,128)(2,1)} %fusion.12), kind=kOutput, calls=%fused_computation.54 | convolution fusion | flops 2283929600 | bytes 41222144 | tf_op jit(solution)/shard_map/sqhk,sqhd->skhd/dot_general | solution.py:259
  588.7 12.0 %fusion.80 = f32[4,2,544,1088]{3,2,1,0:T(8,128)} fusion(bf16[4,2,544,512]{3,2,1,0:T(8,128)(2,1)} %bitcast.490, bf16[1,512,1088]{1,2,0:T(8,128)(2,1)} %param.31), kind=kOutput, calls=%fused_computation.135 | convolution fusion | flops 4848615424 | bytes 24510464 | tf_op jit(solution)/shard_map/rf,rd->fd/dot_general | solution.py:223
  600.8 6.7 dynamic-slice_convert_fusion
  614.2 12.3 %collective-permute-done.9 = bf16[2,1,136,1088]{3,2,1,0:T(8,128)(2,1)S(1)} collective-permute-done((bf16[2,1,136,1088]{3,2,1,0:T(8,128)(2,1)S(1)}, bf16[2,1,136,1088]{3,2,1,0:T(8,128)(2,1)S(1)}, u32[]{:S(2)}, u32[]{:S(2)}) %collective-permute-start.9) | collective-permute-done | bytes 591904 | tf_op jit(solution)/shard_map/ppermute | solution.py:38
  627.5 2.9 collective-permute-done.30
  632.1 4.4 collective-permute-done.10
  641.4 10.0 collective-permute-done.11
  653.1 13.7 %collective-permute-done.32 = bf16[2,1,34,1088]{3,2,1,0:T(8,128)(2,1)S(1)} collective-permute-done((bf16[2,1,34,1088]{3,2,1,0:T(8,128)(2,1)S(1)}, bf16[2,1,34,1088]{3,2,1,0:T(8,128)(2,1)S(1)}, u32[]{:S(2)}, u32[]{:S(2)}) %collective-permute-start.32) | collective-permute-done | bytes 148000 | tf_op jit(solution)/shard_map/ppermute | solution.py:38
  667.0 3.0 collective-permute-start.13
  670.0 14.3 %collective-permute-done.33 = bf16[1,1,34,1088]{3,2,1,0:T(8,128)(2,1)S(1)} collective-permute-done((bf16[1,1,34,1088]{3,2,1,0:T(8,128)(2,1)S(1)}, bf16[1,1,34,1088]{3,2,1,0:T(8,128)(2,1)S(1)}, u32[]{:S(2)}, u32[]{:S(2)}) %collective-permute-start.33) | collective-permute-done | bytes 74016 | tf_op jit(solution)/shard_map/ppermute | solution.py:38
  684.4 7.8 collective-permute-done.13
  692.4 3.1 collective-permute-done.34
  696.3 6.1 fusion.19
  705.6 6.4 add_convert_fusion
  717.4 39.5 %collective-permute-done.42 = bf16[1,2,136,4352]{3,2,1,0:T(8,128)(2,1)} collective-permute-done((bf16[1,2,136,4352]{3,2,1,0:T(8,128)(2,1)}, bf16[1,2,136,4352]{3,2,1,0:T(8,128)(2,1)}, u32[]{:S(2)}, u32[]{:S(2)}) %collective-permute-start.42) | collective-permute-done | bytes 2367520 | tf_op jit(solution)/shard_map/ppermute | solution.py:38
  756.9 2.9 fusion.37
  765.1 7.6 collective-permute-done.49
  772.7 3.1 fusion.35
  780.5 16.3 %collective-permute-done.43 = bf16[1,1,136,4352]{3,2,1,0:T(8,128)(2,1)} collective-permute-done((bf16[1,1,136,4352]{3,2,1,0:T(8,128)(2,1)}, bf16[1,1,136,4352]{3,2,1,0:T(8,128)(2,1)}, u32[]{:S(2)}, u32[]{:S(2)}) %collective-permute-start.43) | collective-permute-done | bytes 1183776 | tf_op jit(solution)/shard_map/ppermute | solution.py:38
  796.8 2.7 add_convert_fusion.6
  802.9 2.8 collective-permute-done.50
  807.7 10.3 %collective-permute-done.44 = bf16[2,1,34,4352]{3,0,2,1:T(2,128)(2,1)S(1)} collective-permute-done((bf16[2,1,34,4352]{3,0,2,1:T(2,128)(2,1)S(1)}, bf16[2,1,34,4352]{3,0,2,1:T(2,128)(2,1)S(1)}, u32[]{:S(2)}, u32[]{:S(2)}) %collective-permute-start.44) | collective-permute-done | bytes 591904 | tf_op jit(solution)/shard_map/ppermute | solution.py:38
  820.0 3.4 collective-permute-start.45
  823.4 13.3 %collective-permute-done.51 = bf16[2,1,136,1088]{3,2,1,0:T(8,128)(2,1)S(1)} collective-permute-done((bf16[2,1,136,1088]{3,2,1,0:T(8,128)(2,1)S(1)}, bf16[2,1,136,1088]{3,2,1,0:T(8,128)(2,1)S(1)}, u32[]{:S(2)}, u32[]{:S(2)}) %collective-permute-start.51) | collective-permute-done | bytes 591904 | tf_op jit(solution)/shard_map/ppermute | solution.py:38
  840.1 8.8 fusion.64
  853.7 2.9 fusion.86
  868.3 2.6 collective-permute-start.6
  880.2 2.7 collective-permute-done.40
  889.4 21.1 %collective-permute-done.46 = bf16[1,34,4352]{2,1,0:T(8,128)(2,1)S(1)} collective-permute-done((bf16[1,34,4352]{2,1,0:T(8,128)(2,1)S(1)}, bf16[1,34,4352]{2,1,0:T(8,128)(2,1)S(1)}, u32[]{:S(2)}, u32[]{:S(2)}) %collective-permute-start.46) | collective-permute-done | bytes 295968 | tf_op jit(solution)/shard_map/ppermute | solution.py:38
  911.2 4.4 collective-permute-done.53
  916.6 11.7 %collective-permute-done.47 = bf16[2,34,4352]{2,0,1:T(2,128)(2,1)S(1)} collective-permute-done((bf16[2,34,4352]{2,0,1:T(2,128)(2,1)S(1)}, bf16[2,34,4352]{2,0,1:T(2,128)(2,1)S(1)}, u32[]{:S(2)}, u32[]{:S(2)}) %collective-permute-start.47) | collective-permute-done | bytes 591904 | tf_op jit(solution)/shard_map/ppermute | solution.py:38
  930.6 3.6 reshape.900
  934.2 7.6 collective-permute-done.54
  950.5 12.4 %collective-permute-done.16 = bf16[2,1,136,1088]{3,2,1,0:T(8,128)(2,1)S(1)} collective-permute-done((bf16[2,1,136,1088]{3,2,1,0:T(8,128)(2,1)S(1)}, bf16[2,1,136,1088]{3,2,1,0:T(8,128)(2,1)S(1)}, u32[]{:S(2)}, u32[]{:S(2)}) %collective-permute-start.16) | collective-permute-done | bytes 591904 | tf_op jit(solution)/shard_map/ppermute | solution.py:38
  966.8 5.0 collective-permute-done.17
  974.4 5.1 collective-permute-done.18
  982.7 6.1 collective-permute-done.19
  988.9 2.8 collective-permute-done.26
  991.9 2.9 collective-permute-done.20
  994.9 2.9 collective-permute-done.27
  998.0 2.9 collective-permute-done.21
  (389 shorter events, 147.1 us)
Async XLA Ops:
  7.2 55.6 %all-gather.9.cloned.1.call-start = ((), (), s32[]{:S(2)}) async-start(), calls=%async_computation.2 | async-start | bytes 8146944 | tf_op jit(solution)/shard_map/all_gather | solution.py:167
  7.9 150.9 %all-gather.19.cloned.1.call-start = ((), (), s32[]{:S(2)}) async-start(), calls=%async_computation.9 | async-start | bytes 5570560 | tf_op jit(solution)/shard_map/all_gather | solution.py:187
  14.1 2.0 collective-permute-start
  16.1 4.3 collective-permute-start.1
  20.5 4.1 collective-permute-start.2
  73.6 171.0 %all-gather.17.cloned.1.call-start = ((), (), s32[]{:S(2)}) async-start(), calls=%async_computation.8 | async-start | bytes 5570560 | tf_op jit(solution)/shard_map/all_gather | solution.py:188
  77.5 196.9 %all-gather.11.cloned.1.call-start = ((), (), s32[]{:S(2)}) async-start(), calls=%async_computation.3 | async-start | bytes 2820096 | tf_op jit(solution)/shard_map/all_gather | solution.py:168
  78.0 257.1 %all-gather.13.cloned.1.call-start = ((), (), s32[]{:S(2)}) async-start(), calls=%async_computation.4 | async-start | bytes 10653696 | tf_op jit(solution)/shard_map/all_gather | solution.py:169
  78.6 319.6 %all-gather.15.cloned.1.call-start = ((), (), s32[]{:S(2)}) async-start(), calls=%async_computation.5 | async-start | bytes 11280384 | tf_op jit(solution)/shard_map/all_gather | solution.py:170
  79.2 760.9 %reduce-scatter.5.cloned.1.call-start = ((), (), s32[]{:S(2)}) async-start(), calls=%async_computation.7 | async-start | bytes 5570560 | tf_op jit(solution)/shard_map/reduce_scatter | solution.py:273
  279.5 118.7 %copy-start.23 = (bf16[1,512,1088]{1,2,0:T(8,128)(2,1)S(1)}, bf16[1,512,1088]{1,2,0:T(8,128)(2,1)}, u32[]{:S(2)}) copy-start(bf16[1,512,1088]{1,2,0:T(8,128)(2,1)} %param.31) | copy-start | bytes 3342340
  454.2 385.9 %reduce-scatter.3.cloned.1.call-start = ((), (), s32[]{:S(2)}) async-start(), calls=%async_computation.6 | async-start | bytes 5570560 | tf_op jit(solution)/shard_map/reduce_scatter | solution.py:270
  522.5 85.1 %collective-permute-start.8 = (bf16[4,1,136,1088]{3,2,1,0:T(8,128)(2,1)}, bf16[4,1,136,1088]{3,2,1,0:T(8,128)(2,1)}, u32[]{:S(2)}, u32[]{:S(2)}) collective-permute-start(bf16[4,1,136,1088]{3,2,1,0:T(8,128)(2,1)} %dynamic-slice_convert_fusion.5), channel_id=1, source_target_pairs={{0,4},{4,0},{8,12},{12,8},{16,20},{20,16},{24,28},{28,24},{1,5},{5... | collective-permute-start | bytes 3551240 | tf_op jit(solution)/shard_map/ppermute | solution.py:38
  529.5 81.8 %collective-permute-start.29 = (bf16[4,1,136,1088]{3,2,1,0:T(8,128)(2,1)}, bf16[4,1,136,1088]{3,2,1,0:T(8,128)(2,1)}, u32[]{:S(2)}, u32[]{:S(2)}) collective-permute-start(bf16[4,1,136,1088]{3,2,1,0:T(8,128)(2,1)} %dynamic-slice_convert_fusion.2), channel_id=1, source_target_pairs={{0,4},{4,0},{8,12},{12,8},{16,20},{20,16},{24,28},{28,24},{1,5},{5... | collective-permute-start | bytes 3551240 | tf_op jit(solution)/shard_map/ppermute | solution.py:38
  548.7 147.6 %collective-permute-start.41 = (bf16[4,1,136,4352]{3,2,0,1:T(8,128)(2,1)}, bf16[4,1,136,4352]{3,2,0,1:T(8,128)(2,1)}, u32[]{:S(2)}, u32[]{:S(2)}) collective-permute-start(bf16[4,1,136,4352]{3,2,0,1:T(8,128)(2,1)} %fusion.36), channel_id=1, source_target_pairs={{0,4},{4,0},{8,12},{12,8},{16,20},{20,16},{24,28},{28,24},{1,5},{5... | collective-permute-start | bytes 14204936 | tf_op jit(solution)/shard_map/ppermute | solution.py:38
  607.5 98.1 %collective-permute-start.48 = (bf16[4,1,544,1088]{3,2,1,0:T(8,128)(2,1)}, bf16[4,1,544,1088]{3,2,1,0:T(8,128)(2,1)}, u32[]{:S(2)}, u32[]{:S(2)}) collective-permute-start(bf16[4,1,544,1088]{3,2,1,0:T(8,128)(2,1)} %dynamic-slice_convert_fusion), channel_id=1, source_target_pairs={{0,4},{4,0},{8,12},{12,8},{16,20},{20,16},{24,28},{28,24},{1,5},{5... | collective-permute-start | bytes 14204936 | tf_op jit(solution)/shard_map/ppermute | solution.py:38
  610.0 16.5 %collective-permute-start.9 = (bf16[2,1,136,1088]{3,2,1,0:T(8,128)(2,1)S(1)}, bf16[2,1,136,1088]{3,2,1,0:T(8,128)(2,1)S(1)}, u32[]{:S(2)}, u32[]{:S(2)}) collective-permute-start(bf16[2,1,136,1088]{3,2,1,0:T(8,128)(2,1)S(1)} %dynamic-slice_bitcast_fusion.6), channel_id=1, source_target_pairs={{0,8},{4,12},{8,0},{12,4},{16,24},{20,28},{24,16},{28,20},{1,9},{5... | collective-permute-start | bytes 1775624 | tf_op jit(solution)/shard_map/ppermute | solution.py:38
  613.7 16.7 %collective-permute-start.30 = (bf16[1,2,136,1088]{3,2,1,0:T(8,128)(2,1)S(1)}, bf16[1,2,136,1088]{3,2,1,0:T(8,128)(2,1)S(1)}, u32[]{:S(2)}, u32[]{:S(2)}) collective-permute-start(bf16[1,2,136,1088]{3,2,1,0:T(8,128)(2,1)S(1)} %dynamic-slice_bitcast_fusion.3), channel_id=1, source_target_pairs={{0,16},{4,20},{8,24},{12,28},{16,0},{20,4},{24,8},{28,12},{1,17},{... | collective-permute-start | bytes 1775624 | tf_op jit(solution)/shard_map/ppermute | solution.py:38
  626.8 9.8 collective-permute-start.10
  631.4 8.2 collective-permute-start.31
  636.8 14.6 %collective-permute-start.11 = (bf16[2,1,34,1088]{3,2,0,1:T(8,128)(2,1)S(1)}, bf16[2,1,34,1088]{3,2,0,1:T(8,128)(2,1)S(1)}, u32[]{:S(2)}, u32[]{:S(2)}) collective-permute-start(bf16[2,1,34,1088]{3,2,0,1:T(8,128)(2,1)S(1)} %dynamic-slice_bitcast_fusion.10), channel_id=1, source_target_pairs={{0,1},{1,0},{2,3},{3,2},{4,5},{5,4},{6,7},{7,6},{8,9},{9,8},{10,11... | collective-permute-start | bytes 443912 | tf_op jit(solution)/shard_map/ppermute | solution.py:38
  639.8 27.0 %collective-permute-start.32 = (bf16[2,1,34,1088]{3,2,1,0:T(8,128)(2,1)S(1)}, bf16[2,1,34,1088]{3,2,1,0:T(8,128)(2,1)S(1)}, u32[]{:S(2)}, u32[]{:S(2)}) collective-permute-start(bf16[2,1,34,1088]{3,2,1,0:T(8,128)(2,1)S(1)} %dynamic-slice_bitcast_fusion.7), channel_id=1, source_target_pairs={{0,1},{1,0},{2,3},{3,2},{4,5},{5,4},{6,7},{7,6},{8,9},{9,8},{10,11... | collective-permute-start | bytes 443912 | tf_op jit(solution)/shard_map/ppermute | solution.py:38
  651.5 15.5 %collective-permute-start.12 = (bf16[1,1,34,1088]{3,2,0,1:T(8,128)(2,1)S(1)}, bf16[1,1,34,1088]{3,2,0,1:T(8,128)(2,1)S(1)}, u32[]{:S(2)}, u32[]{:S(2)}) collective-permute-start(bf16[1,1,34,1088]{3,2,0,1:T(8,128)(2,1)S(1)} %constant_dynamic-slice_fusion.14), channel_id=1, source_target_pairs={{0,2},{1,3},{2,0},{3,1},{4,6},{5,7},{6,4},{7,5},{8,10},{9,11},{10,... | collective-permute-start | bytes 221960 | tf_op jit(solution)/shard_map/ppermute | solution.py:38
  666.9 17.4 %collective-permute-start.33 = (bf16[1,1,34,1088]{3,2,1,0:T(8,128)(2,1)S(1)}, bf16[1,1,34,1088]{3,2,1,0:T(8,128)(2,1)S(1)}, u32[]{:S(2)}, u32[]{:S(2)}) collective-permute-start(bf16[1,1,34,1088]{3,2,1,0:T(8,128)(2,1)S(1)} %constant_dynamic-slice_fusion.8), channel_id=1, source_target_pairs={{0,2},{1,3},{2,0},{3,1},{4,6},{5,7},{6,4},{7,5},{8,10},{9,11},{10,... | collective-permute-start | bytes 221960 | tf_op jit(solution)/shard_map/ppermute | solution.py:38
  667.0 25.2 %collective-permute-start.13 = (bf16[1,34,1088]{2,1,0:T(8,128)(2,1)S(1)}, bf16[1,34,1088]{2,1,0:T(8,128)(2,1)S(1)}, u32[]{:S(2)}, u32[]{:S(2)}) collective-permute-start(bf16[1,34,1088]{2,1,0:T(8,128)(2,1)S(1)} %fusion.99), channel_id=1, source_target_pairs={{0,2},{1,3},{2,0},{3,1},{4,6},{5,7},{6,4},{7,5},{8,10},{9,11},{10,... | collective-permute-start | bytes 221960 | tf_op jit(solution)/shard_map/ppermute | solution.py:38
  684.4 11.2 %collective-permute-start.34 = (bf16[1,34,1088]{2,1,0:T(8,128)(2,1)S(1)}, bf16[1,34,1088]{2,1,0:T(8,128)(2,1)S(1)}, u32[]{:S(2)}, u32[]{:S(2)}) collective-permute-start(bf16[1,34,1088]{2,1,0:T(8,128)(2,1)S(1)} %fusion.102), channel_id=1, source_target_pairs={{0,2},{1,3},{2,0},{3,1},{4,6},{5,7},{6,4},{7,5},{8,10},{9,11},{10,... | collective-permute-start | bytes 221960 | tf_op jit(solution)/shard_map/ppermute | solution.py:38
  692.3 13.0 %collective-permute-start.14 = (bf16[2,34,1088]{2,1,0:T(8,128)(2,1)S(1)}, bf16[2,34,1088]{2,1,0:T(8,128)(2,1)S(1)}, u32[]{:S(2)}, u32[]{:S(2)}) collective-permute-start(bf16[2,34,1088]{2,1,0:T(8,128)(2,1)S(1)} %maximum_bitcast_fusion.2), channel_id=1, source_target_pairs={{0,1},{1,0},{2,3},{3,2},{4,5},{5,4},{6,7},{7,6},{8,9},{9,8},{10,11... | collective-permute-start | bytes 443912 | tf_op jit(solution)/shard_map/ppermute | solution.py:38
  696.3 20.1 %collective-permute-start.35 = (bf16[2,34,1088]{2,1,0:T(8,128)(2,1)}, bf16[2,34,1088]{2,1,0:T(8,128)(2,1)}, u32[]{:S(2)}, u32[]{:S(2)}) collective-permute-start(bf16[2,34,1088]{2,1,0:T(8,128)(2,1)} %maximum_bitcast_fusion.5), channel_id=1, source_target_pairs={{0,1},{1,0},{2,3},{3,2},{4,5},{5,4},{6,7},{7,6},{8,9},{9,8},{10,11... | collective-permute-start | bytes 443912 | tf_op jit(solution)/shard_map/ppermute | solution.py:38
  705.3 51.6 %collective-permute-start.42 = (bf16[1,2,136,4352]{3,2,1,0:T(8,128)(2,1)}, bf16[1,2,136,4352]{3,2,1,0:T(8,128)(2,1)}, u32[]{:S(2)}, u32[]{:S(2)}) collective-permute-start(bf16[1,2,136,4352]{3,2,1,0:T(8,128)(2,1)} %dynamic-slice_bitcast_fusion.1), channel_id=1, source_target_pairs={{0,16},{4,20},{8,24},{12,28},{16,0},{20,4},{24,8},{28,12},{1,17},{... | collective-permute-start | bytes 7102472 | tf_op jit(solution)/shard_map/ppermute | solution.py:38
  715.1 57.6 %collective-permute-start.49 = (bf16[2,1,544,1088]{3,2,0,1:T(8,128)(2,1)}, bf16[2,1,544,1088]{3,2,0,1:T(8,128)(2,1)}, u32[]{:S(2)}, u32[]{:S(2)}) collective-permute-start(bf16[2,1,544,1088]{3,2,0,1:T(8,128)(2,1)} %dynamic-slice_bitcast_fusion), channel_id=1, source_target_pairs={{0,8},{4,12},{8,0},{12,4},{16,24},{20,28},{24,16},{28,20},{1,9},{5... | collective-permute-start | bytes 7102472 | tf_op jit(solution)/shard_map/ppermute | solution.py:38
  762.3 34.5 %collective-permute-start.43 = (bf16[1,1,136,4352]{3,2,1,0:T(8,128)(2,1)}, bf16[1,1,136,4352]{3,2,1,0:T(8,128)(2,1)}, u32[]{:S(2)}, u32[]{:S(2)}) collective-permute-start(bf16[1,1,136,4352]{3,2,1,0:T(8,128)(2,1)} %constant_dynamic-slice_fusion.3), channel_id=1, source_target_pairs={{0,8},{4,12},{8,0},{12,4},{16,24},{20,28},{24,16},{28,20},{1,9},{5... | collective-permute-start | bytes 3551240 | tf_op jit(solution)/shard_map/ppermute | solution.py:38
  778.4 27.3 %collective-permute-start.50 = (bf16[1,1,544,1088]{3,2,0,1:T(8,128)(2,1)}, bf16[1,1,544,1088]{3,2,0,1:T(8,128)(2,1)}, u32[]{:S(2)}, u32[]{:S(2)}) collective-permute-start(bf16[1,1,544,1088]{3,2,0,1:T(8,128)(2,1)} %constant_dynamic-slice_fusion), channel_id=1, source_target_pairs={{0,16},{4,20},{8,24},{12,28},{16,0},{20,4},{24,8},{28,12},{1,17},{... | collective-permute-start | bytes 3551240 | tf_op jit(solution)/shard_map/ppermute | solution.py:38
  801.6 16.4 %collective-permute-start.44 = (bf16[2,1,34,4352]{3,0,2,1:T(2,128)(2,1)S(1)}, bf16[2,1,34,4352]{3,0,2,1:T(2,128)(2,1)S(1)}, u32[]{:S(2)}, u32[]{:S(2)}) collective-permute-start(bf16[2,1,34,4352]{3,0,2,1:T(2,128)(2,1)S(1)} %bitcast.497), channel_id=1, source_target_pairs={{0,1},{1,0},{2,3},{3,2},{4,5},{5,4},{6,7},{7,6},{8,9},{9,8},{10,11... | collective-permute-start | bytes 1775624 | tf_op jit(solution)/shard_map/ppermute | solution.py:38
  807.4 29.2 %collective-permute-start.51 = (bf16[2,1,136,1088]{3,2,1,0:T(8,128)(2,1)S(1)}, bf16[2,1,136,1088]{3,2,1,0:T(8,128)(2,1)S(1)}, u32[]{:S(2)}, u32[]{:S(2)}) collective-permute-start(bf16[2,1,136,1088]{3,2,1,0:T(8,128)(2,1)S(1)} %dynamic-slice_bitcast_fusion.2), channel_id=1, source_target_pairs={{0,1},{1,0},{2,3},{3,2},{4,5},{5,4},{6,7},{7,6},{8,9},{9,8},{10,11... | collective-permute-start | bytes 1775624 | tf_op jit(solution)/shard_map/ppermute | solution.py:38
  820.0 64.2 %collective-permute-start.45 = (bf16[1,1,34,4352]{3,2,0,1:T(8,128)(2,1)}, bf16[1,1,34,4352]{3,2,0,1:T(8,128)(2,1)}, u32[]{:S(2)}, u32[]{:S(2)}) collective-permute-start(bf16[1,1,34,4352]{3,2,0,1:T(8,128)(2,1)} %constant_dynamic-slice_fusion.1), channel_id=1, source_target_pairs={{0,2},{1,3},{2,0},{3,1},{4,6},{5,7},{6,4},{7,5},{8,10},{9,11},{10,... | collective-permute-start | bytes 887816 | tf_op jit(solution)/shard_map/ppermute | solution.py:38
  838.4 48.1 %collective-permute-start.52 = (bf16[1,1,136,1088]{3,2,1,0:T(8,128)(2,1)}, bf16[1,1,136,1088]{3,2,1,0:T(8,128)(2,1)}, u32[]{:S(2)}, u32[]{:S(2)}) collective-permute-start(bf16[1,1,136,1088]{3,2,1,0:T(8,128)(2,1)} %constant_dynamic-slice_fusion.22), channel_id=1, source_target_pairs={{0,2},{1,3},{2,0},{3,1},{4,6},{5,7},{6,4},{7,5},{8,10},{9,11},{10,... | collective-permute-start | bytes 887816 | tf_op jit(solution)/shard_map/ppermute | solution.py:38
  853.7 7.2 collective-permute-start.3
  860.1 85.0 %collective-permute-start.15 = (bf16[4,1,136,1088]{3,2,1,0:T(8,128)(2,1)}, bf16[4,1,136,1088]{3,2,1,0:T(8,128)(2,1)}, u32[]{:S(2)}, u32[]{:S(2)}) collective-permute-start(bf16[4,1,136,1088]{3,2,1,0:T(8,128)(2,1)} %dynamic-slice_convert_fusion.4), channel_id=1, source_target_pairs={{0,4},{4,0},{8,12},{12,8},{16,20},{20,16},{24,28},{28,24},{1,5},{5... | collective-permute-start | bytes 3551240 | tf_op jit(solution)/shard_map/ppermute | solution.py:38
  861.0 3.7 collective-permute-start.4
  862.4 2.4 collective-permute-start.36
  864.7 3.7 collective-permute-start.5
  864.8 6.1 collective-permute-start.37
  868.3 4.4 collective-permute-start.6
  870.9 3.7 collective-permute-start.38
  872.7 4.6 collective-permute-start.7
  874.6 3.7 collective-permute-start.39
  877.3 71.2 %collective-permute-start.22 = (bf16[4,1,136,1088]{3,2,1,0:T(8,128)(2,1)}, bf16[4,1,136,1088]{3,2,1,0:T(8,128)(2,1)S(1)}, u32[]{:S(2)}, u32[]{:S(2)}) collective-permute-start(bf16[4,1,136,1088]{3,2,1,0:T(8,128)(2,1)} %dynamic-slice_convert_fusion.3), channel_id=1, source_target_pairs={{0,4},{4,0},{8,12},{12,8},{16,20},{20,16},{24,28},{28,24},{1,5},{5... | collective-permute-start | bytes 3551240 | tf_op jit(solution)/shard_map/ppermute | solution.py:38
  878.4 4.5 collective-permute-start.40
  885.3 25.3 %collective-permute-start.46 = (bf16[1,34,4352]{2,1,0:T(8,128)(2,1)S(1)}, bf16[1,34,4352]{2,1,0:T(8,128)(2,1)S(1)}, u32[]{:S(2)}, u32[]{:S(2)}) collective-permute-start(bf16[1,34,4352]{2,1,0:T(8,128)(2,1)S(1)} %fusion.96), channel_id=1, source_target_pairs={{0,2},{1,3},{2,0},{3,1},{4,6},{5,7},{6,4},{7,5},{8,10},{9,11},{10,... | collective-permute-start | bytes 887816 | tf_op jit(solution)/shard_map/ppermute | solution.py:38
  887.6 28.1 %collective-permute-start.53 = (bf16[1,136,1088]{2,1,0:T(8,128)(2,1)S(1)}, bf16[1,136,1088]{2,1,0:T(8,128)(2,1)S(1)}, u32[]{:S(2)}, u32[]{:S(2)}) collective-permute-start(bf16[1,136,1088]{2,1,0:T(8,128)(2,1)S(1)} %fusion.98), channel_id=1, source_target_pairs={{0,2},{1,3},{2,0},{3,1},{4,6},{5,7},{6,4},{7,5},{8,10},{9,11},{10,... | collective-permute-start | bytes 887816 | tf_op jit(solution)/shard_map/ppermute | solution.py:38
  911.2 17.2 %collective-permute-start.47 = (bf16[2,34,4352]{2,0,1:T(2,128)(2,1)S(1)}, bf16[2,34,4352]{2,0,1:T(2,128)(2,1)S(1)}, u32[]{:S(2)}, u32[]{:S(2)}) collective-permute-start(bf16[2,34,4352]{2,0,1:T(2,128)(2,1)S(1)} %copy.134), channel_id=1, source_target_pairs={{0,1},{1,0},{2,3},{3,2},{4,5},{5,4},{6,7},{7,6},{8,9},{9,8},{10,11... | collective-permute-start | bytes 1775624 | tf_op jit(solution)/shard_map/ppermute | solution.py:38
  916.6 25.2 %collective-permute-start.54 = (bf16[2,136,1088]{2,1,0:T(8,128)(2,1)}, bf16[2,136,1088]{2,1,0:T(8,128)(2,1)}, u32[]{:S(2)}, u32[]{:S(2)}) collective-permute-start(bf16[2,136,1088]{2,1,0:T(8,128)(2,1)} %maximum_bitcast_fusion.1), channel_id=1, source_target_pairs={{0,1},{1,0},{2,3},{3,2},{4,5},{5,4},{6,7},{7,6},{8,9},{9,8},{10,11... | collective-permute-start | bytes 1775624 | tf_op jit(solution)/shard_map/ppermute | solution.py:38
  946.7 16.2 %collective-permute-start.16 = (bf16[2,1,136,1088]{3,2,1,0:T(8,128)(2,1)S(1)}, bf16[2,1,136,1088]{3,2,1,0:T(8,128)(2,1)S(1)}, u32[]{:S(2)}, u32[]{:S(2)}) collective-permute-start(bf16[2,1,136,1088]{3,2,1,0:T(8,128)(2,1)S(1)} %dynamic-slice_bitcast_fusion.5), channel_id=1, source_target_pairs={{0,8},{4,12},{8,0},{12,4},{16,24},{20,28},{24,16},{28,20},{1,9},{5... | collective-permute-start | bytes 1775624 | tf_op jit(solution)/shard_map/ppermute | solution.py:38
  948.9 16.0 %collective-permute-start.23 = (bf16[1,2,136,1088]{3,2,1,0:T(8,128)(2,1)S(1)}, bf16[1,2,136,1088]{3,2,1,0:T(8,128)(2,1)S(1)}, u32[]{:S(2)}, u32[]{:S(2)}) collective-permute-start(bf16[1,2,136,1088]{3,2,1,0:T(8,128)(2,1)S(1)} %dynamic-slice_bitcast_fusion.4), channel_id=1, source_target_pairs={{0,16},{4,20},{8,24},{12,28},{16,0},{20,4},{24,8},{28,12},{1,17},{... | collective-permute-start | bytes 1775624 | tf_op jit(solution)/shard_map/ppermute | solution.py:38
  963.1 8.7 collective-permute-start.17
  965.0 8.4 collective-permute-start.24
  972.0 7.5 collective-permute-start.18
  973.6 8.3 collective-permute-start.25
  979.6 9.3 collective-permute-start.19
  982.0 9.7 collective-permute-start.26
  988.9 6.0 collective-permute-start.20
  991.8 6.0 collective-permute-start.27
  994.9 6.0 collective-permute-start.21
  997.9 5.6 collective-permute-start.28
  (50 other events, 675.5 us)
Sparse Core Ops, SparseCore 0:
  9.9 52.7 all-gather.8
  73.7 85.0 all-gather.18
  161.0 83.5 all-gather.16
  246.3 28.0 all-gather.10
  276.1 58.9 all-gather.12
  336.8 61.3 all-gather.14
  454.3 80.9 reduce-scatter.4
  607.7 103.9 reduce-scatter.2

commit v2 on v1

--- a/solution.py
+++ b/solution.py
@@ -25,6 +25,7 @@
 
 def block_positions(block_order, first_row, count, block_rows):
     row_index = first_row + jnp.arange(count, dtype=jnp.int32)
+    row_index = row_index % (block_order.shape[0] * block_rows)
     block_index = row_index // block_rows
     numbers = jnp.arange(block_order.shape[0], dtype=jnp.int32)
     picked = jnp.sum(
@@ -46,7 +47,7 @@
     return lax.axis_size(axis).bit_length() - 1
 
 
-def halve(parts, axis, order, wire):
+def halve_steps(parts, axis, order, wire):
     left = list(range(bits_in(axis)))
     for bit in order:
         low = 1 << left.index(bit)
@@ -56,9 +57,35 @@
         mine = bit_of(axis, bit)
         sent = lax.dynamic_index_in_dim(view, 1 - mine, 1, keepdims=False).astype(wire)
         kept = lax.dynamic_index_in_dim(view, mine, 1, keepdims=False)
+        yield sent
         total = kept.astype(jnp.float32) + swap(sent, axis, bit).astype(jnp.float32)
         parts = total.astype(wire).reshape((-1,) + rest)
     return parts[0]
+
+
+def finish(steps):
+    while True:
+        try:
+            next(steps)
+        except StopIteration as stop:
+            return stop.value
+
+
+def tie(value, *others):
+    return lax.optimization_barrier((value,) + others)[0]
+
+
+def ring_gather(values, axis):
+    count = lax.axis_size(axis)
+    place = lax.axis_index(axis)
+    lower, upper = [values], [values]
+    for step in range(1, count):
+        lower.append(lax.ppermute(lower[-1], axis, [(i, i + 1) for i in range(step - 1, count - 1)]))
+        upper.append(lax.ppermute(upper[-1], axis, [(i + 1, i) for i in range(count - step)]))
+    blocks = [values]
+    for step in range(1, count):
+        blocks.append(jnp.where(place + step < count, upper[step], lower[count - step]))
+    return jnp.concatenate(blocks, axis=1)
 
 
 def double(piece, axis, order):
@@ -80,19 +107,23 @@
     return parts
 
 
-def reduce_matrix(grad, flip):
+def reduce_steps(grad, flip):
     dp_count, ctx_count = lax.axis_size("dp"), lax.axis_size("ctx")
     rows, columns = grad.shape
     order = list(range(bits_in("dp")))
     if flip:
         order = order[:1] + order[:0:-1]
     own = rows // dp_count
-    shard = halve(grad.reshape(dp_count, own, columns), "dp", order, jnp.bfloat16)
+    shard = yield from halve_steps(
+        grad.reshape(dp_count, own, columns), "dp", order, jnp.bfloat16
+    )
     order = list(range(bits_in("ctx")))
     extra = -own % ctx_count
     if extra:
         shard = jnp.pad(shard, ((0, extra), (0, 0)))
-    piece = halve(shard.reshape(ctx_count, -1, columns), "ctx", order, jnp.bfloat16)
+    piece = yield from halve_steps(
+        shard.reshape(ctx_count, -1, columns), "ctx", order, jnp.bfloat16
+    )
     gathered = double(piece, "ctx", order[::-1]).reshape(-1, columns)
     return gathered[:own].astype(jnp.float32)
 
@@ -100,7 +131,7 @@
 def reduce_vectors(grads):
     dp_count = lax.axis_size("dp")
     parts = jnp.concatenate([grad.reshape(dp_count, -1) for grad in grads], axis=1)
-    total = halve(parts, "dp", list(range(bits_in("dp"))), jnp.float32)
+    total = finish(halve_steps(parts, "dp", list(range(bits_in("dp"))), jnp.float32))
     for bit in range(bits_in("ctx")):
         total = total + swap(total, "ctx", bit)
     sizes = [grad.shape[0] // dp_count for grad in grads]
@@ -184,10 +215,11 @@
         key_pos = block_positions(block_order, start, count, block_rows)
         return (query_pos[:, None] >= key_pos[None, :], jnp.min(key_pos))
 
-    piece_keys = lax.all_gather(keys, "ctx", axis=1, tiled=True)
-    piece_values = lax.all_gather(values, "ctx", axis=1, tiled=True)
+    piece_keys = ring_gather(keys, "ctx")
+    piece_values = ring_gather(tie(values, piece_keys), "ctx")
+    piece_keys = tie(piece_keys, proj_full)
     count = piece_keys.shape[1]
-    visible, key_lowest = visible_mask(jnp.int32(0), count)
+    visible, key_lowest = visible_mask(place_index * local_rows, count)
     seen = visible[None, :, None, :]
     row_max = jnp.full((seq_count, local_rows, head_count), neg_large, jnp.float32)
     key_heads = piece_keys.reshape(seq_count, count, head_count, head_size)
@@ -199,6 +231,7 @@
     new_max = jnp.maximum(row_max, jnp.max(scores, axis=-1))
     weights = jnp.where(seen, jnp.exp(scores - new_max[..., None]), 0.0)
     row_total = jnp.sum(weights, axis=-1)
+    value_heads = tie(value_heads, up_full)
     accum = jnp.einsum(
         "sqhk,skhd->sqhd",
         weights.astype(jnp.bfloat16),
@@ -210,6 +243,7 @@
     attended_full = accum / row_total[..., None]
     log_total = row_max + jnp.log(row_total)
     attended = attended_full.reshape(total_rows, width).astype(jnp.bfloat16)
+    attended = tie(attended, down_full)
     branch = jnp.dot(attended, proj_full, preferred_element_type=jnp.float32) + pbias_full
     middle = inputs + branch
     normed_two = layer_norm(middle, gain_two, shift_two).astype(jnp.bfloat16)
@@ -240,28 +274,33 @@
     ).astype(jnp.bfloat16)
     d_heads = d_attended.reshape(seq_count, local_rows, head_count, head_size)
     delta = jnp.sum(d_heads.astype(jnp.float32) * attended_full, axis=-1)
-    piece_keys = lax.all_gather(keys, "ctx", axis=1, tiled=True)
-    piece_values = lax.all_gather(values, "ctx", axis=1, tiled=True)
-    count = piece_keys.shape[1]
-    visible, key_lowest = visible_mask(jnp.int32(0), count)
+    running = [reduce_steps(grad_down, False), reduce_steps(grad_up, True), reduce_steps(grad_proj, True)]
+
+    def after_exchange(value):
+        return tie(value, *[next(steps) for steps in running])
+
     seen = visible[None, :, None, :]
-    key_heads = piece_keys.reshape(seq_count, count, head_count, head_size)
-    value_heads = piece_values.reshape(seq_count, count, head_count, head_size)
+    key_heads = after_exchange(piece_keys).reshape(seq_count, count, head_count, head_size)
     scores = jnp.einsum(
         "sqhd,skhd->sqhk", query_heads, key_heads, preferred_element_type=jnp.float32
     )
     weights = jnp.where(seen, jnp.exp(scores - log_total[..., None]), 0.0)
+    value_heads = after_exchange(piece_values).reshape(seq_count, count, head_count, head_size)
     d_weights = jnp.einsum(
         "sqhd,skhd->sqhk", d_heads, value_heads, preferred_element_type=jnp.float32
     )
     d_scores = (weights * (d_weights - delta[..., None])).astype(jnp.bfloat16)
-    d_query = jnp.einsum("sqhk,skhd->sqhd", d_scores, key_heads, preferred_element_type=jnp.float32)
+    d_heads = after_exchange(d_heads)
+    d_value = jnp.einsum(
+        "sqhk,sqhd->skhd", weights.astype(jnp.bfloat16), d_heads, preferred_element_type=jnp.float32
+    ).reshape(seq_count, count, width)
     d_key = jnp.einsum(
         "sqhk,sqhd->skhd", d_scores, query_heads, preferred_element_type=jnp.float32
     ).reshape(seq_count, count, width)
-    d_value = jnp.einsum(
-        "sqhk,sqhd->skhd", weights.astype(jnp.bfloat16), d_heads, preferred_element_type=jnp.float32
-    ).reshape(seq_count, count, width)
+    d_value = jnp.roll(d_value.astype(jnp.bfloat16), place_index * local_rows, axis=1)
+    d_key = jnp.roll(d_key.astype(jnp.bfloat16), place_index * local_rows, axis=1)
+    key_heads = after_exchange(key_heads)
+    d_query = jnp.einsum("sqhk,skhd->sqhd", d_scores, key_heads, preferred_element_type=jnp.float32)
     d_key_all = d_key
     d_value_all = d_value
     result_state = (d_query, d_key_all, d_value_all)
@@ -289,11 +328,9 @@
     d_inputs, grad_gain_one, grad_shift_one = norm_pull_one(d_normed_one)
     grad_tokens = (d_middle + d_inputs).astype(jnp.bfloat16).reshape(tokens.shape)
     shaped_qkv = jnp.concatenate(
-        [reduce_matrix(grad_parts[number], number == 2) for number in range(3)], axis=1
-    )
-    shaped_proj = reduce_matrix(grad_proj, True)
-    shaped_up = reduce_matrix(grad_up, True)
-    shaped_down = reduce_matrix(grad_down, False)
+        [finish(reduce_steps(grad_parts[number], number == 2)) for number in range(3)], axis=1
+    )
+    shaped_down, shaped_up, shaped_proj = [finish(steps) for steps in running]
     early = reduce_vectors(
         (grad_pbias, grad_gain_two, grad_shift_two, grad_ubias, grad_dbias)
     )

time: 1020 us -> 978 us (0.959)
  waiting for transfers between devices: 519 us -> 425 us
  other arithmetic: 79.6 us -> 101 us
  matrix products: 273 us -> 294 us
  starting transfers between devices: 51 us -> 67.9 us
  local copies, waits for them, and re-layouts: 74.9 us -> 63.5 us
    ppermute x0 -> x12, waiting for transfers between devices: none -> 114 us  [the longest x6 73.2 us: ring_gather(): lax.ppermute(upper[-1], axis, [(i + 1, i) for i in range(count - step)])]
    all_gather x2 -> x0, waiting for transfers between devices: 111 us -> none  [the longest x1 77.2 us: per_device(): piece_keys = lax.all_gather(keys, 'ctx', axis=1, tiled=True)]
    all_gather x1, waiting for transfers between devices: 55.6 us -> 0.01 us  [per_device(): up_full = lax.all_gather(up_weight, 'dp', axis=0, tiled=True)]
    all_gather x1, waiting for transfers between devices: 47.9 us -> 0.01 us  [per_device(): down_full = lax.all_gather(down_weight, 'dp', axis=0, tiled=True)]
    dot_general x1 -> x2, matrix products: 28.5 us -> 55.4 us  [per_device(): jnp.einsum('sqhd,skhd->sqhk', query_heads, key_heads, preferred_element_t...]
    concatenate x1 -> x5, other arithmetic: 1.34 us -> 21.5 us  [the longest x1 7.13 us: per_device(): jnp.roll(d_key.astype(jnp.bfloat16), place_index * local_rows, axis=1)]
    ppermute x0 -> x12, starting transfers between devices: none -> 19.6 us  [the longest x6 11.7 us: ring_gather(): lax.ppermute(lower[-1], axis, [(i, i + 1) for i in range(step - 1, count...]
    convert_element_type x28 -> x27, other arithmetic: 37.4 us -> 31.5 us  [the longest x24 27.9 us: halve_steps(): parts = total.astype(wire).reshape((-1,) + rest)]
  transfers between devices with their start and end apart: 63 -> 73, of which waited for: 45 -> 41; matrix products, arithmetic and copies ran while one was open for 34% -> 42% of each run, Pallas kernels for 0% -> 0%
where the time goes in v2:
time: 978 us; the launch traced here: 968 us
  waiting for transfers between devices  425 us (43%)
  matrix products  294 us (30%)
  other arithmetic  101 us (10%)
  starting transfers between devices  67.9 us (7%)
  local copies, waits for them, and re-layouts  63.5 us (6%)
  between operations  16.4 us (2%)
    ppermute x55, waiting for transfers between devices, swap(): return lax.ppermute(values, axis, [(i, i ^ 1 << bit) for i in range(count)])  268 us
    ppermute x6, waiting for transfers between devices, ring_gather(): lax.ppermute(upper[-1], axis, [(i + 1, i) for i in range(count - step)])  73.2 us
    dot_general x2, matrix products, per_device(): jnp.einsum('sqhd,skhd->sqhk', query_heads, key_heads, preferred_element_t...  55.4 us
    ppermute x55, starting transfers between devices, swap(): return lax.ppermute(values, axis, [(i, i ^ 1 << bit) for i in range(count)])  48.1 us
    dot_general x1, matrix products, per_device(): jnp.einsum('sqhd,skhd->sqhk', d_heads, value_heads, preferred_element_typ...  44.3 us
    all_gather x1, waiting for transfers between devices, per_device(): qkv_full = lax.all_gather(qkv_weight, 'dp', axis=0, tiled=True)  41.6 us
    ppermute x6, waiting for transfers between devices, ring_gather(): lax.ppermute(lower[-1], axis, [(i, i + 1) for i in range(step - 1, count...  40.5 us
    dot_general x1, matrix products, per_device(): jnp.einsum('sqhk,skhd->sqhd', weights.astype(jnp.bfloat16), value_heads,...  28.8 us
  transfers between devices with their start and end apart: 73, of which 41 were waited for; matrix products, arithmetic and copies ran while one was open for 42% of the time, Pallas kernels for 0%

profile of v2, /device:TPU:0, one launch (start us, length us, event | category | flops | bytes accessed | tf_op | source)
XLA Modules:
  0.0 968.4 jit_solution(4328415982978326300)
XLA Ops:
  11.3 2.9 collective-permute-start.1
  20.7 41.6 %all-gather.5.cloned.1.call-done = bf16[1088,3264]{1,0:T(8,128)(2,1)} async-done(((bf16[136,3264]{1,0:T(8,128)(2,1)}), bf16[1088,3264]{1,0:T(8,128)(2,1)}) %all-gather.5.cloned.1.call-update) | async-done | bytes 7102480 | tf_op jit(solution)/shard_map/all_gather | solution.py:198
  62.3 6.9 fusion.163
  72.0 3.4 collective-permute-start.4
  76.8 22.8 %collective-permute-done.4 = bf16[1,512,1088]{1,2,0:T(8,128)(2,1)S(1)} collective-permute-done((bf16[1,512,1088]{1,2,0:T(8,128)(2,1)S(1)}, bf16[1,512,1088]{1,2,0:T(8,128)(2,1)S(1)}, u32[]{:S(2)}, u32[]{:S(2)}) %collective-permute-start.4) | collective-permute-done | bytes 1114144 | tf_op jit(solution)/shard_map/ppermute | solution.py:83
  106.4 3.7 fusion.93
  110.1 22.6 %collective-permute-done.7 = bf16[1,512,1088]{1,2,0:T(8,128)(2,1)} collective-permute-done((bf16[1,512,1088]{1,2,0:T(8,128)(2,1)}, bf16[1,512,1088]{1,2,0:T(8,128)(2,1)}, u32[]{:S(2)}, u32[]{:S(2)}) %collective-permute-start.7) | collective-permute-done | bytes 1114144 | tf_op jit(solution)/shard_map/ppermute | solution.py:84
  137.0 22.9 %collective-permute-done.8 = bf16[1,512,1088]{1,2,0:T(8,128)(2,1)S(1)} collective-permute-done((bf16[1,512,1088]{1,2,0:T(8,128)(2,1)}, bf16[1,512,1088]{1,2,0:T(8,128)(2,1)S(1)}, u32[]{:S(2)}, u32[]{:S(2)}) %collective-permute-start.8) | collective-permute-done | bytes 1114144 | tf_op jit(solution)/shard_map/ppermute | solution.py:84
  168.4 17.7 %collective-permute-done.10 = bf16[1,512,1088]{1,2,0:T(8,128)(2,1)} collective-permute-done((bf16[1,512,1088]{1,2,0:T(8,128)(2,1)}, bf16[1,512,1088]{1,2,0:T(8,128)(2,1)}, u32[]{:S(2)}, u32[]{:S(2)}) %collective-permute-start.10) | collective-permute-done | bytes 1114144 | tf_op jit(solution)/shard_map/ppermute | solution.py:83
  187.7 28.2 %fusion.4 = (f32[512,17]{0,1:T(8,128)S(1)}, f32[17,2048,512]{2,1,0:T(8,128)}) fusion(pred[512,2048]{0,1:T(8,128)(4,1)S(1)} %broadcast_compare_fusion, bf16[2048,17,64]{0,2,1:T(8,128)(2,1)} %bitcast.486, bf16[512,17,64]{0,2,1:T(8,128)(2,1)S(1)} %bitcast.490), kind=kOutput, calls=%fused_computation.8 | convolution fusion | flops 2317344256 | bytes 77957120 | tf_op jit(solution)/shard_map/sqhd,skhd->sqhk/dot_general | solution.py:227
  218.9 22.7 %fusion.6 = f32[512,17]{0,1:T(8,128)S(1)} fusion(f32[17,2048,512]{2,1,0:T(8,128)} %get-tuple-element.93, f32[512,17]{0,1:T(8,128)S(1)} %broadcast_maximum_fusion, pred[512,2048]{0,1:T(8,128)(4,1)S(1)} %broadcast_compare_fusion), kind=kLoop, calls=%fused_computation.10 | loop fusion | flops 71294464 | bytes 72421376 | tf_op jit(solution)/shard_map/reduce_sum | solution.py:233
  246.9 23.3 %collective-permute-done.14 = bf16[1,512,1088]{1,2,0:T(8,128)(2,1)S(1)} collective-permute-done((bf16[1,512,1088]{1,2,0:T(8,128)(2,1)S(1)}, bf16[1,512,1088]{1,2,0:T(8,128)(2,1)S(1)}, u32[]{:S(2)}, u32[]{:S(2)}) %collective-permute-start.14) | collective-permute-done | bytes 1114144 | tf_op jit(solution)/shard_map/ppermute | solution.py:84
  270.3 3.5 pad_maximum_fusion.1
  273.8 28.8 %fusion.161 = (bf16[1,512,17,64]{1,3,2,0:T(8,128)(2,1)S(1)}, f32[1,512,17,64]{1,3,2,0:T(8,128)}) fusion(f32[512,17]{0,1:T(8,128)S(1)} %fusion.6, f32[17,2048,512]{2,1,0:T(8,128)} %get-tuple-element.93, f32[512,17]{0,1:T(8,128)S(1)} %broadcast_maximum_fusion, pred[512,2048]{0,1:T(8,128)(4,1)S(1)} %broadcast_compare_fusion, ...), kind=kOutput, calls=%fused_computation.344 | convolution fusion | flops 2354118656 | bytes 80220160 | tf_op jit(solution)/shard_map/sqhk,skhd->sqhd/dot_general | solution.py:235
  302.6 3.6 fusion.162
  307.1 11.7 %fusion.34 = (bf16[4352,512]{0,1:T(8,128)(2,1)}, f32[512,4352]{1,0:T(8,128)}) fusion(f32[4352]{0:T(1024)S(1)} %add.518, bf16[1088,4352]{1,0:T(8,128)(2,1)S(1)} %copy-done.51, f32[512,1088]{0,1:T(8,128)S(1)} %get-tuple-element.97, f32[1088]{0:T(1024)S(1)} %add.515, f32[1088]{0:T(1024)S(1)} %mul.246, f32[512]{0:T(512)S(1)} %fusion.146, ...), kind=kOutput, calls=%fused_computation.43 | convolution fusion | flops 4873682944 | bytes 25097728 | tf_op jit(solution)/shard_map/dot_general | solution.py:250
  318.7 14.4 %convert_reduce_fusion = (f32[4352]{0:T(1024)}, bf16[512,4352]{1,0:T(8,128)(2,1)S(1)}) fusion(f32[512,4352]{1,0:T(8,128)} %get-tuple-element.99, bf16[4352,1088]{1,0:T(8,128)(2,1)} %all-gather.11.cloned.1.call-done, bf16[1,512,1088]{1,2,0:T(8,128)(2,1)S(1)} %copy-done.22), kind=kOutput, calls=%fused_computation.48 | convolution fusion | flops 4897632256 | bytes 23970816 | tf_op jit(solution)/shard_map/rd,fd->rf/dot_general | solution.py:259
  333.1 9.2 multiply_reduce_fusion
  347.3 9.3 fusion.155
  356.6 6.7 copy.118
  363.3 6.7 fusion.36
  372.4 10.0 %fusion.99 = f32[4,2,544,1088]{3,2,1,0:T(8,128)} fusion(bf16[4,2,544,512]{3,2,1,0:T(8,128)(2,1)S(1)} %bitcast.521, bf16[1,512,1088]{1,2,0:T(8,128)(2,1)S(1)} %copy-done.22), kind=kOutput, calls=%fused_computation.153 | convolution fusion | flops 4848615424 | bytes 24510464 | tf_op jit(solution)/shard_map/rf,rd->fd/dot_general | solution.py:257
  382.4 4.7 collective-permute-done.22
  388.8 6.6 dynamic-slice_convert_fusion
  396.9 27.2 %fusion.165 = f32[17,2048,512]{2,1,0:T(8,128)} fusion(bf16[2048,17,64]{0,2,1:T(8,128)(2,1)} %bitcast.487, bf16[512,17,64]{0,2,1:T(8,128)(2,1)S(1)} %bitcast.491), kind=kOutput, calls=%fused_computation.348 | convolution fusion | flops 2281701376 | bytes 76873728 | tf_op jit(solution)/shard_map/sqhd,skhd->sqhk/dot_general | solution.py:284
  425.9 5.6 collective-permute-done.51
  432.1 5.3 collective-permute-done.52
  437.6 6.1 fusion.19
  447.6 8.7 add_convert_fusion
  456.3 3.4 dynamic-slice_bitcast_fusion
  459.6 44.3 %fusion.12 = bf16[512,17,2048]{0,2,1:T(8,128)(2,1)} fusion(f32[17,2048,512]{2,1,0:T(8,128)} %fusion.165, f32[512,17]{0,1:T(8,128)S(1)} %multiply_reduce_fusion.1, f32[512,17]{0,1:T(8,128)S(1)} %copy-done.40, pred[512,2048]{0,1:T(8,128)(4,1)S(1)} %broadcast_compare_fusion, bf16[2048,17,64]{0,2,1:T(8,128)(2,1)} %bitcast.518, ...), kind=kOutput, calls=%fused_computation.15 | convolution fusion | flops 2370830336 | bytes 113643520 | tf_op jit(solution)/shard_map/sqhd,skhd->sqhk/dot_general | solution.py:289
  503.9 18.3 %convolution_convert_fusion = bf16[17,64,2048]{2,1,0:T(8,128)(2,1)} fusion(bf16[512,17,64]{0,2,1:T(8,128)(2,1)S(1)} %bitcast.492, bf16[512,17,2048]{0,2,1:T(8,128)(2,1)} %fusion.12), kind=kOutput, calls=%fused_computation.65 | convolution fusion | flops 2283929600 | bytes 41222144 | tf_op jit(solution)/shard_map/sqhk,sqhd->skhd/dot_general | solution.py:297
  522.2 7.1 fusion.39
  530.0 16.0 %fusion.62 = bf16[1,512,1088]{1,2,0:T(8,128)(2,1)} fusion(f32[512,1088]{0,1:T(8,128)} %copy-done.14, bf16[4352,1088]{1,0:T(8,128)(2,1)} %all-gather.11.cloned.1.call-done, f32[512,4352]{1,0:T(8,128)} %get-tuple-element.99, f32[1088]{0:T(1024)S(1)} %copy-done.48), kind=kOutput, calls=%fused_computation.89 | convolution fusion | flops 4870340608 | bytes 21729536 | tf_op jit(solution)/shard_map/dot_general | solution.py:252
  550.5 3.1 fusion.37
  556.3 50.2 %collective-permute-done.16 = bf16[2,1,544,1088]{3,2,0,1:T(8,128)(2,1)} collective-permute-done((bf16[2,1,544,1088]{3,2,0,1:T(8,128)(2,1)}, bf16[2,1,544,1088]{3,2,0,1:T(8,128)(2,1)}, u32[]{:S(2)}, u32[]{:S(2)}) %collective-permute-start.16) | collective-permute-done | bytes 2367520 | tf_op jit(solution)/shard_map/ppermute | solution.py:39
  612.3 27.3 %fusion.44 = bf16[17,64,2048]{2,1,0:T(8,128)(2,1)} fusion(f32[17,2048,512]{2,1,0:T(8,128)} %fusion.165, f32[512,17]{0,1:T(8,128)S(1)} %copy-done.41, pred[512,2048]{0,1:T(8,128)(4,1)S(1)} %broadcast_compare_fusion, bf16[1,512,17,64]{1,3,2,0:T(8,128)(2,1)S(1)} %bitcast.528), kind=kOutput, calls=%fused_computation.64 | convolution fusion | flops 2337406976 | bytes 77957120 | tf_op jit(solution)/shard_map/sqhk,sqhd->skhd/dot_general | solution.py:294
  639.6 7.1 fusion.38
  649.6 2.8 reshape_reshape_squeeze_reshape.19
  659.9 18.8 %convert_reduce_fusion.5 = (f32[17,64]{1,0:T(8,128)S(1)}, bf16[17,64,512]{2,1,0:T(8,128)(2,1)S(1)}) fusion(bf16[512,17,2048]{0,2,1:T(8,128)(2,1)} %fusion.12, bf16[1,2048,17,64]{1,3,2,0:T(8,128)(2,1)} %bitcast.488), kind=kOutput, calls=%fused_computation.120 | convolution fusion | flops 2283928576 | bytes 41226496 | tf_op jit(solution)/shard_map/sqhk,skhd->sqhd/dot_general | solution.py:303
  681.4 16.8 %collective-permute-done.59 = bf16[2,1,34,4352]{3,0,2,1:T(2,128)(2,1)} collective-permute-done((bf16[2,1,34,4352]{3,0,2,1:T(2,128)(2,1)}, bf16[2,1,34,4352]{3,0,2,1:T(2,128)(2,1)}, u32[]{:S(2)}, u32[]{:S(2)}) %collective-permute-start.59) | collective-permute-done | bytes 591904 | tf_op jit(solution)/shard_map/ppermute | solution.py:39
  700.2 41.6 %collective-permute-done.63 = bf16[2,1,136,1088]{3,2,1,0:T(8,128)(2,1)S(1)} collective-permute-done((bf16[2,1,136,1088]{3,2,1,0:T(8,128)(2,1)S(1)}, bf16[2,1,136,1088]{3,2,1,0:T(8,128)(2,1)S(1)}, u32[]{:S(2)}, u32[]{:S(2)}) %collective-permute-start.63) | collective-permute-done | bytes 591904 | tf_op jit(solution)/shard_map/ppermute | solution.py:39
  742.3 3.0 collective-permute-start.61
  745.2 33.3 %collective-permute-done.64 = bf16[1,1,136,1088]{3,2,1,0:T(8,128)(2,1)S(1)} collective-permute-done((bf16[1,1,136,1088]{3,2,1,0:T(8,128)(2,1)S(1)}, bf16[1,1,136,1088]{3,2,1,0:T(8,128)(2,1)S(1)}, u32[]{:S(2)}, u32[]{:S(2)}) %collective-permute-start.64) | collective-permute-done | bytes 295968 | tf_op jit(solution)/shard_map/ppermute | solution.py:39
  778.7 10.7 %collective-permute-done.61 = bf16[1,34,4352]{2,1,0:T(8,128)(2,1)S(1)} collective-permute-done((bf16[1,34,4352]{2,1,0:T(8,128)(2,1)S(1)}, bf16[1,34,4352]{2,1,0:T(8,128)(2,1)S(1)}, u32[]{:S(2)}, u32[]{:S(2)}) %collective-permute-start.61) | collective-permute-done | bytes 295968 | tf_op jit(solution)/shard_map/ppermute | solution.py:39
  794.4 8.5 collective-permute-done.30
  804.2 2.7 collective-permute-done.62
  808.9 11.3 %collective-permute-done.66 = bf16[2,136,1088]{2,1,0:T(8,128)(2,1)S(1)} collective-permute-done((bf16[2,136,1088]{2,1,0:T(8,128)(2,1)S(1)}, bf16[2,136,1088]{2,1,0:T(8,128)(2,1)S(1)}, u32[]{:S(2)}, u32[]{:S(2)}) %collective-permute-start.66) | collective-permute-done | bytes 591904 | tf_op jit(solution)/shard_map/ppermute | solution.py:39
  820.6 2.9 fusion.97
  824.0 6.9 collective-permute-done.32
  839.8 8.7 collective-permute-done.37
  851.7 6.4 collective-permute-done.38
  859.8 4.2 collective-permute-done.39
  864.0 3.2 collective-permute-start.40
  868.2 4.2 collective-permute-done.40
  873.1 9.1 fusion.70
  883.7 3.3 fusion.68
  889.1 4.6 convert_reduce_fusion.1
  898.2 3.5 fusion.95
  916.7 9.3 collective-permute-done.44
  935.7 4.4 collective-permute-done.46
  942.3 4.4 collective-permute-done.47
  947.0 5.9 collective-permute-done.48
  953.3 5.2 collective-permute-done.49
  (446 shorter events, 152.5 us)
Async XLA Ops:
  7.3 55.0 %all-gather.5.cloned.1.call-start = ((), (), s32[]{:S(2)}) async-start(), calls=%async_computation.2 | async-start | bytes 8146944 | tf_op jit(solution)/shard_map/all_gather | solution.py:198
  8.0 160.4 %all-gather.9.cloned.1.call-start = ((), (), s32[]{:S(2)}) async-start(), calls=%async_computation.4 | async-start | bytes 2820096 | tf_op jit(solution)/shard_map/all_gather | solution.py:199
  8.8 265.0 %all-gather.7.cloned.1.call-start = ((), (), s32[]{:S(2)}) async-start(), calls=%async_computation.3 | async-start | bytes 10653696 | tf_op jit(solution)/shard_map/all_gather | solution.py:200
  9.5 293.1 %all-gather.11.cloned.1.call-start = ((), (), s32[]{:S(2)}) async-start(), calls=%async_computation.5 | async-start | bytes 11280384 | tf_op jit(solution)/shard_map/all_gather | solution.py:201
  11.3 4.6 collective-permute-start.1
  72.0 27.6 %collective-permute-start.4 = (bf16[1,512,1088]{1,2,0:T(8,128)(2,1)S(1)}, bf16[1,512,1088]{1,2,0:T(8,128)(2,1)S(1)}, u32[]{:S(2)}, u32[]{:S(2)}) collective-permute-start(bf16[1,512,1088]{1,2,0:T(8,128)(2,1)S(1)} %fusion.94), channel_id=1, source_target_pairs={{0,1},{1,2},{2,3},{4,5},{5,6},{6,7},{8,9},{9,10},{10,11},{12,13},{... | collective-permute-start | bytes 3342344 | tf_op jit(solution)/shard_map/ppermute | solution.py:83
  75.5 28.4 %collective-permute-start.3 = (bf16[1,512,1088]{1,2,0:T(8,128)(2,1)S(1)}, bf16[1,512,1088]{1,2,0:T(8,128)(2,1)}, u32[]{:S(2)}, u32[]{:S(2)}) collective-permute-start(bf16[1,512,1088]{1,2,0:T(8,128)(2,1)S(1)} %fusion.94), channel_id=1, source_target_pairs={{1,0},{2,1},{3,2},{5,4},{6,5},{7,6},{9,8},{10,9},{11,10},{13,12},{... | collective-permute-start | bytes 3342344 | tf_op jit(solution)/shard_map/ppermute | solution.py:84
  99.7 6.0 collective-permute-start.5
  104.0 28.8 %collective-permute-start.7 = (bf16[1,512,1088]{1,2,0:T(8,128)(2,1)}, bf16[1,512,1088]{1,2,0:T(8,128)(2,1)}, u32[]{:S(2)}, u32[]{:S(2)}) collective-permute-start(bf16[1,512,1088]{1,2,0:T(8,128)(2,1)} %collective-permute-done.3), channel_id=1, source_target_pairs={{1,0},{2,1},{5,4},{6,5},{9,8},{10,9},{13,12},{14,13},{17,16},{18,1... | collective-permute-start | bytes 3342344 | tf_op jit(solution)/shard_map/ppermute | solution.py:84
  105.3 715.4 %reduce-scatter.3.cloned.1.call-start = ((), (), s32[]{:S(2)}) async-start(), calls=%async_computation.6 | async-start | bytes 5570560 | tf_op jit(solution)/shard_map/reduce_scatter | solution.py:309
  105.7 29.8 %collective-permute-start.6 = (bf16[1,512,1088]{1,2,0:T(8,128)(2,1)}, bf16[1,512,1088]{1,2,0:T(8,128)(2,1)S(1)}, u32[]{:S(2)}, u32[]{:S(2)}) collective-permute-start(bf16[1,512,1088]{1,2,0:T(8,128)(2,1)} %collective-permute-done.5), channel_id=1, source_target_pairs={{2,3},{6,7},{10,11},{14,15},{18,19},{22,23},{26,27},{30,31}} | collective-permute-start | bytes 3342344 | tf_op jit(solution)/shard_map/ppermute | solution.py:83
  132.7 27.2 %collective-permute-start.8 = (bf16[1,512,1088]{1,2,0:T(8,128)(2,1)}, bf16[1,512,1088]{1,2,0:T(8,128)(2,1)S(1)}, u32[]{:S(2)}, u32[]{:S(2)}) collective-permute-start(bf16[1,512,1088]{1,2,0:T(8,128)(2,1)} %collective-permute-done.7), channel_id=1, source_target_pairs={{1,0},{5,4},{9,8},{13,12},{17,16},{21,20},{25,24},{29,28}} | collective-permute-start | bytes 3342344 | tf_op jit(solution)/shard_map/ppermute | solution.py:84
  162.5 23.6 %collective-permute-start.10 = (bf16[1,512,1088]{1,2,0:T(8,128)(2,1)}, bf16[1,512,1088]{1,2,0:T(8,128)(2,1)}, u32[]{:S(2)}, u32[]{:S(2)}) collective-permute-start(bf16[1,512,1088]{1,2,0:T(8,128)(2,1)} %get-tuple-element.24), channel_id=1, source_target_pairs={{0,1},{1,2},{2,3},{4,5},{5,6},{6,7},{8,9},{9,10},{10,11},{12,13},{... | collective-permute-start | bytes 3342344 | tf_op jit(solution)/shard_map/ppermute | solution.py:83
  167.1 48.8 %collective-permute-start.9 = (bf16[1,512,1088]{1,2,0:T(8,128)(2,1)}, bf16[1,512,1088]{1,2,0:T(8,128)(2,1)}, u32[]{:S(2)}, u32[]{:S(2)}) collective-permute-start(bf16[1,512,1088]{1,2,0:T(8,128)(2,1)} %get-tuple-element.24), channel_id=1, source_target_pairs={{1,0},{2,1},{3,2},{5,4},{6,5},{7,6},{9,8},{10,9},{11,10},{13,12},{... | collective-permute-start | bytes 3342344 | tf_op jit(solution)/shard_map/ppermute | solution.py:84
  186.1 31.1 %collective-permute-start.11 = (bf16[1,512,1088]{1,2,0:T(8,128)(2,1)}, bf16[1,512,1088]{1,2,0:T(8,128)(2,1)}, u32[]{:S(2)}, u32[]{:S(2)}) collective-permute-start(bf16[1,512,1088]{1,2,0:T(8,128)(2,1)} %collective-permute-done.10), channel_id=1, source_target_pairs={{1,2},{2,3},{5,6},{6,7},{9,10},{10,11},{13,14},{14,15},{17,18},{18... | collective-permute-start | bytes 3342344 | tf_op jit(solution)/shard_map/ppermute | solution.py:83
  215.9 28.0 %collective-permute-start.13 = (bf16[1,512,1088]{1,2,0:T(8,128)(2,1)}, bf16[1,512,1088]{1,2,0:T(8,128)(2,1)S(1)}, u32[]{:S(2)}, u32[]{:S(2)}) collective-permute-start(bf16[1,512,1088]{1,2,0:T(8,128)(2,1)} %collective-permute-done.9), channel_id=1, source_target_pairs={{1,0},{2,1},{5,4},{6,5},{9,8},{10,9},{13,12},{14,13},{17,16},{18,1... | collective-permute-start | bytes 3342344 | tf_op jit(solution)/shard_map/ppermute | solution.py:84
  217.2 28.3 %collective-permute-start.12 = (bf16[1,512,1088]{1,2,0:T(8,128)(2,1)}, bf16[1,512,1088]{1,2,0:T(8,128)(2,1)}, u32[]{:S(2)}, u32[]{:S(2)}) collective-permute-start(bf16[1,512,1088]{1,2,0:T(8,128)(2,1)} %collective-permute-done.11), channel_id=1, source_target_pairs={{2,3},{6,7},{10,11},{14,15},{18,19},{22,23},{26,27},{30,31}} | collective-permute-start | bytes 3342344 | tf_op jit(solution)/shard_map/ppermute | solution.py:83
  243.9 26.3 %collective-permute-start.14 = (bf16[1,512,1088]{1,2,0:T(8,128)(2,1)S(1)}, bf16[1,512,1088]{1,2,0:T(8,128)(2,1)S(1)}, u32[]{:S(2)}, u32[]{:S(2)}) collective-permute-start(bf16[1,512,1088]{1,2,0:T(8,128)(2,1)S(1)} %collective-permute-done.13), channel_id=1, source_target_pairs={{1,0},{5,4},{9,8},{13,12},{17,16},{21,20},{25,24},{29,28}} | collective-permute-start | bytes 3342344 | tf_op jit(solution)/shard_map/ppermute | solution.py:84
  347.3 23.3 %collective-permute-start.21 = (bf16[4,1,136,1088]{3,2,0,1:T(8,128)(2,1)}, bf16[4,1,136,1088]{3,2,0,1:T(8,128)(2,1)S(1)}, u32[]{:S(2)}, u32[]{:S(2)}) collective-permute-start(bf16[4,1,136,1088]{3,2,0,1:T(8,128)(2,1)} %fusion.86), channel_id=1, source_target_pairs={{0,4},{4,0},{8,12},{12,8},{16,20},{20,16},{24,28},{28,24},{1,5},{5... | collective-permute-start | bytes 3551240 | tf_op jit(solution)/shard_map/ppermute | solution.py:39
  370.1 67.5 %collective-permute-start.18 = (bf16[4,1,136,4352]{3,2,0,1:T(8,128)(2,1)}, bf16[4,1,136,4352]{3,2,0,1:T(8,128)(2,1)}, u32[]{:S(2)}, u32[]{:S(2)}) collective-permute-start(bf16[4,1,136,4352]{3,2,0,1:T(8,128)(2,1)} %fusion.36), channel_id=1, source_target_pairs={{0,4},{4,0},{8,12},{12,8},{16,20},{20,16},{24,28},{28,24},{1,5},{5... | collective-permute-start | bytes 14204936 | tf_op jit(solution)/shard_map/ppermute | solution.py:39
  370.9 16.1 %collective-permute-start.22 = (bf16[1,2,136,1088]{3,2,1,0:T(8,128)(2,1)S(1)}, bf16[1,2,136,1088]{3,2,1,0:T(8,128)(2,1)S(1)}, u32[]{:S(2)}, u32[]{:S(2)}) collective-permute-start(bf16[1,2,136,1088]{3,2,1,0:T(8,128)(2,1)S(1)} %dynamic-slice_bitcast_fusion.5), channel_id=1, source_target_pairs={{0,16},{4,20},{8,24},{12,28},{16,0},{20,4},{24,8},{28,12},{1,17},{... | collective-permute-start | bytes 1775624 | tf_op jit(solution)/shard_map/ppermute | solution.py:39
  387.3 8.5 collective-permute-start.23
  395.4 52.2 %collective-permute-start.15 = (bf16[4,1,544,1088]{3,2,1,0:T(8,128)(2,1)}, bf16[4,1,544,1088]{3,2,1,0:T(8,128)(2,1)}, u32[]{:S(2)}, u32[]{:S(2)}) collective-permute-start(bf16[4,1,544,1088]{3,2,1,0:T(8,128)(2,1)} %dynamic-slice_convert_fusion), channel_id=1, source_target_pairs={{0,4},{4,0},{8,12},{12,8},{16,20},{20,16},{24,28},{28,24},{1,5},{5... | collective-permute-start | bytes 14204936 | tf_op jit(solution)/shard_map/ppermute | solution.py:39
  396.0 28.1 %collective-permute-start.50 = (bf16[2,1,34,1088]{3,2,0,1:T(8,128)(2,1)S(1)}, bf16[2,1,34,1088]{3,2,0,1:T(8,128)(2,1)S(1)}, u32[]{:S(2)}, u32[]{:S(2)}) collective-permute-start(bf16[2,1,34,1088]{3,2,0,1:T(8,128)(2,1)S(1)} %dynamic-slice_bitcast_fusion.10), channel_id=1, source_target_pairs={{0,1},{1,0},{2,3},{3,2},{4,5},{5,4},{6,7},{7,6},{8,9},{9,8},{10,11... | collective-permute-start | bytes 443912 | tf_op jit(solution)/shard_map/ppermute | solution.py:39
  424.2 7.3 collective-permute-start.51
  431.6 5.8 collective-permute-start.52
  437.5 111.9 %collective-permute-start.53 = (bf16[2,34,1088]{2,1,0:T(8,128)(2,1)S(1)}, bf16[2,34,1088]{2,1,0:T(8,128)(2,1)S(1)}, u32[]{:S(2)}, u32[]{:S(2)}) collective-permute-start(bf16[2,34,1088]{2,1,0:T(8,128)(2,1)S(1)} %maximum_bitcast_fusion.5), channel_id=1, source_target_pairs={{0,1},{1,0},{2,3},{3,2},{4,5},{5,4},{6,7},{7,6},{8,9},{9,8},{10,11... | collective-permute-start | bytes 443912 | tf_op jit(solution)/shard_map/ppermute | solution.py:39
  446.5 104.0 %collective-permute-start.19 = (bf16[1,2,136,4352]{3,2,1,0:T(8,128)(2,1)}, bf16[1,2,136,4352]{3,2,1,0:T(8,128)(2,1)}, u32[]{:S(2)}, u32[]{:S(2)}) collective-permute-start(bf16[1,2,136,4352]{3,2,1,0:T(8,128)(2,1)} %dynamic-slice_bitcast_fusion.1), channel_id=1, source_target_pairs={{0,16},{4,20},{8,24},{12,28},{16,0},{20,4},{24,8},{28,12},{1,17},{... | collective-permute-start | bytes 7102472 | tf_op jit(solution)/shard_map/ppermute | solution.py:39
  529.4 343.7 %reduce-scatter.5.cloned.1.call-start = ((), (), s32[]{:S(2)}) async-start(), calls=%async_computation.7 | async-start | bytes 5570560 | tf_op jit(solution)/shard_map/reduce_scatter | solution.py:312
  548.8 57.7 %collective-permute-start.16 = (bf16[2,1,544,1088]{3,2,0,1:T(8,128)(2,1)}, bf16[2,1,544,1088]{3,2,0,1:T(8,128)(2,1)}, u32[]{:S(2)}, u32[]{:S(2)}) collective-permute-start(bf16[2,1,544,1088]{3,2,0,1:T(8,128)(2,1)} %dynamic-slice_bitcast_fusion), channel_id=1, source_target_pairs={{0,8},{4,12},{8,0},{12,4},{16,24},{20,28},{24,16},{28,20},{1,9},{5... | collective-permute-start | bytes 7102472 | tf_op jit(solution)/shard_map/ppermute | solution.py:39
  554.8 91.9 %collective-permute-start.20 = (bf16[1,1,136,4352]{3,2,1,0:T(8,128)(2,1)}, bf16[1,1,136,4352]{3,2,1,0:T(8,128)(2,1)S(1)}, u32[]{:S(2)}, u32[]{:S(2)}) collective-permute-start(bf16[1,1,136,4352]{3,2,1,0:T(8,128)(2,1)} %constant_dynamic-slice_fusion.23), channel_id=1, source_target_pairs={{0,8},{4,12},{8,0},{12,4},{16,24},{20,28},{24,16},{28,20},{1,9},{5... | collective-permute-start | bytes 3551240 | tf_op jit(solution)/shard_map/ppermute | solution.py:39
  611.5 45.7 %collective-permute-start.17 = (bf16[1,1,544,1088]{3,2,0,1:T(8,128)(2,1)}, bf16[1,1,544,1088]{3,2,0,1:T(8,128)(2,1)}, u32[]{:S(2)}, u32[]{:S(2)}) collective-permute-start(bf16[1,1,544,1088]{3,2,0,1:T(8,128)(2,1)} %constant_dynamic-slice_fusion.24), channel_id=1, source_target_pairs={{0,16},{4,20},{8,24},{12,28},{16,0},{20,4},{24,8},{28,12},{1,17},{... | collective-permute-start | bytes 3551240 | tf_op jit(solution)/shard_map/ppermute | solution.py:39
  655.1 43.1 %collective-permute-start.59 = (bf16[2,1,34,4352]{3,0,2,1:T(2,128)(2,1)}, bf16[2,1,34,4352]{3,0,2,1:T(2,128)(2,1)}, u32[]{:S(2)}, u32[]{:S(2)}) collective-permute-start(bf16[2,1,34,4352]{3,0,2,1:T(2,128)(2,1)} %bitcast.485), channel_id=1, source_target_pairs={{0,1},{1,0},{2,3},{3,2},{4,5},{5,4},{6,7},{7,6},{8,9},{9,8},{10,11... | collective-permute-start | bytes 1775624 | tf_op jit(solution)/shard_map/ppermute | solution.py:39
  658.9 83.0 %collective-permute-start.63 = (bf16[2,1,136,1088]{3,2,1,0:T(8,128)(2,1)S(1)}, bf16[2,1,136,1088]{3,2,1,0:T(8,128)(2,1)S(1)}, u32[]{:S(2)}, u32[]{:S(2)}) collective-permute-start(bf16[2,1,136,1088]{3,2,1,0:T(8,128)(2,1)S(1)} %dynamic-slice_bitcast_fusion.6), channel_id=1, source_target_pairs={{0,1},{1,0},{2,3},{3,2},{4,5},{5,4},{6,7},{7,6},{8,9},{9,8},{10,11... | collective-permute-start | bytes 1775624 | tf_op jit(solution)/shard_map/ppermute | solution.py:39
  681.3 108.8 %collective-permute-start.29 = (bf16[4,1,136,1088]{3,2,1,0:T(8,128)(2,1)S(1)}, bf16[4,1,136,1088]{3,2,1,0:T(8,128)(2,1)S(1)}, u32[]{:S(2)}, u32[]{:S(2)}) collective-permute-start(bf16[4,1,136,1088]{3,2,1,0:T(8,128)(2,1)S(1)} %dynamic-slice_convert_fusion.4), channel_id=1, source_target_pairs={{0,4},{4,0},{8,12},{12,8},{16,20},{20,16},{24,28},{28,24},{1,5},{5... | collective-permute-start | bytes 3551240 | tf_op jit(solution)/shard_map/ppermute | solution.py:39
  699.5 42.7 %collective-permute-start.60 = (bf16[1,1,34,4352]{3,2,0,1:T(8,128)(2,1)S(1)}, bf16[1,1,34,4352]{3,2,0,1:T(8,128)(2,1)S(1)}, u32[]{:S(2)}, u32[]{:S(2)}) collective-permute-start(bf16[1,1,34,4352]{3,2,0,1:T(8,128)(2,1)S(1)} %constant_dynamic-slice_fusion.1), channel_id=1, source_target_pairs={{0,2},{1,3},{2,0},{3,1},{4,6},{5,7},{6,4},{7,5},{8,10},{9,11},{10,... | collective-permute-start | bytes 887816 | tf_op jit(solution)/shard_map/ppermute | solution.py:39
  742.1 36.5 %collective-permute-start.64 = (bf16[1,1,136,1088]{3,2,1,0:T(8,128)(2,1)S(1)}, bf16[1,1,136,1088]{3,2,1,0:T(8,128)(2,1)S(1)}, u32[]{:S(2)}, u32[]{:S(2)}) collective-permute-start(bf16[1,1,136,1088]{3,2,1,0:T(8,128)(2,1)S(1)} %constant_dynamic-slice_fusion), channel_id=1, source_target_pairs={{0,2},{1,3},{2,0},{3,1},{4,6},{5,7},{6,4},{7,5},{8,10},{9,11},{10,... | collective-permute-start | bytes 887816 | tf_op jit(solution)/shard_map/ppermute | solution.py:39
  742.3 47.2 %collective-permute-start.61 = (bf16[1,34,4352]{2,1,0:T(8,128)(2,1)S(1)}, bf16[1,34,4352]{2,1,0:T(8,128)(2,1)S(1)}, u32[]{:S(2)}, u32[]{:S(2)}) collective-permute-start(bf16[1,34,4352]{2,1,0:T(8,128)(2,1)S(1)} %fusion.110), channel_id=1, source_target_pairs={{0,2},{1,3},{2,0},{3,1},{4,6},{5,7},{6,4},{7,5},{8,10},{9,11},{10,... | collective-permute-start | bytes 887816 | tf_op jit(solution)/shard_map/ppermute | solution.py:39
  778.7 15.6 %collective-permute-start.65 = (bf16[1,136,1088]{2,1,0:T(8,128)(2,1)S(1)}, bf16[1,136,1088]{2,1,0:T(8,128)(2,1)S(1)}, u32[]{:S(2)}, u32[]{:S(2)}) collective-permute-start(bf16[1,136,1088]{2,1,0:T(8,128)(2,1)S(1)} %fusion.112), channel_id=1, source_target_pairs={{0,2},{1,3},{2,0},{3,1},{4,6},{5,7},{6,4},{7,5},{8,10},{9,11},{10,... | collective-permute-start | bytes 887816 | tf_op jit(solution)/shard_map/ppermute | solution.py:39
  790.1 16.8 %collective-permute-start.62 = (bf16[2,34,4352]{2,0,1:T(2,128)(2,1)S(1)}, bf16[2,34,4352]{2,0,1:T(2,128)(2,1)S(1)}, u32[]{:S(2)}, u32[]{:S(2)}) collective-permute-start(bf16[2,34,4352]{2,0,1:T(2,128)(2,1)S(1)} %copy.134), channel_id=1, source_target_pairs={{0,1},{1,0},{2,3},{3,2},{4,5},{5,4},{6,7},{7,6},{8,9},{9,8},{10,11... | collective-permute-start | bytes 1775624 | tf_op jit(solution)/shard_map/ppermute | solution.py:39
  790.7 12.2 %collective-permute-start.30 = (bf16[2,1,136,1088]{3,2,1,0:T(8,128)(2,1)S(1)}, bf16[2,1,136,1088]{3,2,1,0:T(8,128)(2,1)S(1)}, u32[]{:S(2)}, u32[]{:S(2)}) collective-permute-start(bf16[2,1,136,1088]{3,2,1,0:T(8,128)(2,1)S(1)} %dynamic-slice_bitcast_fusion.4), channel_id=1, source_target_pairs={{0,8},{4,12},{8,0},{12,4},{16,24},{20,28},{24,16},{28,20},{1,9},{5... | collective-permute-start | bytes 1775624 | tf_op jit(solution)/shard_map/ppermute | solution.py:39
  794.4 25.9 %collective-permute-start.66 = (bf16[2,136,1088]{2,1,0:T(8,128)(2,1)S(1)}, bf16[2,136,1088]{2,1,0:T(8,128)(2,1)S(1)}, u32[]{:S(2)}, u32[]{:S(2)}) collective-permute-start(bf16[2,136,1088]{2,1,0:T(8,128)(2,1)S(1)} %maximum_bitcast_fusion.1), channel_id=1, source_target_pairs={{0,1},{1,0},{2,3},{3,2},{4,5},{5,4},{6,7},{7,6},{8,9},{9,8},{10,11... | collective-permute-start | bytes 1775624 | tf_op jit(solution)/shard_map/ppermute | solution.py:39
  803.1 17.3 %collective-permute-start.31 = (bf16[1,1,136,1088]{3,2,1,0:T(8,128)(2,1)S(1)}, bf16[1,1,136,1088]{3,2,1,0:T(8,128)(2,1)S(1)}, u32[]{:S(2)}, u32[]{:S(2)}) collective-permute-start(bf16[1,1,136,1088]{3,2,1,0:T(8,128)(2,1)S(1)} %constant_dynamic-slice_fusion.14), channel_id=1, source_target_pairs={{0,16},{4,20},{8,24},{12,28},{16,0},{20,4},{24,8},{28,12},{1,17},{... | collective-permute-start | bytes 887816 | tf_op jit(solution)/shard_map/ppermute | solution.py:39
  823.7 7.6 collective-permute-start.36
  823.8 7.1 collective-permute-start.32
  831.0 7.1 collective-permute-start.33
  832.4 16.0 %collective-permute-start.37 = (bf16[2,1,136,1088]{3,2,1,0:T(8,128)(2,1)}, bf16[2,1,136,1088]{3,2,1,0:T(8,128)(2,1)}, u32[]{:S(2)}, u32[]{:S(2)}) collective-permute-start(bf16[2,1,136,1088]{3,2,1,0:T(8,128)(2,1)} %dynamic-slice_bitcast_fusion.3), channel_id=1, source_target_pairs={{0,8},{4,12},{8,0},{12,4},{16,24},{20,28},{24,16},{28,20},{1,9},{5... | collective-permute-start | bytes 1775624 | tf_op jit(solution)/shard_map/ppermute | solution.py:39
  838.1 12.7 %collective-permute-start.34 = (bf16[1,34,1088]{2,1,0:T(8,128)(2,1)S(1)}, bf16[1,34,1088]{2,1,0:T(8,128)(2,1)S(1)}, u32[]{:S(2)}, u32[]{:S(2)}) collective-permute-start(bf16[1,34,1088]{2,1,0:T(8,128)(2,1)S(1)} %fusion.113), channel_id=1, source_target_pairs={{0,2},{1,3},{2,0},{3,1},{4,6},{5,7},{6,4},{7,5},{8,10},{9,11},{10,... | collective-permute-start | bytes 221960 | tf_op jit(solution)/shard_map/ppermute | solution.py:39
  849.9 8.2 collective-permute-start.38
  850.9 8.8 collective-permute-start.35
  858.4 5.6 collective-permute-start.39
  864.0 8.4 collective-permute-start.40
  872.4 34.8 %collective-permute-start.41 = (bf16[1,34,1088]{2,1,0:T(8,128)(2,1)S(1)}, bf16[1,34,1088]{2,1,0:T(8,128)(2,1)S(1)}, u32[]{:S(2)}, u32[]{:S(2)}) collective-permute-start(bf16[1,34,1088]{2,1,0:T(8,128)(2,1)S(1)} %fusion.114), channel_id=1, source_target_pairs={{0,2},{1,3},{2,0},{3,1},{4,6},{5,7},{6,4},{7,5},{8,10},{9,11},{10,... | collective-permute-start | bytes 221960 | tf_op jit(solution)/shard_map/ppermute | solution.py:39
  896.6 14.9 %collective-permute-start.54 = (f32[4,1,1088]{2,1,0:T(1,128)S(1)}, f32[4,1,1088]{2,1,0:T(1,128)S(1)}, u32[]{:S(2)}, u32[]{:S(2)}) collective-permute-start(f32[4,1,1088]{2,1,0:T(1,128)S(1)} %fusion.119), channel_id=1, source_target_pairs={{0,4},{4,0},{8,12},{12,8},{16,20},{20,16},{24,28},{28,24},{1,5},{5... | collective-permute-start | bytes 52232 | tf_op jit(solution)/shard_map/ppermute | solution.py:39
  903.1 9.6 collective-permute-start.43
  909.1 20.5 %collective-permute-start.28 = (f32[544]{0:T(1024)S(1)}, f32[544]{0:T(1024)S(1)}, u32[]{:S(2)}, u32[]{:S(2)}) collective-permute-start(f32[544]{0:T(1024)S(1)} %add.552), channel_id=1, source_target_pairs={{0,2},{1,3},{2,0},{3,1},{4,6},{5,7},{6,4},{7,5},{8,10},{9,11},{10,... | collective-permute-start | bytes 6536 | tf_op jit(solution)/shard_map/ppermute | solution.py:39
  913.0 13.0 %collective-permute-start.44 = (bf16[1,2,136,1088]{3,2,1,0:T(8,128)(2,1)S(1)}, bf16[1,2,136,1088]{3,2,1,0:T(8,128)(2,1)S(1)}, u32[]{:S(2)}, u32[]{:S(2)}) collective-permute-start(bf16[1,2,136,1088]{3,2,1,0:T(8,128)(2,1)S(1)} %dynamic-slice_bitcast_fusion.2), channel_id=1, source_target_pairs={{0,16},{4,20},{8,24},{12,28},{16,0},{20,4},{24,8},{28,12},{1,17},{... | collective-permute-start | bytes 1775624 | tf_op jit(solution)/shard_map/ppermute | solution.py:39
  915.3 12.0 %collective-permute-start.56 = (f32[1,1,1088]{2,1,0:T(1,128)S(1)}, f32[1,1,1088]{2,1,0:T(1,128)S(1)}, u32[]{:S(2)}, u32[]{:S(2)}) collective-permute-start(f32[1,1,1088]{2,1,0:T(1,128)S(1)} %constant_dynamic-slice_fusion.2), channel_id=1, source_target_pairs={{0,16},{4,20},{8,24},{12,28},{16,0},{20,4},{24,8},{28,12},{1,17},{... | collective-permute-start | bytes 13064 | tf_op jit(solution)/shard_map/ppermute | solution.py:39
  926.3 7.0 collective-permute-start.45
  927.7 19.2 %collective-permute-start.42 = (bf16[2,34,1088]{2,1,0:T(8,128)(2,1)S(1)}, bf16[2,34,1088]{2,1,0:T(8,128)(2,1)S(1)}, u32[]{:S(2)}, u32[]{:S(2)}) collective-permute-start(bf16[2,34,1088]{2,1,0:T(8,128)(2,1)S(1)} %maximum_bitcast_fusion.3), channel_id=1, source_target_pairs={{0,1},{1,0},{2,3},{3,2},{4,5},{5,4},{6,7},{7,6},{8,9},{9,8},{10,11... | collective-permute-start | bytes 443912 | tf_op jit(solution)/shard_map/ppermute | solution.py:39
  933.5 6.6 collective-permute-start.46
  940.1 6.6 collective-permute-start.47
  946.8 6.0 collective-permute-start.48
  952.9 5.6 collective-permute-start.49
  (74 other events, 999.5 us)
Sparse Core Ops, SparseCore 0:
  10.0 52.2 all-gather.4
  64.2 29.6 all-gather.8
  95.7 58.9 all-gather.6
  156.5 61.3 all-gather.10
  529.5 79.9 reduce-scatter.2
  646.8 127.1 reduce-scatter.4

commit v3 on v2

--- a/solution.py
+++ b/solution.py
@@ -57,7 +57,9 @@
         mine = bit_of(axis, bit)
         sent = lax.dynamic_index_in_dim(view, 1 - mine, 1, keepdims=False).astype(wire)
         kept = lax.dynamic_index_in_dim(view, mine, 1, keepdims=False)
-        yield sent
+        after = yield sent
+        if after is not None:
+            sent = tie(sent, after)
         total = kept.astype(jnp.float32) + swap(sent, axis, bit).astype(jnp.float32)
         parts = total.astype(wire).reshape((-1,) + rest)
     return parts[0]
@@ -285,21 +287,22 @@
         "sqhd,skhd->sqhk", query_heads, key_heads, preferred_element_type=jnp.float32
     )
     weights = jnp.where(seen, jnp.exp(scores - log_total[..., None]), 0.0)
-    value_heads = after_exchange(piece_values).reshape(seq_count, count, head_count, head_size)
-    d_weights = jnp.einsum(
-        "sqhd,skhd->sqhk", d_heads, value_heads, preferred_element_type=jnp.float32
-    )
-    d_scores = (weights * (d_weights - delta[..., None])).astype(jnp.bfloat16)
     d_heads = after_exchange(d_heads)
     d_value = jnp.einsum(
         "sqhk,sqhd->skhd", weights.astype(jnp.bfloat16), d_heads, preferred_element_type=jnp.float32
     ).reshape(seq_count, count, width)
+    d_value = jnp.roll(d_value.astype(jnp.bfloat16), place_index * local_rows, axis=1)
+    value_heads = tie(piece_values, d_value).reshape(seq_count, count, head_count, head_size)
+    d_weights = jnp.einsum(
+        "sqhd,skhd->sqhk", d_heads, value_heads, preferred_element_type=jnp.float32
+    )
+    d_scores = (weights * (d_weights - delta[..., None])).astype(jnp.bfloat16)
+    query_heads = after_exchange(query_heads)
     d_key = jnp.einsum(
         "sqhk,sqhd->skhd", d_scores, query_heads, preferred_element_type=jnp.float32
     ).reshape(seq_count, count, width)
-    d_value = jnp.roll(d_value.astype(jnp.bfloat16), place_index * local_rows, axis=1)
     d_key = jnp.roll(d_key.astype(jnp.bfloat16), place_index * local_rows, axis=1)
-    key_heads = after_exchange(key_heads)
+    key_heads = tie(key_heads, d_key)
     d_query = jnp.einsum("sqhk,skhd->sqhd", d_scores, key_heads, preferred_element_type=jnp.float32)
     d_key_all = d_key
     d_value_all = d_value
@@ -313,6 +316,9 @@
             d_value_all.astype(jnp.bfloat16), "ctx", scatter_dimension=1, tiled=True
         ).astype(jnp.float32),
     )
+    for steps in running:
+        next(steps)
+        steps.send(d_key_sum)
     d_queries = d_query.reshape(total_rows, width).astype(jnp.bfloat16) * scale
     d_keys = d_key_sum.reshape(total_rows, width).astype(jnp.bfloat16)
     d_values = d_value_sum.reshape(total_rows, width).astype(jnp.bfloat16)

time: 978 us -> 950 us (0.971)
  waiting for transfers between devices: 425 us -> 370 us
  other arithmetic: 101 us -> 115 us
    ppermute x55, waiting for transfers between devices: 268 us -> 212 us  [swap(): return lax.ppermute(values, axis, [(i, i ^ 1 << bit) for i in range(count)])]
    convert_element_type x24, other arithmetic: 27.9 us -> 40.2 us  [halve_steps(): parts = total.astype(wire).reshape((-1,) + rest)]
  transfers between devices with their start and end apart: 73 -> 73, of which waited for: 41 -> 42; matrix products, arithmetic and copies ran while one was open for 42% -> 43% of each run, Pallas kernels for 0% -> 0%
where the time goes in v3:
time: 950 us; the launch traced here: 939 us
  waiting for transfers between devices  370 us (39%)
  matrix products  292 us (31%)
  other arithmetic  115 us (12%)
  local copies, waits for them, and re-layouts  72.8 us (8%)
  starting transfers between devices  72.8 us (8%)
  between operations  16.2 us (2%)
    ppermute x55, waiting for transfers between devices, swap(): return lax.ppermute(values, axis, [(i, i ^ 1 << bit) for i in range(count)])  212 us
    ppermute x6, waiting for transfers between devices, ring_gather(): lax.ppermute(upper[-1], axis, [(i + 1, i) for i in range(count - step)])  73.1 us
    ppermute x55, starting transfers between devices, swap(): return lax.ppermute(values, axis, [(i, i ^ 1 << bit) for i in range(count)])  53 us
    dot_general x2, matrix products, per_device(): jnp.einsum('sqhd,skhd->sqhk', query_heads, key_heads, preferred_element_t...  52.7 us
    dot_general x1, matrix products, per_device(): jnp.einsum('sqhd,skhd->sqhk', d_heads, value_heads, preferred_element_typ...  44.9 us
    all_gather x1, waiting for transfers between devices, per_device(): qkv_full = lax.all_gather(qkv_weight, 'dp', axis=0, tiled=True)  41.6 us
    ppermute x6, waiting for transfers between devices, ring_gather(): lax.ppermute(lower[-1], axis, [(i, i + 1) for i in range(step - 1, count...  40.5 us
    convert_element_type x24, other arithmetic, halve_steps(): parts = total.astype(wire).reshape((-1,) + rest)  40.2 us
  transfers between devices with their start and end apart: 73, of which 42 were waited for; matrix products, arithmetic and copies ran while one was open for 43% of the time, Pallas kernels for 0%

profile of v3, /device:TPU:0, one launch (start us, length us, event | category | flops | bytes accessed | tf_op | source)
XLA Modules:
  0.0 939.0 jit_solution(9786317920415798335)
XLA Ops:
  11.3 2.9 collective-permute-start.1
  20.7 41.6 %all-gather.5.cloned.1.call-done = bf16[1088,3264]{1,0:T(8,128)(2,1)} async-done(((bf16[136,3264]{1,0:T(8,128)(2,1)}), bf16[1088,3264]{1,0:T(8,128)(2,1)}) %all-gather.5.cloned.1.call-update) | async-done | bytes 7102480 | tf_op jit(solution)/shard_map/all_gather | solution.py:200
  62.3 6.9 fusion.165
  69.4 2.6 copy-done.23
  72.0 3.4 collective-permute-start.4
  76.8 22.8 %collective-permute-done.4 = bf16[1,512,1088]{1,2,0:T(8,128)(2,1)S(1)} collective-permute-done((bf16[1,512,1088]{1,2,0:T(8,128)(2,1)S(1)}, bf16[1,512,1088]{1,2,0:T(8,128)(2,1)S(1)}, u32[]{:S(2)}, u32[]{:S(2)}) %collective-permute-start.4) | collective-permute-done | bytes 1114144 | tf_op jit(solution)/shard_map/ppermute | solution.py:85
  101.3 2.6 collective-permute-done.3
  106.4 3.7 fusion.93
  110.0 22.7 %collective-permute-done.7 = bf16[1,512,1088]{1,2,0:T(8,128)(2,1)} collective-permute-done((bf16[1,512,1088]{1,2,0:T(8,128)(2,1)}, bf16[1,512,1088]{1,2,0:T(8,128)(2,1)}, u32[]{:S(2)}, u32[]{:S(2)}) %collective-permute-start.7) | collective-permute-done | bytes 1114144 | tf_op jit(solution)/shard_map/ppermute | solution.py:86
  137.0 22.9 %collective-permute-done.8 = bf16[1,512,1088]{1,2,0:T(8,128)(2,1)S(1)} collective-permute-done((bf16[1,512,1088]{1,2,0:T(8,128)(2,1)}, bf16[1,512,1088]{1,2,0:T(8,128)(2,1)S(1)}, u32[]{:S(2)}, u32[]{:S(2)}) %collective-permute-start.8) | collective-permute-done | bytes 1114144 | tf_op jit(solution)/shard_map/ppermute | solution.py:86
  168.4 17.6 %collective-permute-done.10 = bf16[1,512,1088]{1,2,0:T(8,128)(2,1)} collective-permute-done((bf16[1,512,1088]{1,2,0:T(8,128)(2,1)}, bf16[1,512,1088]{1,2,0:T(8,128)(2,1)}, u32[]{:S(2)}, u32[]{:S(2)}) %collective-permute-start.10) | collective-permute-done | bytes 1114144 | tf_op jit(solution)/shard_map/ppermute | solution.py:85
  187.7 28.2 %fusion.4 = (f32[512,17]{0,1:T(8,128)S(1)}, f32[17,2048,512]{2,1,0:T(8,128)}) fusion(pred[512,2048]{0,1:T(8,128)(4,1)S(1)} %broadcast_compare_fusion, bf16[2048,17,64]{0,2,1:T(8,128)(2,1)} %bitcast.489, bf16[512,17,64]{0,2,1:T(8,128)(2,1)S(1)} %bitcast.495), kind=kOutput, calls=%fused_computation.8 | convolution fusion | flops 2317344256 | bytes 77957120 | tf_op jit(solution)/shard_map/sqhd,skhd->sqhk/dot_general | solution.py:229
  218.9 22.7 %fusion.6 = f32[512,17]{0,1:T(8,128)S(1)} fusion(f32[17,2048,512]{2,1,0:T(8,128)} %get-tuple-element.101, f32[512,17]{0,1:T(8,128)S(1)} %broadcast_maximum_fusion, pred[512,2048]{0,1:T(8,128)(4,1)S(1)} %broadcast_compare_fusion), kind=kLoop, calls=%fused_computation.10 | loop fusion | flops 71294464 | bytes 72421376 | tf_op jit(solution)/shard_map/reduce_sum | solution.py:235
  246.8 23.3 %collective-permute-done.14 = bf16[1,512,1088]{1,2,0:T(8,128)(2,1)S(1)} collective-permute-done((bf16[1,512,1088]{1,2,0:T(8,128)(2,1)S(1)}, bf16[1,512,1088]{1,2,0:T(8,128)(2,1)S(1)}, u32[]{:S(2)}, u32[]{:S(2)}) %collective-permute-start.14) | collective-permute-done | bytes 1114144 | tf_op jit(solution)/shard_map/ppermute | solution.py:86
  270.2 3.5 pad_maximum_fusion.1
  273.7 28.8 %fusion.163 = (bf16[1,512,17,64]{1,3,2,0:T(8,128)(2,1)S(1)}, f32[1,512,17,64]{1,3,2,0:T(8,128)}) fusion(f32[512,17]{0,1:T(8,128)S(1)} %fusion.6, f32[17,2048,512]{2,1,0:T(8,128)} %get-tuple-element.101, f32[512,17]{0,1:T(8,128)S(1)} %broadcast_maximum_fusion, pred[512,2048]{0,1:T(8,128)(4,1)S(1)} %broadcast_compare_fusion, ...), kind=kOutput, calls=%fused_computation.346 | convolution fusion | flops 2354118656 | bytes 80220160 | tf_op jit(solution)/shard_map/sqhk,skhd->sqhd/dot_general | solution.py:237
  302.5 3.6 fusion.164
  307.0 11.6 %fusion.34 = (bf16[4352,512]{0,1:T(8,128)(2,1)}, f32[512,4352]{1,0:T(8,128)}) fusion(f32[4352]{0:T(1024)S(1)} %add.518, bf16[1088,4352]{1,0:T(8,128)(2,1)S(1)} %copy-done.57, f32[512,1088]{0,1:T(8,128)S(1)} %get-tuple-element.105, f32[1088]{0:T(1024)S(1)} %add.515, f32[1088]{0:T(1024)S(1)} %mul.246, f32[512]{0:T(512)S(1)} %fusion.148, ...), kind=kOutput, calls=%fused_computation.43 | convolution fusion | flops 4873682944 | bytes 25097728 | tf_op jit(solution)/shard_map/dot_general | solution.py:252
  318.6 6.6 copy.118
  325.2 14.3 %convert_reduce_fusion = (f32[4352]{0:T(1024)}, bf16[512,4352]{1,0:T(8,128)(2,1)S(1)}) fusion(f32[512,4352]{1,0:T(8,128)} %get-tuple-element.107, bf16[4352,1088]{1,0:T(8,128)(2,1)} %all-gather.11.cloned.1.call-done, bf16[1,512,1088]{1,2,0:T(8,128)(2,1)S(1)} %copy-done.24), kind=kOutput, calls=%fused_computation.48 | convolution fusion | flops 4897632256 | bytes 23970816 | tf_op jit(solution)/shard_map/rd,fd->rf/dot_general | solution.py:261
  339.5 9.3 fusion.157
  348.8 9.8 %multiply_reduce_fusion = (f32[1088]{0:T(1024)}, f32[512]{0:T(512)S(1)}, f32[1088]{0:T(1024)}, f32[512,1088]{0,1:T(8,128)S(1)}) fusion(f32[512,1088]{0,1:T(8,128)S(1)} %copy-done.14, f32[512]{0:T(512)S(1)} %fusion.148, f32[512]{0:T(512)S(1)} %broadcast_multiply_fusion, f32[1088]{0:T(1024)S(1)} %mul.246, bf16[512,4352]{1,0:T(8,128)(2,1)S(1)} %get-tuple-element.114, ...), kind=kOutput, calls=%fused_computation.117 | convolution fusion | flops 4853069312 | bytes 18402048 | tf_op jit(solution)/shard_map/rf,df->rd/dot_general | solution.py:266
  364.5 4.3 fusion.36
  368.9 10.4 %fusion.99 = f32[4,2,544,1088]{3,2,1,0:T(8,128)} fusion(bf16[4,2,544,512]{3,2,1,0:T(8,128)(2,1)S(1)} %bitcast.526, bf16[1,512,1088]{1,2,0:T(8,128)(2,1)S(1)} %copy-done.24), kind=kOutput, calls=%fused_computation.153 | convolution fusion | flops 4848615424 | bytes 24510464 | tf_op jit(solution)/shard_map/rf,rd->fd/dot_general | solution.py:259
  379.4 6.8 dynamic-slice_convert_fusion
  386.6 24.5 %fusion.167 = f32[17,2048,512]{2,1,0:T(8,128)} fusion(bf16[2048,17,64]{0,2,1:T(8,128)(2,1)S(1)} %bitcast.493, bf16[512,17,64]{0,2,1:T(8,128)(2,1)S(1)} %bitcast.496), kind=kOutput, calls=%fused_computation.350 | convolution fusion | flops 2281701376 | bytes 76873728 | tf_op jit(solution)/shard_map/sqhd,skhd->sqhk/dot_general | solution.py:286
  416.8 12.6 %collective-permute-done.20 = bf16[1,2,136,1088]{3,2,1,0:T(8,128)(2,1)S(1)} collective-permute-done((bf16[1,2,136,1088]{3,2,1,0:T(8,128)(2,1)S(1)}, bf16[1,2,136,1088]{3,2,1,0:T(8,128)(2,1)S(1)}, u32[]{:S(2)}, u32[]{:S(2)}) %collective-permute-start.20) | collective-permute-done | bytes 591904 | tf_op jit(solution)/shard_map/ppermute | solution.py:39
  431.9 6.1 fusion.19
  441.2 8.8 add_convert_fusion
  450.0 3.4 dynamic-slice_bitcast_fusion
  455.0 27.3 %fusion.44 = bf16[17,64,2048]{2,1,0:T(8,128)(2,1)} fusion(f32[17,2048,512]{2,1,0:T(8,128)} %fusion.167, f32[512,17]{0,1:T(8,128)S(1)} %copy-done.44, pred[512,2048]{0,1:T(8,128)(4,1)S(1)} %broadcast_compare_fusion, bf16[1,512,17,64]{1,3,2,0:T(8,128)(2,1)S(1)} %bitcast.532), kind=kOutput, calls=%fused_computation.64 | convolution fusion | flops 2337406976 | bytes 77957120 | tf_op jit(solution)/shard_map/sqhk,sqhd->skhd/dot_general | solution.py:291
  482.4 7.1 fusion.39
  489.5 44.9 %fusion.12 = bf16[512,17,2048]{0,2,1:T(8,128)(2,1)} fusion(f32[17,2048,512]{2,1,0:T(8,128)} %fusion.167, f32[512,17]{0,1:T(8,128)S(1)} %multiply_reduce_fusion.1, f32[512,17]{0,1:T(8,128)S(1)} %copy-done.44, pred[512,2048]{0,1:T(8,128)(4,1)S(1)} %broadcast_compare_fusion, bf16[2048,17,64]{0,2,1:T(8,128)(2,1)} %bitcast.523, ...), kind=kOutput, calls=%fused_computation.15 | convolution fusion | flops 2370830336 | bytes 113643520 | tf_op jit(solution)/shard_map/sqhd,skhd->sqhk/dot_general | solution.py:296
  534.4 3.0 fusion.37
  537.5 3.1 fusion.35
  543.0 18.8 %convolution_convert_fusion = bf16[17,64,2048]{2,1,0:T(8,128)(2,1)} fusion(bf16[512,17,2048]{0,2,1:T(8,128)(2,1)} %fusion.12, bf16[1,512,17,64]{1,3,2,0:T(8,128)(2,1)S(1)} %bitcast.497), kind=kOutput, calls=%fused_computation.65 | convolution fusion | flops 2283929600 | bytes 41222144 | tf_op jit(solution)/shard_map/sqhk,sqhd->skhd/dot_general | solution.py:301
  561.8 7.2 fusion.38
  568.9 19.6 %convert_reduce_fusion.5 = (f32[17,64]{1,0:T(8,128)S(1)}, bf16[17,64,512]{2,1,0:T(8,128)(2,1)}) fusion(bf16[512,17,2048]{0,2,1:T(8,128)(2,1)} %fusion.12, bf16[1,2048,17,64]{1,3,2,0:T(8,128)(2,1)} %bitcast.490), kind=kOutput, calls=%fused_computation.120 | convolution fusion | flops 2283928576 | bytes 41226496 | tf_op jit(solution)/shard_map/sqhk,skhd->sqhd/dot_general | solution.py:306
  588.6 2.9 fusion.168
  595.8 14.7 %fusion.62 = bf16[1,512,1088]{1,2,0:T(8,128)(2,1)} fusion(f32[512,1088]{0,1:T(8,128)S(1)} %copy-done.15, bf16[4352,1088]{1,0:T(8,128)(2,1)} %all-gather.11.cloned.1.call-done, f32[512,4352]{1,0:T(8,128)} %get-tuple-element.107, f32[1088]{0:T(1024)S(1)} %copy-done.53), kind=kOutput, calls=%fused_computation.89 | convolution fusion | flops 4870340608 | bytes 21729536 | tf_op jit(solution)/shard_map/dot_general | solution.py:254
  624.8 17.9 %collective-permute-done.57 = bf16[1,1,136,4352]{3,2,1,0:T(8,128)(2,1)} collective-permute-done((bf16[1,1,136,4352]{3,2,1,0:T(8,128)(2,1)}, bf16[1,1,136,4352]{3,2,1,0:T(8,128)(2,1)}, u32[]{:S(2)}, u32[]{:S(2)}) %collective-permute-start.57) | collective-permute-done | bytes 1183776 | tf_op jit(solution)/shard_map/ppermute | solution.py:39
  646.9 7.8 collective-permute-done.27
  656.3 2.6 add_convert_fusion.1
  658.9 5.3 collective-permute-done.28
  664.7 2.9 fusion.95
  667.8 15.4 %collective-permute-done.29 = bf16[2,1,34,1088]{3,2,0,1:T(8,128)(2,1)S(1)} collective-permute-done((bf16[2,1,34,1088]{3,2,0,1:T(8,128)(2,1)S(1)}, bf16[2,1,34,1088]{3,2,0,1:T(8,128)(2,1)S(1)}, u32[]{:S(2)}, u32[]{:S(2)}) %collective-permute-start.29) | collective-permute-done | bytes 148000 | tf_op jit(solution)/shard_map/ppermute | solution.py:39
  685.6 10.1 %collective-permute-done.30 = bf16[1,1,34,1088]{3,2,0,1:T(8,128)(2,1)S(1)} collective-permute-done((bf16[1,1,34,1088]{3,2,0,1:T(8,128)(2,1)S(1)}, bf16[1,1,34,1088]{3,2,0,1:T(8,128)(2,1)S(1)}, u32[]{:S(2)}, u32[]{:S(2)}) %collective-permute-start.30) | collective-permute-done | bytes 74016 | tf_op jit(solution)/shard_map/ppermute | solution.py:39
  696.3 10.7 %collective-permute-done.31 = bf16[1,34,1088]{2,1,0:T(8,128)(2,1)S(1)} collective-permute-done((bf16[1,34,1088]{2,1,0:T(8,128)(2,1)S(1)}, bf16[1,34,1088]{2,1,0:T(8,128)(2,1)S(1)}, u32[]{:S(2)}, u32[]{:S(2)}) %collective-permute-start.31) | collective-permute-done | bytes 74016 | tf_op jit(solution)/shard_map/ppermute | solution.py:39
  714.0 2.8 collective-permute-done.42
  735.9 7.4 fusion.70
  747.1 4.7 convert_reduce_fusion.1
  760.7 3.2 fusion.97
  773.4 15.2 %collective-permute-done.24 = f32[544]{0:T(1024)S(1)} collective-permute-done((f32[544]{0:T(1024)S(1)}, f32[544]{0:T(1024)S(1)}, u32[]{:S(2)}, u32[]{:S(2)}) %collective-permute-start.24) | collective-permute-done | bytes 2208 | tf_op jit(solution)/shard_map/ppermute | solution.py:39
  801.7 3.3 collective-permute-done.49
  807.1 3.4 collective-permute-done.50
  810.6 3.0 collective-permute-start.51
  826.0 16.8 %collective-permute-done.64 = bf16[1,1,136,1088]{3,2,1,0:T(8,128)(2,1)S(1)} collective-permute-done((bf16[1,1,136,1088]{3,2,1,0:T(8,128)(2,1)S(1)}, bf16[1,1,136,1088]{3,2,1,0:T(8,128)(2,1)S(1)}, u32[]{:S(2)}, u32[]{:S(2)}) %collective-permute-start.64) | collective-permute-done | bytes 295968 | tf_op jit(solution)/shard_map/ppermute | solution.py:39
  843.0 14.0 %collective-permute-done.59 = bf16[1,1,34,4352]{3,2,0,1:T(8,128)(2,1)S(1)} collective-permute-done((bf16[1,1,34,4352]{3,2,0,1:T(8,128)(2,1)S(1)}, bf16[1,1,34,4352]{3,2,0,1:T(8,128)(2,1)S(1)}, u32[]{:S(2)}, u32[]{:S(2)}) %collective-permute-start.59) | collective-permute-done | bytes 295968 | tf_op jit(solution)/shard_map/ppermute | solution.py:39
  857.1 14.0 %collective-permute-done.65 = bf16[1,136,1088]{2,1,0:T(8,128)(2,1)S(1)} collective-permute-done((bf16[1,136,1088]{2,1,0:T(8,128)(2,1)S(1)}, bf16[1,136,1088]{2,1,0:T(8,128)(2,1)S(1)}, u32[]{:S(2)}, u32[]{:S(2)}) %collective-permute-start.65) | collective-permute-done | bytes 295968 | tf_op jit(solution)/shard_map/ppermute | solution.py:39
  878.2 10.3 %collective-permute-done.34 = bf16[2,1,136,1088]{3,2,1,0:T(8,128)(2,1)S(1)} collective-permute-done((bf16[2,1,136,1088]{3,2,1,0:T(8,128)(2,1)S(1)}, bf16[2,1,136,1088]{3,2,1,0:T(8,128)(2,1)S(1)}, u32[]{:S(2)}, u32[]{:S(2)}) %collective-permute-start.34) | collective-permute-done | bytes 591904 | tf_op jit(solution)/shard_map/ppermute | solution.py:39
  891.1 12.1 %collective-permute-done.61 = bf16[2,34,4352]{2,0,1:T(2,128)(2,1)S(1)} collective-permute-done((bf16[2,34,4352]{2,0,1:T(2,128)(2,1)S(1)}, bf16[2,34,4352]{2,0,1:T(2,128)(2,1)S(1)}, u32[]{:S(2)}, u32[]{:S(2)}) %collective-permute-start.61) | collective-permute-done | bytes 591904 | tf_op jit(solution)/shard_map/ppermute | solution.py:39
  903.9 6.3 collective-permute-done.36
  912.6 4.4 collective-permute-done.37
  918.1 5.5 collective-permute-done.38
  (463 shorter events, 186.7 us)
Async XLA Ops:
  7.3 55.0 %all-gather.5.cloned.1.call-start = ((), (), s32[]{:S(2)}) async-start(), calls=%async_computation.2 | async-start | bytes 8146944 | tf_op jit(solution)/shard_map/all_gather | solution.py:200
  8.0 160.4 %all-gather.9.cloned.1.call-start = ((), (), s32[]{:S(2)}) async-start(), calls=%async_computation.4 | async-start | bytes 2820096 | tf_op jit(solution)/shard_map/all_gather | solution.py:201
  8.8 264.9 %all-gather.7.cloned.1.call-start = ((), (), s32[]{:S(2)}) async-start(), calls=%async_computation.3 | async-start | bytes 10653696 | tf_op jit(solution)/shard_map/all_gather | solution.py:202
  9.5 293.0 %all-gather.11.cloned.1.call-start = ((), (), s32[]{:S(2)}) async-start(), calls=%async_computation.5 | async-start | bytes 11280384 | tf_op jit(solution)/shard_map/all_gather | solution.py:203
  72.0 27.6 %collective-permute-start.4 = (bf16[1,512,1088]{1,2,0:T(8,128)(2,1)S(1)}, bf16[1,512,1088]{1,2,0:T(8,128)(2,1)S(1)}, u32[]{:S(2)}, u32[]{:S(2)}) collective-permute-start(bf16[1,512,1088]{1,2,0:T(8,128)(2,1)S(1)} %fusion.94), channel_id=1, source_target_pairs={{0,1},{1,2},{2,3},{4,5},{5,6},{6,7},{8,9},{9,10},{10,11},{12,13},{... | collective-permute-start | bytes 3342344 | tf_op jit(solution)/shard_map/ppermute | solution.py:85
  75.5 28.4 %collective-permute-start.3 = (bf16[1,512,1088]{1,2,0:T(8,128)(2,1)S(1)}, bf16[1,512,1088]{1,2,0:T(8,128)(2,1)}, u32[]{:S(2)}, u32[]{:S(2)}) collective-permute-start(bf16[1,512,1088]{1,2,0:T(8,128)(2,1)S(1)} %fusion.94), channel_id=1, source_target_pairs={{1,0},{2,1},{3,2},{5,4},{6,5},{7,6},{9,8},{10,9},{11,10},{13,12},{... | collective-permute-start | bytes 3342344 | tf_op jit(solution)/shard_map/ppermute | solution.py:86
  99.6 6.0 collective-permute-start.5
  103.9 28.8 %collective-permute-start.7 = (bf16[1,512,1088]{1,2,0:T(8,128)(2,1)}, bf16[1,512,1088]{1,2,0:T(8,128)(2,1)}, u32[]{:S(2)}, u32[]{:S(2)}) collective-permute-start(bf16[1,512,1088]{1,2,0:T(8,128)(2,1)} %collective-permute-done.3), channel_id=1, source_target_pairs={{1,0},{2,1},{5,4},{6,5},{9,8},{10,9},{13,12},{14,13},{17,16},{18,1... | collective-permute-start | bytes 3342344 | tf_op jit(solution)/shard_map/ppermute | solution.py:86
  105.2 559.5 %reduce-scatter.5.cloned.1.call-start = ((), (), s32[]{:S(2)}) async-start(), calls=%async_computation.7 | async-start | bytes 5570560 | tf_op jit(solution)/shard_map/reduce_scatter | solution.py:315
  105.6 29.8 %collective-permute-start.6 = (bf16[1,512,1088]{1,2,0:T(8,128)(2,1)}, bf16[1,512,1088]{1,2,0:T(8,128)(2,1)S(1)}, u32[]{:S(2)}, u32[]{:S(2)}) collective-permute-start(bf16[1,512,1088]{1,2,0:T(8,128)(2,1)} %collective-permute-done.5), channel_id=1, source_target_pairs={{2,3},{6,7},{10,11},{14,15},{18,19},{22,23},{26,27},{30,31}} | collective-permute-start | bytes 3342344 | tf_op jit(solution)/shard_map/ppermute | solution.py:85
  132.7 27.2 %collective-permute-start.8 = (bf16[1,512,1088]{1,2,0:T(8,128)(2,1)}, bf16[1,512,1088]{1,2,0:T(8,128)(2,1)S(1)}, u32[]{:S(2)}, u32[]{:S(2)}) collective-permute-start(bf16[1,512,1088]{1,2,0:T(8,128)(2,1)} %collective-permute-done.7), channel_id=1, source_target_pairs={{1,0},{5,4},{9,8},{13,12},{17,16},{21,20},{25,24},{29,28}} | collective-permute-start | bytes 3342344 | tf_op jit(solution)/shard_map/ppermute | solution.py:86
  162.5 23.6 %collective-permute-start.10 = (bf16[1,512,1088]{1,2,0:T(8,128)(2,1)}, bf16[1,512,1088]{1,2,0:T(8,128)(2,1)}, u32[]{:S(2)}, u32[]{:S(2)}) collective-permute-start(bf16[1,512,1088]{1,2,0:T(8,128)(2,1)} %get-tuple-element.28), channel_id=1, source_target_pairs={{0,1},{1,2},{2,3},{4,5},{5,6},{6,7},{8,9},{9,10},{10,11},{12,13},{... | collective-permute-start | bytes 3342344 | tf_op jit(solution)/shard_map/ppermute | solution.py:85
  167.1 48.8 %collective-permute-start.9 = (bf16[1,512,1088]{1,2,0:T(8,128)(2,1)}, bf16[1,512,1088]{1,2,0:T(8,128)(2,1)}, u32[]{:S(2)}, u32[]{:S(2)}) collective-permute-start(bf16[1,512,1088]{1,2,0:T(8,128)(2,1)} %get-tuple-element.28), channel_id=1, source_target_pairs={{1,0},{2,1},{3,2},{5,4},{6,5},{7,6},{9,8},{10,9},{11,10},{13,12},{... | collective-permute-start | bytes 3342344 | tf_op jit(solution)/shard_map/ppermute | solution.py:86
  186.1 31.2 %collective-permute-start.11 = (bf16[1,512,1088]{1,2,0:T(8,128)(2,1)}, bf16[1,512,1088]{1,2,0:T(8,128)(2,1)}, u32[]{:S(2)}, u32[]{:S(2)}) collective-permute-start(bf16[1,512,1088]{1,2,0:T(8,128)(2,1)} %collective-permute-done.10), channel_id=1, source_target_pairs={{1,2},{2,3},{5,6},{6,7},{9,10},{10,11},{13,14},{14,15},{17,18},{18... | collective-permute-start | bytes 3342344 | tf_op jit(solution)/shard_map/ppermute | solution.py:85
  215.9 27.9 %collective-permute-start.13 = (bf16[1,512,1088]{1,2,0:T(8,128)(2,1)}, bf16[1,512,1088]{1,2,0:T(8,128)(2,1)S(1)}, u32[]{:S(2)}, u32[]{:S(2)}) collective-permute-start(bf16[1,512,1088]{1,2,0:T(8,128)(2,1)} %collective-permute-done.9), channel_id=1, source_target_pairs={{1,0},{2,1},{5,4},{6,5},{9,8},{10,9},{13,12},{14,13},{17,16},{18,1... | collective-permute-start | bytes 3342344 | tf_op jit(solution)/shard_map/ppermute | solution.py:86
  217.2 28.2 %collective-permute-start.12 = (bf16[1,512,1088]{1,2,0:T(8,128)(2,1)}, bf16[1,512,1088]{1,2,0:T(8,128)(2,1)}, u32[]{:S(2)}, u32[]{:S(2)}) collective-permute-start(bf16[1,512,1088]{1,2,0:T(8,128)(2,1)} %collective-permute-done.11), channel_id=1, source_target_pairs={{2,3},{6,7},{10,11},{14,15},{18,19},{22,23},{26,27},{30,31}} | collective-permute-start | bytes 3342344 | tf_op jit(solution)/shard_map/ppermute | solution.py:85
  243.8 26.3 %collective-permute-start.14 = (bf16[1,512,1088]{1,2,0:T(8,128)(2,1)S(1)}, bf16[1,512,1088]{1,2,0:T(8,128)(2,1)S(1)}, u32[]{:S(2)}, u32[]{:S(2)}) collective-permute-start(bf16[1,512,1088]{1,2,0:T(8,128)(2,1)S(1)} %collective-permute-done.13), channel_id=1, source_target_pairs={{1,0},{5,4},{9,8},{13,12},{17,16},{21,20},{25,24},{29,28}} | collective-permute-start | bytes 3342344 | tf_op jit(solution)/shard_map/ppermute | solution.py:86
  362.5 48.7 %collective-permute-start.19 = (bf16[4,1,136,1088]{3,2,0,1:T(8,128)(2,1)S(1)}, bf16[4,1,136,1088]{3,2,0,1:T(8,128)(2,1)S(1)}, u32[]{:S(2)}, u32[]{:S(2)}) collective-permute-start(bf16[4,1,136,1088]{3,2,0,1:T(8,128)(2,1)S(1)} %fusion.86), channel_id=1, source_target_pairs={{0,4},{4,0},{8,12},{12,8},{16,20},{20,16},{24,28},{28,24},{1,5},{5... | collective-permute-start | bytes 3551240 | tf_op jit(solution)/shard_map/ppermute | solution.py:39
  368.8 63.1 %collective-permute-start.17 = (bf16[4,1,136,4352]{3,2,0,1:T(8,128)(2,1)S(1)}, bf16[4,1,136,4352]{3,2,0,1:T(8,128)(2,1)}, u32[]{:S(2)}, u32[]{:S(2)}) collective-permute-start(bf16[4,1,136,4352]{3,2,0,1:T(8,128)(2,1)S(1)} %fusion.36), channel_id=1, source_target_pairs={{0,4},{4,0},{8,12},{12,8},{16,20},{20,16},{24,28},{28,24},{1,5},{5... | collective-permute-start | bytes 14204936 | tf_op jit(solution)/shard_map/ppermute | solution.py:39
  386.1 55.0 %collective-permute-start.15 = (bf16[4,1,544,1088]{3,2,1,0:T(8,128)(2,1)}, bf16[4,1,544,1088]{3,2,1,0:T(8,128)(2,1)}, u32[]{:S(2)}, u32[]{:S(2)}) collective-permute-start(bf16[4,1,544,1088]{3,2,1,0:T(8,128)(2,1)} %dynamic-slice_convert_fusion), channel_id=1, source_target_pairs={{0,4},{4,0},{8,12},{12,8},{16,20},{20,16},{24,28},{28,24},{1,5},{5... | collective-permute-start | bytes 14204936 | tf_op jit(solution)/shard_map/ppermute | solution.py:39
  413.3 16.1 %collective-permute-start.20 = (bf16[1,2,136,1088]{3,2,1,0:T(8,128)(2,1)S(1)}, bf16[1,2,136,1088]{3,2,1,0:T(8,128)(2,1)S(1)}, u32[]{:S(2)}, u32[]{:S(2)}) collective-permute-start(bf16[1,2,136,1088]{3,2,1,0:T(8,128)(2,1)S(1)} %dynamic-slice_bitcast_fusion.6), channel_id=1, source_target_pairs={{0,16},{4,20},{8,24},{12,28},{16,0},{20,4},{24,8},{28,12},{1,17},{... | collective-permute-start | bytes 1775624 | tf_op jit(solution)/shard_map/ppermute | solution.py:39
  430.4 182.9 %collective-permute-start.47 = (bf16[1,1,136,1088]{3,2,1,0:T(8,128)(2,1)}, bf16[1,1,136,1088]{3,2,1,0:T(8,128)(2,1)}, u32[]{:S(2)}, u32[]{:S(2)}) collective-permute-start(bf16[1,1,136,1088]{3,2,1,0:T(8,128)(2,1)} %constant_dynamic-slice_fusion.22), channel_id=1, source_target_pairs={{0,8},{4,12},{8,0},{12,4},{16,24},{20,28},{24,16},{28,20},{1,9},{5... | collective-permute-start | bytes 887816 | tf_op jit(solution)/shard_map/ppermute | solution.py:39
  440.9 93.6 %collective-permute-start.18 = (bf16[1,2,136,4352]{3,2,1,0:T(8,128)(2,1)}, bf16[1,2,136,4352]{3,2,1,0:T(8,128)(2,1)}, u32[]{:S(2)}, u32[]{:S(2)}) collective-permute-start(bf16[1,2,136,4352]{3,2,1,0:T(8,128)(2,1)} %dynamic-slice_bitcast_fusion.1), channel_id=1, source_target_pairs={{0,16},{4,20},{8,24},{12,28},{16,0},{20,4},{24,8},{28,12},{1,17},{... | collective-permute-start | bytes 7102472 | tf_op jit(solution)/shard_map/ppermute | solution.py:39
  453.4 84.1 %collective-permute-start.16 = (bf16[2,1,544,1088]{3,2,0,1:T(8,128)(2,1)}, bf16[2,1,544,1088]{3,2,0,1:T(8,128)(2,1)}, u32[]{:S(2)}, u32[]{:S(2)}) collective-permute-start(bf16[2,1,544,1088]{3,2,0,1:T(8,128)(2,1)} %dynamic-slice_bitcast_fusion), channel_id=1, source_target_pairs={{0,8},{4,12},{8,0},{12,4},{16,24},{20,28},{24,16},{28,20},{1,9},{5... | collective-permute-start | bytes 7102472 | tf_op jit(solution)/shard_map/ppermute | solution.py:39
  489.4 246.4 %reduce-scatter.3.cloned.1.call-start = ((), (), s32[]{:S(2)}) async-start(), calls=%async_computation.6 | async-start | bytes 5570560 | tf_op jit(solution)/shard_map/reduce_scatter | solution.py:312
  594.9 26.0 %collective-permute-start.26 = (bf16[4,1,136,1088]{3,2,1,0:T(8,128)(2,1)}, bf16[4,1,136,1088]{3,2,1,0:T(8,128)(2,1)}, u32[]{:S(2)}, u32[]{:S(2)}) collective-permute-start(bf16[4,1,136,1088]{3,2,1,0:T(8,128)(2,1)} %dynamic-slice_convert_fusion.4), channel_id=1, source_target_pairs={{0,4},{4,0},{8,12},{12,8},{16,20},{20,16},{24,28},{28,24},{1,5},{5... | collective-permute-start | bytes 3551240 | tf_op jit(solution)/shard_map/ppermute | solution.py:39
  613.3 29.3 %collective-permute-start.57 = (bf16[1,1,136,4352]{3,2,1,0:T(8,128)(2,1)}, bf16[1,1,136,4352]{3,2,1,0:T(8,128)(2,1)}, u32[]{:S(2)}, u32[]{:S(2)}) collective-permute-start(bf16[1,1,136,4352]{3,2,1,0:T(8,128)(2,1)} %constant_dynamic-slice_fusion.23), channel_id=1, source_target_pairs={{0,8},{4,12},{8,0},{12,4},{16,24},{20,28},{24,16},{28,20},{1,9},{5... | collective-permute-start | bytes 3551240 | tf_op jit(solution)/shard_map/ppermute | solution.py:39
  618.6 37.7 %collective-permute-start.62 = (bf16[1,1,544,1088]{3,2,0,1:T(8,128)(2,1)}, bf16[1,1,544,1088]{3,2,0,1:T(8,128)(2,1)}, u32[]{:S(2)}, u32[]{:S(2)}) collective-permute-start(bf16[1,1,544,1088]{3,2,0,1:T(8,128)(2,1)} %constant_dynamic-slice_fusion.24), channel_id=1, source_target_pairs={{0,16},{4,20},{8,24},{12,28},{16,0},{20,4},{24,8},{28,12},{1,17},{... | collective-permute-start | bytes 3551240 | tf_op jit(solution)/shard_map/ppermute | solution.py:39
  624.2 30.4 %collective-permute-start.27 = (bf16[2,1,136,1088]{3,2,1,0:T(8,128)(2,1)}, bf16[2,1,136,1088]{3,2,1,0:T(8,128)(2,1)}, u32[]{:S(2)}, u32[]{:S(2)}) collective-permute-start(bf16[2,1,136,1088]{3,2,1,0:T(8,128)(2,1)} %dynamic-slice_bitcast_fusion.5), channel_id=1, source_target_pairs={{0,8},{4,12},{8,0},{12,4},{16,24},{20,28},{24,16},{28,20},{1,9},{5... | collective-permute-start | bytes 1775624 | tf_op jit(solution)/shard_map/ppermute | solution.py:39
  656.2 8.0 collective-permute-start.28
  664.4 18.9 %collective-permute-start.29 = (bf16[2,1,34,1088]{3,2,0,1:T(8,128)(2,1)S(1)}, bf16[2,1,34,1088]{3,2,0,1:T(8,128)(2,1)S(1)}, u32[]{:S(2)}, u32[]{:S(2)}) collective-permute-start(bf16[2,1,34,1088]{3,2,0,1:T(8,128)(2,1)S(1)} %dynamic-slice_bitcast_fusion.10), channel_id=1, source_target_pairs={{0,1},{1,0},{2,3},{3,2},{4,5},{5,4},{6,7},{7,6},{8,9},{9,8},{10,11... | collective-permute-start | bytes 443912 | tf_op jit(solution)/shard_map/ppermute | solution.py:39
  667.8 28.1 %collective-permute-start.40 = (bf16[4,1,136,1088]{3,2,1,0:T(8,128)(2,1)S(1)}, bf16[4,1,136,1088]{3,2,1,0:T(8,128)(2,1)S(1)}, u32[]{:S(2)}, u32[]{:S(2)}) collective-permute-start(bf16[4,1,136,1088]{3,2,1,0:T(8,128)(2,1)S(1)} %dynamic-slice_convert_fusion.2), channel_id=1, source_target_pairs={{0,4},{4,0},{8,12},{12,8},{16,20},{20,16},{24,28},{28,24},{1,5},{5... | collective-permute-start | bytes 3551240 | tf_op jit(solution)/shard_map/ppermute | solution.py:39
  683.4 12.4 %collective-permute-start.30 = (bf16[1,1,34,1088]{3,2,0,1:T(8,128)(2,1)S(1)}, bf16[1,1,34,1088]{3,2,0,1:T(8,128)(2,1)S(1)}, u32[]{:S(2)}, u32[]{:S(2)}) collective-permute-start(bf16[1,1,34,1088]{3,2,0,1:T(8,128)(2,1)S(1)} %constant_dynamic-slice_fusion.14), channel_id=1, source_target_pairs={{0,2},{1,3},{2,0},{3,1},{4,6},{5,7},{6,4},{7,5},{8,10},{9,11},{10,... | collective-permute-start | bytes 221960 | tf_op jit(solution)/shard_map/ppermute | solution.py:39
  695.8 11.2 %collective-permute-start.31 = (bf16[1,34,1088]{2,1,0:T(8,128)(2,1)S(1)}, bf16[1,34,1088]{2,1,0:T(8,128)(2,1)S(1)}, u32[]{:S(2)}, u32[]{:S(2)}) collective-permute-start(bf16[1,34,1088]{2,1,0:T(8,128)(2,1)S(1)} %fusion.115), channel_id=1, source_target_pairs={{0,2},{1,3},{2,0},{3,1},{4,6},{5,7},{6,4},{7,5},{8,10},{9,11},{10,... | collective-permute-start | bytes 221960 | tf_op jit(solution)/shard_map/ppermute | solution.py:39
  696.2 13.2 %collective-permute-start.41 = (bf16[1,2,136,1088]{3,2,1,0:T(8,128)(2,1)S(1)}, bf16[1,2,136,1088]{3,2,1,0:T(8,128)(2,1)S(1)}, u32[]{:S(2)}, u32[]{:S(2)}) collective-permute-start(bf16[1,2,136,1088]{3,2,1,0:T(8,128)(2,1)S(1)} %dynamic-slice_bitcast_fusion.3), channel_id=1, source_target_pairs={{0,16},{4,20},{8,24},{12,28},{16,0},{20,4},{24,8},{28,12},{1,17},{... | collective-permute-start | bytes 1775624 | tf_op jit(solution)/shard_map/ppermute | solution.py:39
  707.1 6.2 collective-permute-start.32
  709.7 7.1 collective-permute-start.42
  718.4 5.9 collective-permute-start.43
  726.0 6.8 collective-permute-start.44
  734.3 23.8 %collective-permute-start.45 = (bf16[1,34,1088]{2,1,0:T(8,128)(2,1)}, bf16[1,34,1088]{2,1,0:T(8,128)(2,1)}, u32[]{:S(2)}, u32[]{:S(2)}) collective-permute-start(bf16[1,34,1088]{2,1,0:T(8,128)(2,1)} %fusion.117), channel_id=1, source_target_pairs={{0,2},{1,3},{2,0},{3,1},{4,6},{5,7},{6,4},{7,5},{8,10},{9,11},{10,... | collective-permute-start | bytes 221960 | tf_op jit(solution)/shard_map/ppermute | solution.py:39
  755.3 11.3 %collective-permute-start.52 = (f32[4,1,1088]{2,1,0:T(1,128)S(1)}, f32[4,1,1088]{2,1,0:T(1,128)S(1)}, u32[]{:S(2)}, u32[]{:S(2)}) collective-permute-start(f32[4,1,1088]{2,1,0:T(1,128)S(1)} %fusion.121), channel_id=1, source_target_pairs={{0,4},{4,0},{8,12},{12,8},{16,20},{20,16},{24,28},{28,24},{1,5},{5... | collective-permute-start | bytes 52232 | tf_op jit(solution)/shard_map/ppermute | solution.py:39
  755.8 43.0 %collective-permute-start.48 = (bf16[2,1,34,1088]{3,2,1,0:T(8,128)(2,1)S(1)}, bf16[2,1,34,1088]{3,2,1,0:T(8,128)(2,1)S(1)}, u32[]{:S(2)}, u32[]{:S(2)}) collective-permute-start(bf16[2,1,34,1088]{3,2,1,0:T(8,128)(2,1)S(1)} %copy-done.39), channel_id=1, source_target_pairs={{0,1},{1,0},{2,3},{3,2},{4,5},{5,4},{6,7},{7,6},{8,9},{9,8},{10,11... | collective-permute-start | bytes 443912 | tf_op jit(solution)/shard_map/ppermute | solution.py:39
  755.8 67.5 %collective-permute-start.58 = (bf16[2,1,34,4352]{3,0,2,1:T(2,128)(2,1)}, bf16[2,1,34,4352]{3,0,2,1:T(2,128)(2,1)}, u32[]{:S(2)}, u32[]{:S(2)}) collective-permute-start(bf16[2,1,34,4352]{3,0,2,1:T(2,128)(2,1)} %bitcast.534), channel_id=1, source_target_pairs={{0,1},{1,0},{2,3},{3,2},{4,5},{5,4},{6,7},{7,6},{8,9},{9,8},{10,11... | collective-permute-start | bytes 1775624 | tf_op jit(solution)/shard_map/ppermute | solution.py:39
  758.0 62.4 %collective-permute-start.63 = (bf16[2,1,136,1088]{3,2,1,0:T(8,128)(2,1)}, bf16[2,1,136,1088]{3,2,1,0:T(8,128)(2,1)}, u32[]{:S(2)}, u32[]{:S(2)}) collective-permute-start(bf16[2,1,136,1088]{3,2,1,0:T(8,128)(2,1)} %dynamic-slice_bitcast_fusion.2), channel_id=1, source_target_pairs={{0,1},{1,0},{2,3},{3,2},{4,5},{5,4},{6,7},{7,6},{8,9},{9,8},{10,11... | collective-permute-start | bytes 1775624 | tf_op jit(solution)/shard_map/ppermute | solution.py:39
  759.1 4.8 collective-permute-start.22
  768.1 20.5 %collective-permute-start.24 = (f32[544]{0:T(1024)S(1)}, f32[544]{0:T(1024)S(1)}, u32[]{:S(2)}, u32[]{:S(2)}) collective-permute-start(f32[544]{0:T(1024)S(1)} %fusion.143), channel_id=1, source_target_pairs={{0,1},{1,0},{2,3},{3,2},{4,5},{5,4},{6,7},{7,6},{8,9},{9,8},{10,11... | collective-permute-start | bytes 6536 | tf_op jit(solution)/shard_map/ppermute | solution.py:39
  770.4 19.7 %collective-permute-start.54 = (f32[1,1,1088]{2,1,0:T(1,128)S(1)}, f32[1,1,1088]{2,1,0:T(1,128)S(1)}, u32[]{:S(2)}, u32[]{:S(2)}) collective-permute-start(f32[1,1,1088]{2,1,0:T(1,128)S(1)} %constant_dynamic-slice_fusion.3), channel_id=1, source_target_pairs={{0,16},{4,20},{8,24},{12,28},{16,0},{20,4},{24,8},{28,12},{1,17},{... | collective-permute-start | bytes 13064 | tf_op jit(solution)/shard_map/ppermute | solution.py:39
  793.2 79.0 %collective-permute-start.33 = (bf16[4,1,136,1088]{3,2,1,0:T(8,128)(2,1)}, bf16[4,1,136,1088]{3,2,1,0:T(8,128)(2,1)}, u32[]{:S(2)}, u32[]{:S(2)}) collective-permute-start(bf16[4,1,136,1088]{3,2,1,0:T(8,128)(2,1)} %dynamic-slice_convert_fusion.3), channel_id=1, source_target_pairs={{0,4},{4,0},{8,12},{12,8},{16,20},{20,16},{24,28},{28,24},{1,5},{5... | collective-permute-start | bytes 3551240 | tf_op jit(solution)/shard_map/ppermute | solution.py:39
  798.4 8.7 collective-permute-start.46
  798.8 6.1 collective-permute-start.49
  804.9 5.6 collective-permute-start.50
  810.6 6.6 collective-permute-start.51
  821.7 21.1 %collective-permute-start.64 = (bf16[1,1,136,1088]{3,2,1,0:T(8,128)(2,1)S(1)}, bf16[1,1,136,1088]{3,2,1,0:T(8,128)(2,1)S(1)}, u32[]{:S(2)}, u32[]{:S(2)}) collective-permute-start(bf16[1,1,136,1088]{3,2,1,0:T(8,128)(2,1)S(1)} %constant_dynamic-slice_fusion), channel_id=1, source_target_pairs={{0,2},{1,3},{2,0},{3,1},{4,6},{5,7},{6,4},{7,5},{8,10},{9,11},{10,... | collective-permute-start | bytes 887816 | tf_op jit(solution)/shard_map/ppermute | solution.py:39
  824.6 32.4 %collective-permute-start.59 = (bf16[1,1,34,4352]{3,2,0,1:T(8,128)(2,1)S(1)}, bf16[1,1,34,4352]{3,2,0,1:T(8,128)(2,1)S(1)}, u32[]{:S(2)}, u32[]{:S(2)}) collective-permute-start(bf16[1,1,34,4352]{3,2,0,1:T(8,128)(2,1)S(1)} %constant_dynamic-slice_fusion.1), channel_id=1, source_target_pairs={{0,2},{1,3},{2,0},{3,1},{4,6},{5,7},{6,4},{7,5},{8,10},{9,11},{10,... | collective-permute-start | bytes 887816 | tf_op jit(solution)/shard_map/ppermute | solution.py:39
  842.9 28.3 %collective-permute-start.65 = (bf16[1,136,1088]{2,1,0:T(8,128)(2,1)S(1)}, bf16[1,136,1088]{2,1,0:T(8,128)(2,1)S(1)}, u32[]{:S(2)}, u32[]{:S(2)}) collective-permute-start(bf16[1,136,1088]{2,1,0:T(8,128)(2,1)S(1)} %fusion.114), channel_id=1, source_target_pairs={{0,2},{1,3},{2,0},{3,1},{4,6},{5,7},{6,4},{7,5},{8,10},{9,11},{10,... | collective-permute-start | bytes 887816 | tf_op jit(solution)/shard_map/ppermute | solution.py:39
  857.1 20.1 %collective-permute-start.60 = (bf16[1,34,4352]{2,1,0:T(8,128)(2,1)S(1)}, bf16[1,34,4352]{2,1,0:T(8,128)(2,1)S(1)}, u32[]{:S(2)}, u32[]{:S(2)}) collective-permute-start(bf16[1,34,4352]{2,1,0:T(8,128)(2,1)S(1)} %fusion.112), channel_id=1, source_target_pairs={{0,2},{1,3},{2,0},{3,1},{4,6},{5,7},{6,4},{7,5},{8,10},{9,11},{10,... | collective-permute-start | bytes 887816 | tf_op jit(solution)/shard_map/ppermute | solution.py:39
  872.1 40.3 %collective-permute-start.66 = (bf16[2,136,1088]{2,1,0:T(8,128)(2,1)}, bf16[2,136,1088]{2,1,0:T(8,128)(2,1)S(1)}, u32[]{:S(2)}, u32[]{:S(2)}) collective-permute-start(bf16[2,136,1088]{2,1,0:T(8,128)(2,1)} %maximum_bitcast_fusion.1), channel_id=1, source_target_pairs={{0,1},{1,0},{2,3},{3,2},{4,5},{5,4},{6,7},{7,6},{8,9},{9,8},{10,11... | collective-permute-start | bytes 1775624 | tf_op jit(solution)/shard_map/ppermute | solution.py:39
  873.8 14.7 %collective-permute-start.34 = (bf16[2,1,136,1088]{3,2,1,0:T(8,128)(2,1)S(1)}, bf16[2,1,136,1088]{3,2,1,0:T(8,128)(2,1)S(1)}, u32[]{:S(2)}, u32[]{:S(2)}) collective-permute-start(bf16[2,1,136,1088]{3,2,1,0:T(8,128)(2,1)S(1)} %dynamic-slice_bitcast_fusion.4), channel_id=1, source_target_pairs={{0,8},{4,12},{8,0},{12,4},{16,24},{20,28},{24,16},{28,20},{1,9},{5... | collective-permute-start | bytes 1775624 | tf_op jit(solution)/shard_map/ppermute | solution.py:39
  877.8 25.4 %collective-permute-start.61 = (bf16[2,34,4352]{2,0,1:T(2,128)(2,1)S(1)}, bf16[2,34,4352]{2,0,1:T(2,128)(2,1)S(1)}, u32[]{:S(2)}, u32[]{:S(2)}) collective-permute-start(bf16[2,34,4352]{2,0,1:T(2,128)(2,1)S(1)} %copy.134), channel_id=1, source_target_pairs={{0,1},{1,0},{2,3},{3,2},{4,5},{5,4},{6,7},{7,6},{8,9},{9,8},{10,11... | collective-permute-start | bytes 1775624 | tf_op jit(solution)/shard_map/ppermute | solution.py:39
  888.7 14.6 %collective-permute-start.35 = (bf16[1,1,136,1088]{3,2,1,0:T(8,128)(2,1)S(1)}, bf16[1,1,136,1088]{3,2,1,0:T(8,128)(2,1)S(1)}, u32[]{:S(2)}, u32[]{:S(2)}) collective-permute-start(bf16[1,1,136,1088]{3,2,1,0:T(8,128)(2,1)S(1)} %constant_dynamic-slice_fusion.13), channel_id=1, source_target_pairs={{0,16},{4,20},{8,24},{12,28},{16,0},{20,4},{24,8},{28,12},{1,17},{... | collective-permute-start | bytes 887816 | tf_op jit(solution)/shard_map/ppermute | solution.py:39
  903.6 6.6 collective-permute-start.36
  910.3 6.7 collective-permute-start.37
  917.0 6.6 collective-permute-start.38
  923.7 5.6 collective-permute-start.39
  (82 other events, 982.5 us)
Sparse Core Ops, SparseCore 0:
  10.0 52.2 all-gather.4
  64.2 29.6 all-gather.8
  95.7 58.9 all-gather.6
  156.5 61.3 all-gather.10
  489.6 78.5 reduce-scatter.4
  621.0 86.0 reduce-scatter.2
